TPU v7x, 32 devices: a whole 2x2x4 slice. The times are simulated.
32 devices in a mesh: row: 8 (over y, x, core), col: 4 (over z).
Axes of the slice: x: 2, y: 2, z: 4, core: 2. Of those that a mesh axis runs over, the one named last changes fastest.
Arguments:
- panel_cols: bfloat16 [48, 2048, 512], P('col', 'row'), may hold values from -6 to 6
- inverses: bfloat16 [2, 256, 256], replicated, as said below
- trailing: bfloat16 [48, 2048, 1024], P(None, 'row', 'col'), may hold values from -6 to 6
Outputs:
- updated: bfloat16 [48, 2048, 1024], P(None, 'row', 'col')
Inputs may be any that keep to these rules, and one draw needn't show every extreme that they name: `inverses`: each of the two 256 x 256 matrices is lower triangular with a positive diagonal.
All inputs are finite; a program needn't handle non-finite values.
Results may differ from a plain program's by a relative error of at most 0.0063.
Values may be sent and summed in bfloat16 or wider, within the bound.
No kernel may reach another device: no remote copies, remote signals or barrier semaphores. Data moves between devices by JAX's collectives and lax.ppermute only.
A program may use at most 128 MiB of HBM per device.

v0:
```python
import jax
import jax.numpy as jnp
from jax import lax
from jax.sharding import PartitionSpec as P


def broadcast(value, axis, source):
    kept = jnp.where(lax.axis_index(axis) == source, value, 0).astype(value.dtype)
    return lax.psum(kept, axis)


def shards(panel_cols, inverses, trailing):
    tile_size = panel_cols.shape[1]
    grid_rows = lax.axis_size("row")
    grid_cols = lax.axis_size("col")
    col_index = lax.axis_index("col")
    left_factor = jnp.einsum(
        "tak,bk->tab", panel_cols[:, :, :tile_size], inverses[0], preferred_element_type=jnp.float32
    ).astype(jnp.bfloat16)
    couple_tile = broadcast(left_factor[0], ("row", "col"), grid_cols)
    reduced = (
        panel_cols[:, :, tile_size:].astype(jnp.float32)
        - jnp.einsum("tak,bk->tab", left_factor, couple_tile, preferred_element_type=jnp.float32)
    ).astype(jnp.bfloat16)
    right_factor = jnp.einsum(
        "tak,bk->tab", reduced, inverses[1], preferred_element_type=jnp.float32
    ).astype(jnp.bfloat16)
    factored = jnp.concatenate([left_factor, right_factor], axis=2)
    root_row = (col_index + 2) % grid_rows
    source_tile = (col_index + 2) // grid_rows
    whole_panel = lax.all_gather(factored, "col", axis=0, tiled=True)
    key_tile = broadcast(
        lax.dynamic_index_in_dim(whole_panel, source_tile, 0, keepdims=False), "row", root_row
    )
    update_sum = jnp.einsum(
        "tak,bk->tab", whole_panel, key_tile, preferred_element_type=jnp.float32
    )
    return (trailing.astype(jnp.float32) - update_sum).astype(jnp.bfloat16)


def solution(mesh):
    in_specs = (P("col", "row", None), P(), P(None, "row", "col"))
    out_specs = P(None, "row", "col")
    return jax.shard_map(shards, mesh=mesh, in_specs=in_specs, out_specs=out_specs, check_vma=False)
```

profile of v0, /device:TPU:4, one launch (start us, length us, event | category | flops | bytes accessed | tf_op | source)
XLA Modules:
  0.0 436.3 jit_solution(18001026137176645713)
XLA Ops:
  6.5 0.0 copy-start.1
  6.5 0.0 all-reduce.3.cloned.1.call-start
  6.5 2.1 convolution_convert_fusion.1
  8.6 0.0 copy-start
  8.6 0.7 fusion.2
  9.3 0.0 all-reduce.3.cloned.1.call-update
  9.4 0.0 all-gather.2.cloned.1.call-start
  9.4 127.1 %all-reduce.3.cloned.1.call-done = bf16[256,256]{0,1:T(8,128)(2,1)} async-done(((bf16[256,256]{0,1:T(8,128)(2,1)}), bf16[256,256]{0,1:T(8,128)(2,1)}) %all-reduce.3.cloned.1.call-update) | async-done | bytes 131088 | tf_op jit(solution)/shard_map/psum | solution.py:9
  136.5 0.0 copy-done
  136.5 0.0 copy-done.1
  136.5 4.2 convolution_convert_fusion
  140.7 2.1 pad_maximum_fusion
  142.8 2.8 copy.6
  145.6 0.0 all-gather.2.cloned.1.call-update
  145.6 0.0 all-reduce.5.cloned.1.call-start
  145.7 217.3 %all-gather.2.cloned.1.call-done = bf16[48,256,512]{2,1,0:T(8,128)(2,1)} async-done(((bf16[12,256,512]{2,1,0:T(8,128)(2,1)}), bf16[48,256,512]{2,1,0:T(8,128)(2,1)}) %all-gather.2.cloned.1.call-update) | async-done | bytes 12582928 | tf_op jit(solution)/shard_map/all_gather | solution.py:31
  363.0 1.7 select_bitcast_fusion
  364.7 0.0 all-reduce.5.cloned.1.call-update
  364.7 52.5 %all-reduce.5.cloned.1.call-done = bf16[256,512]{1,0:T(8,128)(2,1)} async-done(((bf16[256,512]{1,0:T(8,128)(2,1)}), bf16[256,512]{1,0:T(8,128)(2,1)}) %all-reduce.5.cloned.1.call-update) | async-done | bytes 262160 | tf_op jit(solution)/shard_map/psum | solution.py:9
  417.1 12.6 %subtract_convert_fusion = bf16[48,256,256]{2,1,0:T(8,128)(2,1)} fusion(bf16[48,256,256]{2,1,0:T(8,128)(2,1)} %param.5, bf16[48,256,512]{2,1,0:T(8,128)(2,1)} %all-gather.2.cloned.1.call-done, bf16[256,512]{1,0:T(8,128)(2,1)} %all-reduce.5.cloned.1.call-done), kind=kOutput, calls=%fused_computation | convolution fusion | flops 3230662656 | bytes 25427968 | tf_op jit(solution)/shard_map/tak,bk->tab/dot_general | solution.py:35
Async XLA Ops:
  6.5 130.0 %copy-start.1 = (bf16[2,256,256]{2,1,0:T(8,128)(2,1)S(1)}, bf16[2,256,256]{2,1,0:T(8,128)(2,1)}, u32[]{:S(2)}) copy-start(bf16[2,256,256]{2,1,0:T(8,128)(2,1)} %param.4) | copy-start | bytes 786436
  6.5 130.0 %all-reduce.3.cloned.1.call-start = ((), (), s32[]{:S(2)}) async-start(), calls=%async_computation | async-start | bytes 262144 | tf_op jit(solution)/shard_map/psum | solution.py:9
  8.6 127.9 %copy-start = (bf16[12,256,256]{1,2,0:T(8,128)(2,1)}, bf16[12,256,256]{1,2,0:T(8,128)(2,1)S(1)}, u32[]{:S(2)}) copy-start(bf16[12,256,256]{1,2,0:T(8,128)(2,1)S(1)} %convolution_convert_fusion.1) | copy-start | bytes 4718596
  9.4 353.6 %all-gather.2.cloned.1.call-start = ((), (), s32[]{:S(2)}) async-start(), calls=%async_computation.1 | async-start | bytes 15728640 | tf_op jit(solution)/shard_map/all_gather | solution.py:31
  145.6 271.6 %all-reduce.5.cloned.1.call-start = ((), (), s32[]{:S(2)}) async-start(), calls=%async_computation.2 | async-start | bytes 524288 | tf_op jit(solution)/shard_map/psum | solution.py:9
Sparse Core Ops, SparseCore 0:
  12.9 123.5 all-reduce.2
  145.7 217.2 all-gather.1
  366.0 51.0 all-reduce.4
where the time goes:
time: 439 us; the launch traced here: 436 us
  waiting for transfers between devices  397 us (90%)
  matrix products  18.9 us (4%)
  between operations  13.1 us (3%)
  other arithmetic  4.49 us (1%)
    all_gather x1, waiting for transfers between devices, shards(): whole_panel = lax.all_gather(factored, 'col', axis=0, tiled=True)  217 us
    psum x2, waiting for transfers between devices, broadcast(): return lax.psum(kept, axis)  180 us
    dot_general x1, matrix products, shards(): jnp.einsum('tak,bk->tab', whole_panel, key_tile, preferred_element_type=j...  12.6 us
  transfers between devices with their start and end apart: 3, of which 3 were waited for; matrix products, arithmetic and copies ran while one was open for 0% of the time, Pallas kernels for 0%

commit v1 on v0

v1 whole, which is shorter than its diff:
```python
import functools

import jax
import jax.numpy as jnp
from jax import lax
from jax.experimental import pallas as pl
from jax.experimental.pallas import tpu as pltpu
from jax.sharding import PartitionSpec as P


def dot_nt(left, right):
    return jnp.einsum("tak,bk->tab", left, right, preferred_element_type=jnp.float32)


def factor(panel, inverses, couple_tile):
    size = couple_tile.shape[0]
    left = dot_nt(panel[:, :, :size], inverses[0]).astype(jnp.bfloat16)
    reduced = (
        panel[:, :, size:].astype(jnp.float32) - dot_nt(left, couple_tile)
    ).astype(jnp.bfloat16)
    right = dot_nt(reduced, inverses[1]).astype(jnp.bfloat16)
    return jnp.concatenate([left, right], axis=2)


def product(factored, key_tile):
    return dot_nt(factored, key_tile).astype(jnp.bfloat16)


def pick(choices, index):
    return lax.dynamic_index_in_dim(choices, index, 0, keepdims=False)


def update_body(place, held, trailing, first, second, out):
    del held
    total = trailing[...].astype(jnp.float32)

    @pl.when(place[1] == 0)
    def _():
        out[...] = (total - first[...].astype(jnp.float32)).astype(out.dtype)

    @pl.when(place[1] != 0)
    def _():
        out[...] = (total - second[...].astype(jnp.float32)).astype(out.dtype)


def update(held, trailing, first, second, start, use_second):
    tiles, size, width = first.shape
    step = 2 if tiles % 2 == 0 else 1
    block = (step, size, width)
    place = jnp.stack([start // step, use_second]).astype(jnp.int32)
    body = update_body
    args = [trailing, first, second]
    in_specs = [
        pl.BlockSpec(block, lambda t, p: (p[0] + t, 0, 0)),
        pl.BlockSpec(block, lambda t, p: (jnp.where(p[1] == 0, t, 0), 0, 0)),
        pl.BlockSpec(block, lambda t, p: (jnp.where(p[1] == 0, 0, t), 0, 0)),
    ]
    aliases = {}
    if held is None:
        body = lambda place, *refs: update_body(place, None, *refs)
    else:
        args = [held] + args
        in_specs = [pl.BlockSpec(memory_space=pl.ANY)] + in_specs
        aliases = {1: 0}
    return pl.pallas_call(
        body,
        out_shape=jax.ShapeDtypeStruct(trailing.shape, trailing.dtype),
        grid_spec=pltpu.PrefetchScalarGridSpec(
            num_scalar_prefetch=1,
            grid=(tiles // step,),
            in_specs=in_specs,
            out_specs=pl.BlockSpec(block, lambda t, p: (p[0] + t, 0, 0)),
        ),
        input_output_aliases=aliases,
        cost_estimate=pl.CostEstimate(
            flops=first.size, bytes_accessed=6 * first.size, transcendentals=0
        ),
    )(place, *args)


def key_tiles(head, rows, cols, first_tile):
    row_index = lax.axis_index("row")
    col_index = lax.axis_index("col")
    wanted = sorted({tile % rows for tile in range(first_tile, cols + 2)})
    span = cols // 2
    while span:
        pairs = [
            (r * cols + c, r * cols + c + span)
            for r in wanted
            for c in range(0, cols, 2 * span)
        ]
        arrived = lax.ppermute(head, ("row", "col"), pairs)
        head = jnp.where(col_index % (2 * span) == span, arrived, head)
        span //= 2
    same = [head]
    for offset in range(2, rows, 2):
        same.append(lax.ppermute(head, "row", [(r, r ^ offset) for r in wanted]))
    same = jnp.stack(same)
    other = lax.ppermute(same, "row", [(r, r ^ 1) for r in range(rows)])
    heads = jnp.concatenate([same, other])
    tiles = []
    for tile in range(first_tile, cols + 2):
        offset = row_index ^ (tile % rows)
        tiles.append(pick(heads, offset // 2 + (offset % 2) * (rows // 2))[tile // rows])
    return tiles


def shards(panel_cols, inverses, trailing):
    tiles, size, _ = panel_cols.shape
    rows = lax.axis_size("row")
    cols = lax.axis_size("col")
    col_index = lax.axis_index("col")
    low, high = cols // 2 - 1, cols // 2
    in_low = col_index <= low
    inner = jnp.where(in_low, low, high)
    parts = 3 if tiles % 3 == 0 else 1
    part = tiles // parts

    raw = [
        lax.ppermute(panel_cols[i * part:(i + 1) * part], "col", [(low, high), (high, low)])
        for i in range(parts)
    ]

    head_tiles = (cols + 1) // rows + 1
    raw_keys = key_tiles(panel_cols[:head_tiles], rows, cols, 1)
    couple_tile = dot_nt(raw_keys[0][None, :, :size], inverses[0]).astype(jnp.bfloat16)[0]
    keys = factor(jnp.stack(raw_keys[1:]), inverses, couple_tile)

    factored = factor(panel_cols, inverses, couple_tile)
    arrived = {}
    for offset in range(1, cols):
        pairs = [
            (c, (c + offset) % cols)
            for c in range(cols)
            if not (c == low and (c + offset) % cols > low)
            and not (c == high and (c + offset) % cols < high)
        ]
        piece = product(factored, pick(keys, (col_index + offset) % cols))
        arrived[offset] = lax.ppermute(piece, "col", pairs)

    own = product(factored, pick(keys, col_index))
    out = update(None, trailing, own, own, col_index * tiles, jnp.int32(0))

    special = jnp.where(in_low, high, low)
    for i in range(parts):
        crossed = factor(raw[i], inverses, couple_tile)
        mine = product(crossed, pick(keys, col_index))
        handed = jnp.zeros_like(mine)
        for k in range(1, cols // 2):
            target = jnp.clip(jnp.where(in_low, col_index - k, col_index + k), 0, cols - 1)
            piece = product(crossed, pick(keys, target))
            got = lax.ppermute(piece, "col", [(high, high + k), (low, low - k)])
            handed = got if cols == 4 else jnp.where(jnp.abs(col_index - inner) == k, got, handed)
        out = update(
            out, trailing, mine, handed, special * tiles + i * part, (col_index != inner).astype(jnp.int32)
        )

    for offset in range(1, cols):
        source = (col_index - offset) % cols
        skip = source == special
        out = update(
            out,
            trailing,
            arrived[offset],
            own,
            jnp.where(skip, col_index, source) * tiles,
            skip.astype(jnp.int32),
        )
    return out


def solution(mesh):
    in_specs = (P("col", "row", None), P(), P(None, "row", "col"))
    out_specs = P(None, "row", "col")
    return jax.shard_map(shards, mesh=mesh, in_specs=in_specs, out_specs=out_specs, check_vma=False)
```

time: 439 us -> 268 us (0.61)
  waiting for transfers between devices: 397 us -> 68.8 us
  starting transfers between devices: 0.09 us -> 100 us
  Pallas kernels: 0 us -> 31.5 us
  matrix products: 18.9 us -> 47.5 us
  between operations: 13.1 us -> 0.27 us
  local copies, waits for them, and re-layouts: 2.8 us -> 11.3 us
    all_gather x1 -> x0, waiting for transfers between devices: 217 us -> none  [shards(): whole_panel = lax.all_gather(factored, 'col', axis=0, tiled=True)]
    psum x2 -> x0, waiting for transfers between devices: 180 us -> none  [broadcast(): return lax.psum(kept, axis)]
    ppermute x0 -> x15, starting transfers between devices: none -> 100 us  [the longest x3 77.2 us: shards(): arrived[offset] = lax.ppermute(piece, 'col', pairs)]
    ppermute x0 -> x15, waiting for transfers between devices: none -> 68.8 us  [the longest x3 62.2 us: shards(): got = lax.ppermute(piece, 'col', [(high, high + k), (low, low - k)])]
    pallas_call x0 -> x7, Pallas kernels: none -> 31.5 us  [update(): pl.pallas_call(body, out_shape=jax.ShapeDtypeStruct(trailing.shape, trail...]
    dot_general x3 -> x21, matrix products: 18.9 us -> 47.5 us  [dot_nt(): jnp.einsum('tak,bk->tab', left, right, preferred_element_type=jnp.float32)]
    unnamed x4 -> x47, local copies, waits for them, and re-layouts: 0.01 us -> 5.88 us
    slice x0 -> x2, local copies, waits for them, and re-layouts: none -> 5.24 us  [the longest x1 3.57 us: shards(): panel_cols[i * part:(i + 1) * part]]
  transfers between devices with their start and end apart: 3 -> 15, of which waited for: 3 -> 5; matrix products, arithmetic and copies ran while one was open for 0% -> 17% of each run, Pallas kernels for 0% -> 10%
where the time goes in v1:
time: 268 us; the launch traced here: 266 us
  starting transfers between devices  100 us (37%)
  waiting for transfers between devices  68.8 us (26%)
  matrix products  47.5 us (18%)
  Pallas kernels  31.5 us (12%)
  local copies, waits for them, and re-layouts  11.3 us (4%)
  other arithmetic  6.75 us (3%)
    ppermute x3, starting transfers between devices, shards(): arrived[offset] = lax.ppermute(piece, 'col', pairs)  77.2 us
    ppermute x3, waiting for transfers between devices, shards(): got = lax.ppermute(piece, 'col', [(high, high + k), (low, low - k)])  62.2 us
    dot_general x21, matrix products, dot_nt(): jnp.einsum('tak,bk->tab', left, right, preferred_element_type=jnp.float32)  47.5 us
    pallas_call x7, Pallas kernels, update(): pl.pallas_call(body, out_shape=jax.ShapeDtypeStruct(trailing.shape, trail...  31.5 us
    ppermute x2, starting transfers between devices, key_tiles(): arrived = lax.ppermute(head, ('row', 'col'), pairs)  7.6 us
    ppermute x3, starting transfers between devices, key_tiles(): same.append(lax.ppermute(head, 'row', [(r, r ^ offset) for r in wanted]))  7.32 us
    unnamed x47, local copies, waits for them, and re-layouts  5.88 us
  transfers between devices with their start and end apart: 15, of which 5 were waited for; matrix products, arithmetic and copies ran while one was open for 17% of the time, Pallas kernels for 10%

profile of v1, /device:TPU:4, one launch (start us, length us, event | category | flops | bytes accessed | tf_op | source)
XLA Modules:
  0.0 266.4 jit_solution(13710954312352245128)
XLA Ops:
  0.0 1.7 slice.63
  1.7 5.5 %collective-permute-start = (bf16[1,256,512]{2,1,0:T(8,128)(2,1)}, bf16[1,256,512]{2,1,0:T(8,128)(2,1)}, u32[]{:S(2)}, u32[]{:S(2)}) collective-permute-start(bf16[1,256,512]{2,1,0:T(8,128)(2,1)} %slice.63), channel_id=1, source_target_pairs={{4,6},{8,10},{12,14},{16,18},{20,22}} | collective-permute-start | bytes 786440 | tf_op jit(solution)/shard_map/ppermute | solution.py:92
  7.1 3.6 %fusion.66 = (bf16[4,256,512]{2,1,0:T(8,128)(2,1)}, bf16[4,256,512]{2,1,0:T(8,128)(2,1)}, bf16[4,256,512]{2,1,0:T(8,128)(2,1)}) fusion(bf16[12,256,512]{2,1,0:T(8,128)(2,1)} %param.3), kind=kLoop, calls=%fused_computation.121 | loop fusion | bytes 6291456 | tf_op jit(solution)/shard_map/slice | solution.py:120
  10.7 1.6 collective-permute-start.10
  12.3 1.6 collective-permute-start.6
  14.0 0.6 pad_add_fusion.3.place
  14.6 0.6 pad_add_fusion.4.place
  15.2 0.6 pad_add_fusion.5.place
  15.8 2.1 collective-permute-start.1
  17.9 1.8 convolution_convert_fusion.1
  19.7 3.2 %collective-permute-done.1 = bf16[1,256,512]{2,1,0:T(8,128)(2,1)S(1)} collective-permute-done((bf16[1,256,512]{2,1,0:T(8,128)(2,1)S(1)}, bf16[1,256,512]{2,1,0:T(8,128)(2,1)S(1)}, u32[]{:S(2)}, u32[]{:S(2)}) %collective-permute-start.1) | collective-permute-done | bytes 262176 | tf_op jit(solution)/shard_map/ppermute | solution.py:92
  22.9 0.9 constant_dynamic-update-slice_fusion.4
  23.8 3.3 %collective-permute-start.4 = (bf16[1,256,512]{2,1,0:T(8,128)(2,1)}, bf16[1,256,512]{2,1,0:T(8,128)(2,1)}, u32[]{:S(2)}, u32[]{:S(2)}) collective-permute-start(bf16[1,256,512]{2,1,0:T(8,128)(2,1)} %get-tuple-element.6), channel_id=1, source_target_pairs={{4,28},{8,16},{12,20},{16,8},{20,12},{5,29},{9,17},{13,21},{17,9},... | collective-permute-start | bytes 786440 | tf_op jit(solution)/shard_map/ppermute | solution.py:97
  27.1 2.0 collective-permute-start.3
  29.1 2.0 collective-permute-start.2
  31.1 0.6 pad_add_fusion.2.place
  31.7 0.6 pad_add_fusion.6.place
  32.2 0.6 pad_add_fusion
  32.9 1.0 collective-permute-done.4
  33.9 0.7 collective-permute-start.8
  34.6 2.4 collective-permute-done.2
  37.1 1.3 pad_maximum_fusion.1
  38.5 1.0 constant_dynamic-update-slice_fusion.3
  39.5 1.0 constant_dynamic-update-slice_fusion.2
  40.4 1.0 constant_dynamic-update-slice_fusion.1
  41.4 2.2 convolution_convert_fusion.9
  43.6 2.2 convolution_convert_fusion.17
  45.8 1.2 convolution_convert_fusion.13
  47.2 0.2 fusion.2
  47.6 1.0 copy-done.2
  48.6 1.1 convolution_convert_fusion.19
  49.7 2.6 convolution_convert_fusion.18
  52.3 3.7 %convolution_convert_fusion = bf16[12,256,256]{1,2,0:T(8,128)(2,1)} fusion(bf16[12,256,256]{1,2,0:T(8,128)(2,1)} %convolution_convert_fusion.1, bf16[256,256,1]{1,0,2:T(8,128)(2,1)S(1)} %fusion.2, bf16[12,256,512]{2,1,0:T(8,128)(2,1)S(1)} %copy-done, bf16[2,256,256]{2,1,0:T(8,128)(2,1)S(1)} %copy-done.1), kind=kOutput, calls=%fused_computation.2 | convolution fusion | flops 808452096 | bytes 4980736 | tf_op jit(solution)/shard_map/tak,bk->tab/dot_general | solution.py:12
  56.1 4.2 %convolution_convert_fusion.4 = bf16[12,256,256]{2,1,0:T(8,128)(2,1)} fusion(s32[]{:T(128)S(6)} %select_n.203, bf16[4,256,256]{1,2,0:T(8,128)(2,1)} %convolution_convert_fusion.19, bf16[4,256,256]{1,2,0:T(8,128)(2,1)} %convolution_convert_fusion.18, bf16[12,256,256]{1,2,0:T(8,128)(2,1)} %convolution_convert_fusion, ...), kind=kOutput, calls=%fused_computation.6 | convolution fusion | flops 812908544 | bytes 5767172 | tf_op jit(solution)/shard_map/tak,bk->tab/dot_general | solution.py:12
  60.3 2.3 convolution_convert_fusion.3
  62.6 2.2 convolution_convert_fusion.2
  64.8 5.8 %collective-permute-start.14 = (bf16[12,256,256]{2,1,0:T(8,128)(2,1)}, bf16[12,256,256]{2,1,0:T(8,128)(2,1)S(1)}, u32[]{:S(2)}, u32[]{:S(2)}) collective-permute-start(bf16[12,256,256]{2,1,0:T(8,128)(2,1)} %convolution_convert_fusion.2), channel_id=1, source_target_pairs={{0,3},{1,0},{3,2},{4,7},{5,4},{7,6},{8,11},{9,8},{11,10},{12,15},{... | collective-permute-start | bytes 4718600 | tf_op jit(solution)/shard_map/ppermute | solution.py:139
  70.6 69.5 %collective-permute-start.13 = (bf16[12,256,256]{2,1,0:T(8,128)(2,1)}, bf16[12,256,256]{2,1,0:T(8,128)(2,1)}, u32[]{:S(2)}, u32[]{:S(2)}) collective-permute-start(bf16[12,256,256]{2,1,0:T(8,128)(2,1)} %convolution_convert_fusion.3), channel_id=1, source_target_pairs={{0,2},{3,1},{4,6},{7,5},{8,10},{11,9},{12,14},{15,13},{16,18},{19,... | collective-permute-start | bytes 4718600 | tf_op jit(solution)/shard_map/ppermute | solution.py:139
  140.1 1.9 collective-permute-start.12
  142.0 0.8 fusion.24
  142.9 2.5 convolution_convert_fusion.8
  145.3 2.5 convolution_convert_fusion.6
  147.8 1.3 collective-permute-start.11
  149.1 2.5 convolution_convert_fusion.16
  151.6 2.4 convolution_convert_fusion.14
  154.0 1.5 collective-permute-start.7
  155.5 2.5 convolution_convert_fusion.12
  158.0 2.7 %convolution_convert_fusion.10 = bf16[4,256,256]{2,1,0:T(8,128)(2,1)} fusion(bf16[256,512,1]{0,1,2:T(8,128)(2,1)} %get-tuple-element.15, bf16[4,256,256]{1,2,0:T(8,128)(2,1)} %convolution_convert_fusion.12, bf16[4,256,256]{1,2,0:T(8,128)(2,1)} %convolution_convert_fusion.13), kind=kOutput, calls=%fused_computation.24 | convolution fusion | flops 270794752 | bytes 1835008 | tf_op jit(solution)/shard_map/tak,bk->tab/dot_general | solution.py:12
  160.7 3.7 %convolution_convert_fusion.5.refs_1_.refs_2_.second = bf16[12,256,256]{2,1,0:T(8,128)(2,1)} fusion(bf16[256,512,1]{0,1,2:T(8,128)(2,1)S(1)} %copy-done.17, bf16[12,256,256]{1,2,0:T(8,128)(2,1)} %convolution_convert_fusion, bf16[12,256,256]{1,2,0:T(8,128)(2,1)S(1)} %copy-done.6), kind=kOutput, calls=%fused_computation.7 | convolution fusion | flops 812384256 | bytes 4980736 | tf_op jit(solution)/shard_map/tak,bk->tab/dot_general | solution.py:12
  164.4 28.1 %collective-permute-done.7.second = bf16[4,256,256]{2,1,0:T(8,128)(2,1)} collective-permute-done((bf16[4,256,256]{2,1,0:T(8,128)(2,1)}, bf16[4,256,256]{2,1,0:T(8,128)(2,1)}, u32[]{:S(2)}, u32[]{:S(2)}) %collective-permute-start.7) | collective-permute-done | bytes 524320 | tf_op jit(solution)/shard_map/ppermute | solution.py:152
  192.5 1.3 collective-permute-start.9
  193.8 1.3 convolution_convert_fusion.7.first
  195.1 6.0 %shard_map.37.held = bf16[48,256,256]{2,1,0:T(8,128)(2,1)} custom-call(s32[2]{0:T(128)} %pad_add_fusion.6.place, bf16[48,256,256]{2,1,0:T(8,128)(2,1)} %trailing.11, bf16[12,256,256]{2,1,0:T(8,128)(2,1)} %convolution_convert_fusion.5.refs_1_.refs_2_.second, bf16[12,256,256]{2,1,0:T(8,128)(2,1)} %convolution_convert_fusion.5.refs_1_.refs_2_.second), custom_call_target="tpu_custom_call" | custom-call | flops 786432 | bytes 4718592 | tf_op jit(solution)/shard_map/pallas_call | solution.py:65
  201.2 2.4 convolution_convert_fusion.15.first
  203.6 1.3 convolution_convert_fusion.11.first
  204.9 2.7 %shard_map.38.held = bf16[48,256,256]{2,1,0:T(8,128)(2,1)} custom-call(s32[2]{0:T(128)} %pad_add_fusion.5.place, bf16[48,256,256]{2,1,0:T(8,128)(2,1)} %shard_map.37.held, bf16[48,256,256]{2,1,0:T(8,128)(2,1)} %trailing.11, bf16[4,256,256]{2,1,0:T(8,128)(2,1)} %convolution_convert_fusion.15.first, ...), custom_call_target="tpu_custom_call", output_to_operand_aliasing={{}: (1, {})} | custom-call | flops 262144 | bytes 1572864 | tf_op jit(solution)/shard_map/pallas_call | solution.py:65
  207.6 34.0 %collective-permute-done.9.second = bf16[4,256,256]{2,1,0:T(8,128)(2,1)S(1)} collective-permute-done((bf16[4,256,256]{2,1,0:T(8,128)(2,1)}, bf16[4,256,256]{2,1,0:T(8,128)(2,1)S(1)}, u32[]{:S(2)}, u32[]{:S(2)}) %collective-permute-start.9) | collective-permute-done | bytes 524320 | tf_op jit(solution)/shard_map/ppermute | solution.py:152
  241.7 0.8 copy-done.8
  242.4 2.7 %shard_map.39.held = bf16[48,256,256]{2,1,0:T(8,128)(2,1)} custom-call(s32[2]{0:T(128)} %pad_add_fusion.4.place, bf16[48,256,256]{2,1,0:T(8,128)(2,1)} %shard_map.38.held, bf16[48,256,256]{2,1,0:T(8,128)(2,1)} %trailing.11, bf16[4,256,256]{2,1,0:T(8,128)(2,1)} %convolution_convert_fusion.11.first, ...), custom_call_target="tpu_custom_call", output_to_operand_aliasing={{}: (1, {})} | custom-call | flops 262144 | bytes 1572864 | tf_op jit(solution)/shard_map/pallas_call | solution.py:65
  245.2 2.7 %shard_map.40.held = bf16[48,256,256]{2,1,0:T(8,128)(2,1)} custom-call(s32[2]{0:T(128)} %pad_add_fusion.3.place, bf16[48,256,256]{2,1,0:T(8,128)(2,1)} %shard_map.39.held, bf16[48,256,256]{2,1,0:T(8,128)(2,1)} %trailing.11, bf16[4,256,256]{2,1,0:T(8,128)(2,1)} %convolution_convert_fusion.7.first, ...), custom_call_target="tpu_custom_call", output_to_operand_aliasing={{}: (1, {})} | custom-call | flops 262144 | bytes 1572864 | tf_op jit(solution)/shard_map/pallas_call | solution.py:65
  247.9 5.8 %shard_map.41.held = bf16[48,256,256]{2,1,0:T(8,128)(2,1)} custom-call(s32[2]{0:T(128)} %pad_add_fusion.2.place, bf16[48,256,256]{2,1,0:T(8,128)(2,1)} %shard_map.40.held, bf16[48,256,256]{2,1,0:T(8,128)(2,1)} %trailing.11, bf16[12,256,256]{2,1,0:T(8,128)(2,1)} %collective-permute-done.12.first, ...), custom_call_target="tpu_custom_call", output_to_operand_aliasing={{}: (1, {})} | custom-call | flops 786432 | bytes 4718592 | tf_op jit(solution)/shard_map/pallas_call | solution.py:65
  253.7 5.7 %shard_map.42.held = bf16[48,256,256]{2,1,0:T(8,128)(2,1)} custom-call(s32[2]{0:T(128)} %get-tuple-element.18.place, bf16[48,256,256]{2,1,0:T(8,128)(2,1)} %shard_map.41.held, bf16[48,256,256]{2,1,0:T(8,128)(2,1)} %trailing.11, bf16[12,256,256]{2,1,0:T(8,128)(2,1)} %collective-permute-done.13.first, ...), custom_call_target="tpu_custom_call", output_to_operand_aliasing={{}: (1, {})} | custom-call | flops 786432 | bytes 4718592 | tf_op jit(solution)/shard_map/pallas_call | solution.py:65
  259.5 1.2 copy-done.4
  260.6 5.8 %shard_map.43 = bf16[48,256,256]{2,1,0:T(8,128)(2,1)} custom-call(s32[2]{0:T(128)} %get-tuple-element.17.place, bf16[48,256,256]{2,1,0:T(8,128)(2,1)} %shard_map.42.held, bf16[48,256,256]{2,1,0:T(8,128)(2,1)} %trailing.11, bf16[12,256,256]{2,1,0:T(8,128)(2,1)} %copy-done.4, ...), custom_call_target="tpu_custom_call", output_to_operand_aliasing={{}: (1, {})} | custom-call | flops 786432 | bytes 4718592 | tf_op jit(solution)/shard_map/pallas_call | solution.py:65
  (56 shorter events, 0.5 us)
Async XLA Ops:
  1.7 14.1 %copy-start = (bf16[12,256,512]{2,1,0:T(8,128)(2,1)S(1)}, bf16[12,256,512]{2,1,0:T(8,128)(2,1)}, u32[]{:S(2)}) copy-start(bf16[12,256,512]{2,1,0:T(8,128)(2,1)} %param.3) | copy-start | bytes 9437188
  1.7 16.2 %copy-start.1 = (bf16[2,256,256]{2,1,0:T(8,128)(2,1)S(1)}, bf16[2,256,256]{2,1,0:T(8,128)(2,1)}, u32[]{:S(2)}) copy-start(bf16[2,256,256]{2,1,0:T(8,128)(2,1)} %param.4) | copy-start | bytes 786436
  1.7 14.1 %collective-permute-start = (bf16[1,256,512]{2,1,0:T(8,128)(2,1)}, bf16[1,256,512]{2,1,0:T(8,128)(2,1)}, u32[]{:S(2)}, u32[]{:S(2)}) collective-permute-start(bf16[1,256,512]{2,1,0:T(8,128)(2,1)} %slice.63), channel_id=1, source_target_pairs={{4,6},{8,10},{12,14},{16,18},{20,22}} | collective-permute-start | bytes 786440 | tf_op jit(solution)/shard_map/ppermute | solution.py:92
  10.7 30.7 %collective-permute-start.10 = (bf16[4,256,512]{2,1,0:T(8,128)(2,1)}, bf16[4,256,512]{2,1,0:T(8,128)(2,1)}, u32[]{:S(2)}, u32[]{:S(2)}) collective-permute-start(bf16[4,256,512]{2,1,0:T(8,128)(2,1)} %get-tuple-element.7), channel_id=1, source_target_pairs={{1,2},{2,1},{5,6},{6,5},{9,10},{10,9},{13,14},{14,13},{17,18},{18,... | collective-permute-start | bytes 3145736 | tf_op jit(solution)/shard_map/ppermute | solution.py:120
  12.3 31.3 %collective-permute-start.6 = (bf16[4,256,512]{2,1,0:T(8,128)(2,1)}, bf16[4,256,512]{2,1,0:T(8,128)(2,1)}, u32[]{:S(2)}, u32[]{:S(2)}) collective-permute-start(bf16[4,256,512]{2,1,0:T(8,128)(2,1)} %get-tuple-element.8), channel_id=1, source_target_pairs={{1,2},{2,1},{5,6},{6,5},{9,10},{10,9},{13,14},{14,13},{17,18},{18,... | collective-permute-start | bytes 3145736 | tf_op jit(solution)/shard_map/ppermute | solution.py:120
  15.8 7.1 %collective-permute-start.1 = (bf16[1,256,512]{2,1,0:T(8,128)(2,1)S(1)}, bf16[1,256,512]{2,1,0:T(8,128)(2,1)S(1)}, u32[]{:S(2)}, u32[]{:S(2)}) collective-permute-start(bf16[1,256,512]{2,1,0:T(8,128)(2,1)S(1)} %broadcast_select_fusion), channel_id=1, source_target_pairs={{4,5},{6,7},{8,9},{10,11},{12,13},{14,15},{16,17},{18,19},{20,21},... | collective-permute-start | bytes 786440 | tf_op jit(solution)/shard_map/ppermute | solution.py:92
  23.8 10.1 %collective-permute-start.4 = (bf16[1,256,512]{2,1,0:T(8,128)(2,1)}, bf16[1,256,512]{2,1,0:T(8,128)(2,1)}, u32[]{:S(2)}, u32[]{:S(2)}) collective-permute-start(bf16[1,256,512]{2,1,0:T(8,128)(2,1)} %get-tuple-element.6), channel_id=1, source_target_pairs={{4,28},{8,16},{12,20},{16,8},{20,12},{5,29},{9,17},{13,21},{17,9},... | collective-permute-start | bytes 786440 | tf_op jit(solution)/shard_map/ppermute | solution.py:97
  27.1 7.5 %collective-permute-start.3 = (bf16[1,256,512]{2,1,0:T(8,128)(2,1)}, bf16[1,256,512]{2,1,0:T(8,128)(2,1)}, u32[]{:S(2)}, u32[]{:S(2)}) collective-permute-start(bf16[1,256,512]{2,1,0:T(8,128)(2,1)} %get-tuple-element.6), channel_id=1, source_target_pairs={{4,20},{8,24},{12,28},{16,0},{20,4},{5,21},{9,25},{13,29},{17,1},{... | collective-permute-start | bytes 786440 | tf_op jit(solution)/shard_map/ppermute | solution.py:97
  29.1 8.0 %collective-permute-start.2 = (bf16[1,256,512]{2,1,0:T(8,128)(2,1)}, bf16[1,256,512]{2,1,0:T(8,128)(2,1)}, u32[]{:S(2)}, u32[]{:S(2)}) collective-permute-start(bf16[1,256,512]{2,1,0:T(8,128)(2,1)} %get-tuple-element.6), channel_id=1, source_target_pairs={{4,12},{8,0},{12,4},{16,24},{20,28},{5,13},{9,1},{13,5},{17,25},{2... | collective-permute-start | bytes 786440 | tf_op jit(solution)/shard_map/ppermute | solution.py:97
  31.7 6.8 %copy-start.7 = (bf16[8,1,256,512]{3,2,1,0:T(8,128)(2,1)S(1)}, bf16[8,1,256,512]{3,2,1,0:T(8,128)(2,1)}, u32[]{:S(2)}) copy-start(bf16[8,1,256,512]{3,2,1,0:T(8,128)(2,1)} %get-tuple-element.5) | copy-start | bytes 6291460
  33.9 11.9 %collective-permute-start.8 = (bf16[4,256,512]{2,1,0:T(8,128)(2,1)}, bf16[4,256,512]{2,1,0:T(8,128)(2,1)S(1)}, u32[]{:S(2)}, u32[]{:S(2)}) collective-permute-start(bf16[4,256,512]{2,1,0:T(8,128)(2,1)} %get-tuple-element.9), channel_id=1, source_target_pairs={{1,2},{2,1},{5,6},{6,5},{9,10},{10,9},{13,14},{14,13},{17,18},{18,... | collective-permute-start | bytes 3145736 | tf_op jit(solution)/shard_map/ppermute | solution.py:120
  38.4 8.6 %collective-permute-start.5 = (bf16[4,1,256,512]{3,2,1,0:T(8,128)(2,1)S(1)}, bf16[4,1,256,512]{3,2,1,0:T(8,128)(2,1)S(1)}, u32[]{:S(2)}, u32[]{:S(2)}) collective-permute-start(bf16[4,1,256,512]{3,2,1,0:T(8,128)(2,1)S(1)} %pad_maximum_fusion.1), channel_id=1, source_target_pairs={{0,4},{4,0},{8,12},{12,8},{16,20},{20,16},{24,28},{28,24},{1,5},{5... | collective-permute-start | bytes 3145736 | tf_op jit(solution)/shard_map/ppermute | solution.py:99
  45.8 1.4 copy-start.16
  47.6 1.0 copy-start.2
  56.1 4.2 %copy-start.3 = (bf16[4,256,256]{1,2,0:T(8,128)(2,1)S(1)}, bf16[4,256,256]{1,2,0:T(8,128)(2,1)}, u32[]{:S(2)}) copy-start(bf16[4,256,256]{1,2,0:T(8,128)(2,1)} %convolution_convert_fusion.19) | copy-start | bytes 1572868
  56.1 4.2 %copy-start.5 = (bf16[12,256,256]{1,2,0:T(8,128)(2,1)S(1)}, bf16[12,256,256]{1,2,0:T(8,128)(2,1)}, u32[]{:S(2)}) copy-start(bf16[12,256,256]{1,2,0:T(8,128)(2,1)} %convolution_convert_fusion.1) | copy-start | bytes 4718596
  56.1 4.2 %copy-start.15 = (bf16[4,256,256]{1,2,0:T(8,128)(2,1)S(1)}, bf16[4,256,256]{1,2,0:T(8,128)(2,1)}, u32[]{:S(2)}) copy-start(bf16[4,256,256]{1,2,0:T(8,128)(2,1)} %convolution_convert_fusion.18) | copy-start | bytes 1572868
  56.1 4.2 %copy-start.21 = (bf16[12,256,256]{1,2,0:T(8,128)(2,1)S(1)}, bf16[12,256,256]{1,2,0:T(8,128)(2,1)}, u32[]{:S(2)}) copy-start(bf16[12,256,256]{1,2,0:T(8,128)(2,1)} %convolution_convert_fusion) | copy-start | bytes 4718596
  62.6 80.2 %copy-start.9 = (bf16[4,256,256]{1,2,0:T(8,128)(2,1)S(1)}, bf16[4,256,256]{1,2,0:T(8,128)(2,1)}, u32[]{:S(2)}) copy-start(bf16[4,256,256]{1,2,0:T(8,128)(2,1)} %convolution_convert_fusion.9) | copy-start | bytes 1572868
  64.8 194.6 %collective-permute-start.14 = (bf16[12,256,256]{2,1,0:T(8,128)(2,1)}, bf16[12,256,256]{2,1,0:T(8,128)(2,1)S(1)}, u32[]{:S(2)}, u32[]{:S(2)}) collective-permute-start(bf16[12,256,256]{2,1,0:T(8,128)(2,1)} %convolution_convert_fusion.2), channel_id=1, source_target_pairs={{0,3},{1,0},{3,2},{4,7},{5,4},{7,6},{8,11},{9,8},{11,10},{12,15},{... | collective-permute-start | bytes 4718600 | tf_op jit(solution)/shard_map/ppermute | solution.py:139
  70.6 183.1 %collective-permute-start.13 = (bf16[12,256,256]{2,1,0:T(8,128)(2,1)}, bf16[12,256,256]{2,1,0:T(8,128)(2,1)}, u32[]{:S(2)}, u32[]{:S(2)}) collective-permute-start(bf16[12,256,256]{2,1,0:T(8,128)(2,1)} %convolution_convert_fusion.3), channel_id=1, source_target_pairs={{0,2},{3,1},{4,6},{7,5},{8,10},{11,9},{12,14},{15,13},{16,18},{19,... | collective-permute-start | bytes 4718600 | tf_op jit(solution)/shard_map/ppermute | solution.py:139
  140.1 107.8 %collective-permute-start.12 = (bf16[12,256,256]{2,1,0:T(8,128)(2,1)}, bf16[12,256,256]{2,1,0:T(8,128)(2,1)}, u32[]{:S(2)}, u32[]{:S(2)}) collective-permute-start(bf16[12,256,256]{2,1,0:T(8,128)(2,1)} %convolution_convert_fusion.4), channel_id=1, source_target_pairs={{0,1},{2,3},{3,0},{4,5},{6,7},{7,4},{8,9},{10,11},{11,8},{12,13},{... | collective-permute-start | bytes 4718600 | tf_op jit(solution)/shard_map/ppermute | solution.py:139
  145.3 3.8 %copy-start.11 = (bf16[4,256,256]{1,2,0:T(8,128)(2,1)S(1)}, bf16[4,256,256]{1,2,0:T(8,128)(2,1)}, u32[]{:S(2)}) copy-start(bf16[4,256,256]{1,2,0:T(8,128)(2,1)} %convolution_convert_fusion.17) | copy-start | bytes 1572868
  145.3 6.3 %copy-start.18 = (bf16[256,512,1]{0,1,2:T(8,128)(2,1)S(1)}, bf16[256,512,1]{0,1,2:T(8,128)(2,1)}, u32[]{:S(2)}) copy-start(bf16[256,512,1]{0,1,2:T(8,128)(2,1)} %get-tuple-element.15) | copy-start | bytes 786436
  147.8 97.4 %collective-permute-start.11 = (bf16[4,256,256]{2,1,0:T(8,128)(2,1)}, bf16[4,256,256]{2,1,0:T(8,128)(2,1)}, u32[]{:S(2)}, u32[]{:S(2)}) collective-permute-start(bf16[4,256,256]{2,1,0:T(8,128)(2,1)} %convolution_convert_fusion.6), channel_id=1, source_target_pairs={{2,3},{1,0},{6,7},{5,4},{10,11},{9,8},{14,15},{13,12},{18,19},{17,... | collective-permute-start | bytes 1572872 | tf_op jit(solution)/shard_map/ppermute | solution.py:152
  151.6 3.9 %copy-start.13 = (bf16[4,256,256]{1,2,0:T(8,128)(2,1)S(1)}, bf16[4,256,256]{1,2,0:T(8,128)(2,1)}, u32[]{:S(2)}) copy-start(bf16[4,256,256]{1,2,0:T(8,128)(2,1)} %convolution_convert_fusion.13) | copy-start | bytes 1572868
  154.0 38.5 %collective-permute-start.7 = (bf16[4,256,256]{2,1,0:T(8,128)(2,1)}, bf16[4,256,256]{2,1,0:T(8,128)(2,1)}, u32[]{:S(2)}, u32[]{:S(2)}) collective-permute-start(bf16[4,256,256]{2,1,0:T(8,128)(2,1)} %convolution_convert_fusion.14), channel_id=1, source_target_pairs={{2,3},{1,0},{6,7},{5,4},{10,11},{9,8},{14,15},{13,12},{18,19},{17,... | collective-permute-start | bytes 1572872 | tf_op jit(solution)/shard_map/ppermute | solution.py:152
  158.0 2.7 %copy-start.6 = (bf16[12,256,256]{1,2,0:T(8,128)(2,1)S(1)}, bf16[12,256,256]{1,2,0:T(8,128)(2,1)}, u32[]{:S(2)}) copy-start(bf16[12,256,256]{1,2,0:T(8,128)(2,1)} %convolution_convert_fusion.1) | copy-start | bytes 4718596
  158.0 2.7 %copy-start.17 = (bf16[256,512,1]{0,1,2:T(8,128)(2,1)S(1)}, bf16[256,512,1]{0,1,2:T(8,128)(2,1)}, u32[]{:S(2)}) copy-start(bf16[256,512,1]{0,1,2:T(8,128)(2,1)} %get-tuple-element.16) | copy-start | bytes 786436
  160.7 33.2 %copy-start.10 = (bf16[4,256,256]{1,2,0:T(8,128)(2,1)S(1)}, bf16[4,256,256]{1,2,0:T(8,128)(2,1)}, u32[]{:S(2)}) copy-start(bf16[4,256,256]{1,2,0:T(8,128)(2,1)} %convolution_convert_fusion.9) | copy-start | bytes 1572868
  160.7 33.2 %copy-start.19 = (bf16[4,256,256]{1,2,0:T(8,128)(2,1)S(1)}, bf16[4,256,256]{1,2,0:T(8,128)(2,1)}, u32[]{:S(2)}) copy-start(bf16[4,256,256]{1,2,0:T(8,128)(2,1)} %convolution_convert_fusion.8) | copy-start | bytes 1572868
  192.5 49.1 %collective-permute-start.9 = (bf16[4,256,256]{2,1,0:T(8,128)(2,1)}, bf16[4,256,256]{2,1,0:T(8,128)(2,1)S(1)}, u32[]{:S(2)}, u32[]{:S(2)}) collective-permute-start(bf16[4,256,256]{2,1,0:T(8,128)(2,1)} %convolution_convert_fusion.10), channel_id=1, source_target_pairs={{2,3},{1,0},{6,7},{5,4},{10,11},{9,8},{14,15},{13,12},{18,19},{17,... | collective-permute-start | bytes 1572872 | tf_op jit(solution)/shard_map/ppermute | solution.py:152
  195.1 6.1 %copy-start.12 = (bf16[4,256,256]{1,2,0:T(8,128)(2,1)S(1)}, bf16[4,256,256]{1,2,0:T(8,128)(2,1)}, u32[]{:S(2)}) copy-start(bf16[4,256,256]{1,2,0:T(8,128)(2,1)} %convolution_convert_fusion.17) | copy-start | bytes 1572868
  201.2 2.4 copy-start.14
  201.2 2.4 copy-start.20
  241.7 0.8 copy-start.8
  259.5 1.2 copy-start.4

commit v2 on v0

v2 whole, which is shorter than its diff:
```python
import functools

import jax
import jax.numpy as jnp
from jax import lax
from jax.experimental import pallas as pl
from jax.experimental.pallas import tpu as pltpu
from jax.sharding import PartitionSpec as P

VMEM_LIMIT = 40 * 1024 * 1024
BF16 = jnp.bfloat16


def dot(left, right):
    return jnp.dot(left, right, preferred_element_type=jnp.float32)


def factor_rows(rows, inverses_t, couple_t):
    size = couple_t.shape[0]
    left = dot(rows[:, :size], inverses_t[0]).astype(BF16)
    reduced = (rows[:, size:].astype(jnp.float32) - dot(left, couple_t)).astype(BF16)
    right = dot(reduced, inverses_t[1]).astype(BF16)
    return left, right


def times_key(left, right, key_t):
    size = left.shape[1]
    return dot(left, key_t[:size]) + dot(right, key_t[size:])


def special_source(col, cols):
    return jnp.where(col < cols // 2, cols // 2, cols // 2 - 1)


def keys_body(rows, info, same, other, inverses_t, couple_t, keys_t):
    size = couple_t.shape[0]

    def raw(tile):
        offset = info[0] ^ (tile % rows)
        index, place = offset // 2, tile // rows
        return jnp.where(offset % 2 == 0, same[index, place], other[index, place])

    couple = dot(raw(1)[:, :size], inverses_t[0]).astype(BF16)
    couple_t[...] = couple.astype(jnp.float32).T.astype(BF16)
    for j in range(keys_t.shape[0]):
        left, right = factor_rows(raw(j + 2), inverses_t, couple_t[...])
        keys_t[j, :size] = left.astype(jnp.float32).T.astype(BF16)
        keys_t[j, size:] = right.astype(jnp.float32).T.astype(BF16)


def make_keys(info, same, other, inverses_t, rows, cols):
    size, width = same.shape[2:]
    vmem = pl.BlockSpec(memory_space=pltpu.VMEM)
    return pl.pallas_call(
        functools.partial(keys_body, rows),
        in_specs=[pl.BlockSpec(memory_space=pltpu.SMEM), vmem, vmem, vmem],
        out_specs=[vmem, vmem],
        out_shape=[
            jax.ShapeDtypeStruct((size, size), BF16),
            jax.ShapeDtypeStruct((cols, width, size), BF16),
        ],
        compiler_params=pltpu.CompilerParams(vmem_limit_bytes=VMEM_LIMIT),
        cost_estimate=pl.CostEstimate(
            flops=8 * cols * size**3, bytes_accessed=8 * cols * width * size, transcendentals=0
        ),
    )(info, same, other, inverses_t)


def own_body(cols, info, panel, inverses_t, couple_t, keys_t, trailing, out, *pieces):
    part, size, width = panel.shape
    left, right = factor_rows(panel[...].reshape(part * size, width), inverses_t, couple_t[...])
    for offset in range(cols):
        total = times_key(left, right, keys_t[info[1] ^ offset]).reshape(part, size, size)
        if offset == 0:
            out[...] = (trailing[...].astype(jnp.float32) - total).astype(BF16)
        else:
            pieces[offset - 1][...] = total.astype(BF16)


def own_tiles(info, panel, inverses_t, couple_t, keys_t, trailing, part, near_raw, cols):
    tiles, size, width = panel.shape
    parts = tiles // part
    block = (part, size, size)

    def whole(array):
        return pl.BlockSpec(array.shape, lambda t, p: (0,) * array.ndim)

    mine = pl.BlockSpec(block, lambda t, p: (p[1] * parts + t, 0, 0))
    near = pl.BlockSpec(block, lambda t, p: (jnp.maximum(t - near_raw, 0), 0, 0))
    far = pl.BlockSpec(block, lambda t, p: (t, 0, 0))
    piece = jax.ShapeDtypeStruct((tiles, size, size), BF16)
    near_piece = jax.ShapeDtypeStruct((tiles - near_raw * part, size, size), BF16)
    return pl.pallas_call(
        functools.partial(own_body, cols),
        grid_spec=pltpu.PrefetchScalarGridSpec(
            num_scalar_prefetch=1,
            grid=(parts,),
            in_specs=[
                pl.BlockSpec((part, size, width), lambda t, p: (t, 0, 0)),
                whole(inverses_t),
                whole(couple_t),
                whole(keys_t),
                mine,
            ],
            out_specs=[mine, near] + [far] * (cols - 2),
        ),
        out_shape=[jax.ShapeDtypeStruct(trailing.shape, BF16), near_piece]
        + [piece] * (cols - 2),
        compiler_params=pltpu.CompilerParams(vmem_limit_bytes=VMEM_LIMIT),
        cost_estimate=pl.CostEstimate(
            flops=2 * tiles * size**3 * (3 + 2 * cols),
            bytes_accessed=2 * tiles * size * size * (3 + cols),
            transcendentals=0,
        ),
    )(info, panel, inverses_t, couple_t, keys_t, trailing)


def near_body(info, held, raw, inverses_t, couple_t, keys_t, trailing, out):
    del held
    part, size, width = raw.shape
    left, right = factor_rows(raw[...].reshape(part * size, width), inverses_t, couple_t[...])
    total = times_key(left, right, keys_t[info[1]]).reshape(part, size, size)
    out[...] = (trailing[...].astype(jnp.float32) - total).astype(BF16)


def near_tiles(info, held, raw, index, inverses_t, couple_t, keys_t, trailing, parts):
    part, size, width = raw.shape

    def whole(array):
        return pl.BlockSpec(array.shape, lambda t, p: (0,) * array.ndim)

    place = pl.BlockSpec((part, size, size), lambda t, p: ((p[1] ^ 1) * parts + index, 0, 0))
    return pl.pallas_call(
        near_body,
        grid_spec=pltpu.PrefetchScalarGridSpec(
            num_scalar_prefetch=1,
            grid=(1,),
            in_specs=[
                pl.BlockSpec(memory_space=pl.ANY),
                whole(raw),
                whole(inverses_t),
                whole(couple_t),
                whole(keys_t),
                place,
            ],
            out_specs=place,
        ),
        out_shape=jax.ShapeDtypeStruct(trailing.shape, BF16),
        input_output_aliases={1: 0},
        compiler_params=pltpu.CompilerParams(vmem_limit_bytes=VMEM_LIMIT),
        cost_estimate=pl.CostEstimate(
            flops=10 * part * size**3, bytes_accessed=8 * part * size * size, transcendentals=0
        ),
    )(info, held, raw, inverses_t, couple_t, keys_t, trailing)


def crossed_body(cols, info, held, raw, inverses_t, couple_t, keys_t, kept, *pieces):
    del held, kept
    part, size, width = raw.shape
    left, right = factor_rows(raw[...].reshape(part * size, width), inverses_t, couple_t[...])
    col = info[1]
    for k in range(cols // 2):
        target = jnp.clip(jnp.where(col < cols // 2, col - k, col + k), 0, cols - 1)
        total = times_key(left, right, keys_t[target])
        pieces[k][...] = total.reshape(part, size, size).astype(BF16)


def crossed_tiles(info, held, raw, inverses_t, couple_t, keys_t, cols):
    part, size, width = raw.shape
    vmem = pl.BlockSpec(memory_space=pltpu.VMEM)
    anywhere = pl.BlockSpec(memory_space=pl.ANY)
    pieces = [jax.ShapeDtypeStruct((part, size, size), BF16)] * (cols // 2)
    out = pl.pallas_call(
        functools.partial(crossed_body, cols),
        in_specs=[pl.BlockSpec(memory_space=pltpu.SMEM), anywhere, vmem, vmem, vmem, vmem],
        out_specs=[anywhere] + [vmem] * (cols // 2),
        out_shape=[jax.ShapeDtypeStruct(held.shape, BF16)] + pieces,
        input_output_aliases={1: 0},
        compiler_params=pltpu.CompilerParams(vmem_limit_bytes=VMEM_LIMIT),
        cost_estimate=pl.CostEstimate(
            flops=2 * part * size**3 * (3 + cols), bytes_accessed=8 * part * size * size, transcendentals=0
        ),
    )(info, held, raw, inverses_t, couple_t, keys_t)
    return out[0], out[1:]


def update_body(use_second, info, held, trailing, first, second, out):
    del held
    flag = use_second(info[1])

    @pl.when(jnp.logical_not(flag))
    def _():
        out[...] = (trailing[...].astype(jnp.float32) - first[...].astype(jnp.float32)).astype(BF16)

    @pl.when(flag)
    def _():
        out[...] = (trailing[...].astype(jnp.float32) - second[...].astype(jnp.float32)).astype(BF16)


def update(info, held, trailing, first, second, part, start, use_second):
    tiles, size, width = first.shape
    block = (part, size, width)
    place = pl.BlockSpec(block, lambda t, p: (start(p[1]) + t, 0, 0))
    return pl.pallas_call(
        functools.partial(update_body, use_second),
        grid_spec=pltpu.PrefetchScalarGridSpec(
            num_scalar_prefetch=1,
            grid=(tiles // part,),
            in_specs=[
                pl.BlockSpec(memory_space=pl.ANY),
                place,
                pl.BlockSpec(block, lambda t, p: (jnp.where(use_second(p[1]), 0, t), 0, 0)),
                pl.BlockSpec(block, lambda t, p: (jnp.where(use_second(p[1]), t, 0), 0, 0)),
            ],
            out_specs=place,
        ),
        out_shape=jax.ShapeDtypeStruct(trailing.shape, trailing.dtype),
        input_output_aliases={1: 0},
        compiler_params=pltpu.CompilerParams(vmem_limit_bytes=VMEM_LIMIT),
        cost_estimate=pl.CostEstimate(
            flops=first.size, bytes_accessed=6 * first.size, transcendentals=0
        ),
    )(info, held, trailing, first, second)


def spread_heads(head, rows, cols):
    wanted = sorted({tile % rows for tile in range(1, cols + 2)})
    col_index = lax.axis_index("col")
    span = cols // 2
    while span:
        pairs = [
            (r * cols + c, r * cols + c + span) for r in wanted for c in range(0, cols, 2 * span)
        ]
        arrived = lax.ppermute(head, ("row", "col"), pairs)
        head = jnp.where(col_index % (2 * span) == span, arrived, head)
        span //= 2
    same = [head]
    for offset in range(2, rows, 2):
        same.append(lax.ppermute(head, "row", [(r, r ^ offset) for r in wanted]))
    same = jnp.stack(same)
    return same, lax.ppermute(same, "row", [(r, r ^ 1) for r in range(rows)])


def shards(panel_cols, inverses, trailing):
    tiles = panel_cols.shape[0]
    rows = lax.axis_size("row")
    cols = lax.axis_size("col")
    low, high = cols // 2 - 1, cols // 2
    parts = 3 if tiles % 3 == 0 else 1
    part = tiles // parts
    near_raw = parts - 1
    info = jnp.stack([lax.axis_index("row"), lax.axis_index("col")]).astype(jnp.int32)
    inverses_t = jnp.swapaxes(inverses, 1, 2)

    chunks = [panel_cols[i * part:(i + 1) * part] for i in range(parts)]
    swap = [(low, high), (high, low)]
    beside = [(c, c ^ 1) for c in range(cols)]
    crossed = [lax.ppermute(chunk, "col", swap) for chunk in chunks]
    next_raw = [lax.ppermute(chunk, "col", beside) for chunk in chunks[:near_raw]]

    head_tiles = (cols + 1) // rows + 1
    same, other = spread_heads(panel_cols[:head_tiles], rows, cols)
    couple_t, keys_t = make_keys(info, same, other, inverses_t, rows, cols)
    small = (inverses_t, couple_t, keys_t)

    out, near, *far = own_tiles(info, panel_cols, *small, trailing, part, near_raw, cols)
    arrived = {1: lax.ppermute(near, "col", beside)}
    for offset in range(cols - 1, 1, -1):
        pairs = [
            (c, c ^ offset)
            for c in range(cols)
            if not (c == low and c ^ offset > low) and not (c == high and c ^ offset < high)
        ]
        arrived[offset] = lax.ppermute(far[offset - 2], "col", pairs)

    for i in range(near_raw):
        out = near_tiles(info, out, next_raw[i], i, *small, trailing, parts)

    outward = []
    col_index = lax.axis_index("col")
    for i in range(parts):
        out, (mine, *handed) = crossed_tiles(info, out, crossed[i], *small, cols)
        got = [
            lax.ppermute(handed[k], "col", [(high, high + k + 1), (low, low - k - 1)])
            for k in range(cols // 2 - 1)
        ]
        chosen = got[0]
        for k in range(1, len(got)):
            here = (col_index == high + k + 1) | (col_index == low - k - 1)
            chosen = jnp.where(here, got[k], chosen)
        outward.append((mine, chosen))

    never = lambda col: col < 0
    out = update(
        info, out, trailing, arrived[1], arrived[1], part,
        lambda col: (col ^ 1) * parts + near_raw, never,
    )

    def outer(col):
        return (col != low) & (col != high)

    for i, (mine, got) in enumerate(outward[:-1]):
        out = update(
            info, out, trailing, mine, got, part,
            lambda col, i=i: special_source(col, cols) * parts + i, outer,
        )
    for offset in range(2, cols - 1):
        def second(col, offset=offset):
            return (col ^ special_source(col, cols)) <= offset

        def source(col, offset=offset, second=second):
            return (col ^ jnp.where(second(col), offset + 1, offset)) * parts

        out = update(
            info, out, trailing, arrived[offset], arrived[offset + 1], part, source, second
        )
    mine, got = outward[-1]
    return update(
        info, out, trailing, mine, got, part,
        lambda col: special_source(col, cols) * parts + parts - 1, outer,
    )


def solution(mesh):
    in_specs = (P("col", "row", None), P(), P(None, "row", "col"))
    out_specs = P(None, "row", "col")
    return jax.shard_map(shards, mesh=mesh, in_specs=in_specs, out_specs=out_specs, check_vma=False)
```

time: 439 us -> 208 us (0.47)
  waiting for transfers between devices: 397 us -> 127 us
  starting transfers between devices: 0.09 us -> 35.4 us
  Pallas kernels: 0 us -> 32.5 us
  matrix products: 18.9 us -> 0 us
  between operations: 13.1 us -> 0.24 us
  local copies, waits for them, and re-layouts: 2.8 us -> 10.5 us
    all_gather x1 -> x0, waiting for transfers between devices: 217 us -> none  [shards(): whole_panel = lax.all_gather(factored, 'col', axis=0, tiled=True)]
    psum x2 -> x0, waiting for transfers between devices: 180 us -> none  [broadcast(): return lax.psum(kept, axis)]
    ppermute x0 -> x17, waiting for transfers between devices: none -> 127 us  [the longest x1 53.6 us: shards(): arrived = {1: lax.ppermute(near, 'col', beside)}]
    ppermute x0 -> x17, starting transfers between devices: none -> 35.4 us  [the longest x2 11.9 us: shards(): arrived[offset] = lax.ppermute(far[offset - 2], 'col', pairs)]
    pallas_call x0 -> x12, Pallas kernels: none -> 32.5 us  [the longest x5 8.37 us: update(): pl.pallas_call(functools.partial(update_body, use_second), grid_spec=pltp...]
    dot_general x3 -> x0, matrix products: 18.9 us -> none  [the longest x1 12.6 us: shards(): jnp.einsum('tak,bk->tab', whole_panel, key_tile, preferred_element_type=j...]
    unnamed x4 -> x9, local copies, waits for them, and re-layouts: 0.01 us -> 5.76 us
    slice x0 -> x2, local copies, waits for them, and re-layouts: none -> 4.72 us  [the longest x1 3.75 us: shards(): chunks = [panel_cols[i * part:(i + 1) * part] for i in range(parts)]]
  transfers between devices with their start and end apart: 3 -> 17, of which waited for: 3 -> 10; matrix products, arithmetic and copies ran while one was open for 0% -> 2% of each run, Pallas kernels for 0% -> 15%
where the time goes in v2:
time: 208 us; the launch traced here: 207 us
  waiting for transfers between devices  127 us (61%)
  starting transfers between devices  35.4 us (17%)
  Pallas kernels  32.5 us (16%)
  local copies, waits for them, and re-layouts  10.5 us (5%)
    ppermute x1, waiting for transfers between devices, shards(): arrived = {1: lax.ppermute(near, 'col', beside)}  53.6 us
    ppermute x3, waiting for transfers between devices, shards(): lax.ppermute(handed[k], 'col', [(high, high + k + 1), (low, low - k - 1)])  33.6 us
    ppermute x2, waiting for transfers between devices, shards(): lax.ppermute(chunk, 'col', beside)  21 us
    ppermute x2, starting transfers between devices, shards(): arrived[offset] = lax.ppermute(far[offset - 2], 'col', pairs)  11.9 us
    ppermute x2, waiting for transfers between devices, spread_heads(): arrived = lax.ppermute(head, ('row', 'col'), pairs)  10.4 us
    ppermute x3, waiting for transfers between devices, spread_heads(): same.append(lax.ppermute(head, 'row', [(r, r ^ offset) for r in wanted]))  8.61 us
    pallas_call x5, Pallas kernels, update(): pl.pallas_call(functools.partial(update_body, use_second), grid_spec=pltp...  8.37 us
    pallas_call x2, Pallas kernels, near_tiles(): pl.pallas_call(near_body, grid_spec=pltpu.PrefetchScalarGridSpec(num_scal...  7.59 us
  transfers between devices with their start and end apart: 17, of which 10 were waited for; matrix products, arithmetic and copies ran while one was open for 2% of the time, Pallas kernels for 15%

profile of v2, /device:TPU:4, one launch (start us, length us, event | category | flops | bytes accessed | tf_op | source)
XLA Modules:
  0.0 207.1 jit_solution(6324093760753506137)
XLA Ops:
  0.0 1.0 slice.12
  1.0 4.5 %collective-permute-start = (bf16[1,256,512]{2,1,0:T(8,128)(2,1)S(1)}, bf16[1,256,512]{2,1,0:T(8,128)(2,1)S(1)}, u32[]{:S(2)}, u32[]{:S(2)}) collective-permute-start(bf16[1,256,512]{2,1,0:T(8,128)(2,1)S(1)} %slice.12), channel_id=1, source_target_pairs={{4,6},{8,10},{12,14},{16,18},{20,22}} | collective-permute-start | bytes 786440 | tf_op jit(solution)/shard_map/ppermute | solution.py:234
  5.5 5.5 %collective-permute-done = bf16[1,256,512]{2,1,0:T(8,128)(2,1)S(1)} collective-permute-done((bf16[1,256,512]{2,1,0:T(8,128)(2,1)S(1)}, bf16[1,256,512]{2,1,0:T(8,128)(2,1)S(1)}, u32[]{:S(2)}, u32[]{:S(2)}) %collective-permute-start) | collective-permute-done | bytes 262176 | tf_op jit(solution)/shard_map/ppermute | solution.py:234
  11.0 1.0 broadcast_select_fusion
  12.0 1.3 collective-permute-start.1
  13.3 4.9 %collective-permute-done.1 = bf16[1,256,512]{2,1,0:T(8,128)(2,1)S(1)} collective-permute-done((bf16[1,256,512]{2,1,0:T(8,128)(2,1)S(1)}, bf16[1,256,512]{2,1,0:T(8,128)(2,1)S(1)}, u32[]{:S(2)}, u32[]{:S(2)}) %collective-permute-start.1) | collective-permute-done | bytes 262176 | tf_op jit(solution)/shard_map/ppermute | solution.py:234
  18.3 1.3 collective-permute-start.2
  19.6 1.3 collective-permute-start.3
  20.9 3.3 %collective-permute-start.4 = (bf16[1,256,512]{2,1,0:T(8,128)(2,1)S(1)}, bf16[1,256,512]{2,1,0:T(8,128)(2,1)S(1)}, u32[]{:S(2)}, u32[]{:S(2)}) collective-permute-start(bf16[1,256,512]{2,1,0:T(8,128)(2,1)S(1)} %broadcast_select_fusion.1), channel_id=1, source_target_pairs={{4,28},{8,16},{12,20},{16,8},{20,12},{5,29},{9,17},{13,21},{17,9},... | collective-permute-start | bytes 786440 | tf_op jit(solution)/shard_map/ppermute | solution.py:239
  24.3 0.0 collective-permute-done.2
  24.3 3.0 %collective-permute-done.3 = bf16[1,256,512]{2,1,0:T(8,128)(2,1)S(1)} collective-permute-done((bf16[1,256,512]{2,1,0:T(8,128)(2,1)S(1)}, bf16[1,256,512]{2,1,0:T(8,128)(2,1)S(1)}, u32[]{:S(2)}, u32[]{:S(2)}) %collective-permute-start.3) | collective-permute-done | bytes 262176 | tf_op jit(solution)/shard_map/ppermute | solution.py:239
  27.3 5.6 %collective-permute-done.4 = bf16[1,256,512]{2,1,0:T(8,128)(2,1)S(1)} collective-permute-done((bf16[1,256,512]{2,1,0:T(8,128)(2,1)S(1)}, bf16[1,256,512]{2,1,0:T(8,128)(2,1)S(1)}, u32[]{:S(2)}, u32[]{:S(2)}) %collective-permute-start.4) | collective-permute-done | bytes 262176 | tf_op jit(solution)/shard_map/ppermute | solution.py:239
  32.9 0.1 pad_maximum_fusion.same
  33.0 0.2 collective-permute-start.5
  33.2 0.0 slice-start
  33.2 3.8 %fusion = (bf16[4,256,512]{2,1,0:T(8,128)(2,1)}, bf16[4,256,512]{2,1,0:T(8,128)(2,1)}, bf16[4,256,512]{2,1,0:T(8,128)(2,1)}) fusion(bf16[12,256,512]{2,1,0:T(8,128)(2,1)} %panel.1), kind=kLoop, calls=%fused_computation.4 | loop fusion | bytes 6291456 | tf_op jit(solution)/shard_map/slice | solution.py:255
  37.0 2.5 %collective-permute-start.6 = (bf16[4,256,512]{2,1,0:T(8,128)(2,1)}, bf16[4,256,512]{2,1,0:T(8,128)(2,1)}, u32[]{:S(2)}, u32[]{:S(2)}) collective-permute-start(bf16[4,256,512]{2,1,0:T(8,128)(2,1)} %get-tuple-element.36), channel_id=1, source_target_pairs={{0,1},{1,0},{2,3},{3,2},{4,5},{5,4},{6,7},{7,6},{8,9},{9,8},{10,11... | collective-permute-start | bytes 3145736 | tf_op jit(solution)/shard_map/ppermute | solution.py:259
  39.4 0.0 collective-permute-start.7
  39.5 1.7 collective-permute-start.8
  41.2 1.7 collective-permute-start.9
  42.9 1.1 copy.14
  44.0 0.1 pad_add_fusion.info
  44.0 0.0 collective-permute-done.5.other
  44.0 1.7 collective-permute-start.10
  45.8 2.4 %shard_map.37 = (bf16[256,256]{1,0:T(8,128)(2,1)S(1)}, bf16[4,512,256]{2,1,0:T(8,128)(2,1)S(1)}) custom-call(s32[2]{0:T(128)S(1)} %pad_add_fusion.info, bf16[4,1,256,512]{3,2,1,0:T(8,128)(2,1)S(1)} %pad_maximum_fusion.same, bf16[4,1,256,512]{3,2,1,0:T(8,128)(2,1)} %collective-permute-done.5.other, bf16[2,256,256]{2,1,0:T(8,128)(2,1)S(1)} %bitcast.9), custom_call_target="tpu_custom_call" | custom-call | flops 536870912 | bytes 4194304 | tf_op jit(solution)/shard_map/pallas_call | solution.py:54
  48.2 0.0 copy-start
  48.2 2.8 %copy-done = bf16[48,256,256]{2,1,0:T(8,128)(2,1)S(1)} copy-done((bf16[48,256,256]{2,1,0:T(8,128)(2,1)S(1)}, bf16[48,256,256]{2,1,0:T(8,128)(2,1)}, u32[]{:S(2)}) %copy-start) | copy-done | bytes 6291480
  51.0 0.0 copy-start.1
  51.0 1.9 copy-done.1
  52.9 0.0 slice-start.1
  52.9 6.6 %shard_map.38 = (bf16[48,256,256]{2,1,0:T(8,128)(2,1)}, bf16[4,256,256]{2,1,0:T(8,128)(2,1)S(1)}, bf16[12,256,256]{2,1,0:T(8,128)(2,1)S(1)}, bf16[12,256,256]{2,1,0:T(8,128)(2,1)S(1)}) custom-call(s32[2]{0:T(128)S(1)} %pad_add_fusion.info, bf16[12,256,512]{2,1,0:T(8,128)(2,1)S(1)} %copy-done.1, bf16[2,256,256]{2,1,0:T(8,128)(2,1)S(1)} %bitcast.10, ...), custom_call_target="tpu_custom_call" | custom-call | flops 4429185024 | bytes 11010048 | tf_op jit(solution)/shard_map/pallas_call | solution.py:93
  59.5 4.2 %collective-permute-done.6.raw = bf16[4,256,512]{2,1,0:T(8,128)(2,1)} collective-permute-done((bf16[4,256,512]{2,1,0:T(8,128)(2,1)}, bf16[4,256,512]{2,1,0:T(8,128)(2,1)}, u32[]{:S(2)}, u32[]{:S(2)}) %collective-permute-start.6) | collective-permute-done | bytes 1048608 | tf_op jit(solution)/shard_map/ppermute | solution.py:259
  63.7 5.4 %collective-permute-start.14 = (bf16[12,256,256]{2,1,0:T(8,128)(2,1)S(1)}, bf16[12,256,256]{2,1,0:T(8,128)(2,1)S(1)}, u32[]{:S(2)}, u32[]{:S(2)}) collective-permute-start(bf16[12,256,256]{2,1,0:T(8,128)(2,1)S(1)} %get-tuple-element.31), channel_id=1, source_target_pairs={{0,2},{3,1},{4,6},{7,5},{8,10},{11,9},{12,14},{15,13},{16,18},{19,... | collective-permute-start | bytes 4718600 | tf_op jit(solution)/shard_map/ppermute | solution.py:274
  69.1 16.8 %collective-permute-done.7.raw = bf16[4,256,512]{2,1,0:T(8,128)(2,1)} collective-permute-done((bf16[4,256,512]{2,1,0:T(8,128)(2,1)}, bf16[4,256,512]{2,1,0:T(8,128)(2,1)}, u32[]{:S(2)}, u32[]{:S(2)}) %collective-permute-start.7) | collective-permute-done | bytes 1048608 | tf_op jit(solution)/shard_map/ppermute | solution.py:259
  85.9 6.5 %collective-permute-start.15 = (bf16[12,256,256]{2,1,0:T(8,128)(2,1)S(1)}, bf16[12,256,256]{2,1,0:T(8,128)(2,1)S(1)}, u32[]{:S(2)}, u32[]{:S(2)}) collective-permute-start(bf16[12,256,256]{2,1,0:T(8,128)(2,1)S(1)} %get-tuple-element.32), channel_id=1, source_target_pairs={{0,3},{3,0},{4,7},{7,4},{8,11},{11,8},{12,15},{15,12},{16,19},{19,... | collective-permute-start | bytes 4718600 | tf_op jit(solution)/shard_map/ppermute | solution.py:274
  92.4 0.0 collective-permute-done.8.raw
  92.5 0.1 collective-permute-start.11
  92.5 0.0 slice-done
  92.5 0.0 slice-done.1
  92.6 3.8 %shard_map.39.held = bf16[48,256,256]{2,1,0:T(8,128)(2,1)} custom-call(s32[2]{0:T(128)S(1)} %pad_add_fusion.info, bf16[48,256,256]{2,1,0:T(8,128)(2,1)} %get-tuple-element.22.held, bf16[4,256,512]{2,1,0:T(8,128)(2,1)} %collective-permute-done.6.raw, bf16[2,256,256]{2,1,0:T(8,128)(2,1)S(1)} %bitcast.11, ...), custom_call_target="tpu_custom_call", output_to_operand_aliasing={{}: (1, {})} | custom-call | flops 671088640 | bytes 2097152 | tf_op jit(solution)/shard_map/pallas_call | solution.py:133
  96.4 3.8 %shard_map.40.held = bf16[48,256,256]{2,1,0:T(8,128)(2,1)} custom-call(s32[2]{0:T(128)S(1)} %pad_add_fusion.info, bf16[48,256,256]{2,1,0:T(8,128)(2,1)} %shard_map.39.held, bf16[4,256,512]{2,1,0:T(8,128)(2,1)} %collective-permute-done.7.raw, bf16[2,256,256]{2,1,0:T(8,128)(2,1)S(1)} %bitcast.12, ...), custom_call_target="tpu_custom_call", output_to_operand_aliasing={{}: (1, {})} | custom-call | flops 671088640 | bytes 2097152 | tf_op jit(solution)/shard_map/pallas_call | solution.py:133
  100.1 2.5 %shard_map.41 = (bf16[48,256,256]{2,1,0:T(8,128)(2,1)}, bf16[4,256,256]{2,1,0:T(8,128)(2,1)S(1)}, bf16[4,256,256]{2,1,0:T(8,128)(2,1)S(1)}) custom-call(s32[2]{0:T(128)S(1)} %pad_add_fusion.info, bf16[48,256,256]{2,1,0:T(8,128)(2,1)} %shard_map.40.held, bf16[4,256,512]{2,1,0:T(8,128)(2,1)} %collective-permute-done.8.raw, ...), custom_call_target="tpu_custom_call", output_to_operand_aliasing={{0}: (1, {})} | custom-call | flops 939524096 | bytes 2097152 | tf_op jit(solution)/shard_map/pallas_call | solution.py:173
  102.6 0.0 collective-permute-done.9.raw
  102.6 1.3 collective-permute-start.12
  103.9 2.5 %shard_map.42 = (bf16[48,256,256]{2,1,0:T(8,128)(2,1)}, bf16[4,256,256]{2,1,0:T(8,128)(2,1)S(1)}, bf16[4,256,256]{2,1,0:T(8,128)(2,1)S(1)}) custom-call(s32[2]{0:T(128)S(1)} %pad_add_fusion.info, bf16[48,256,256]{2,1,0:T(8,128)(2,1)} %get-tuple-element.23.held, bf16[4,256,512]{2,1,0:T(8,128)(2,1)} %collective-permute-done.9.raw, ...), custom_call_target="tpu_custom_call", output_to_operand_aliasing={{0}: (1, {})} | custom-call | flops 939524096 | bytes 2097152 | tf_op jit(solution)/shard_map/pallas_call | solution.py:173
  106.4 0.0 collective-permute-done.10.raw
  106.4 1.3 collective-permute-start.13
  107.7 2.5 %shard_map.43 = (bf16[48,256,256]{2,1,0:T(8,128)(2,1)}, bf16[4,256,256]{2,1,0:T(8,128)(2,1)S(1)}, bf16[4,256,256]{2,1,0:T(8,128)(2,1)S(1)}) custom-call(s32[2]{0:T(128)S(1)} %pad_add_fusion.info, bf16[48,256,256]{2,1,0:T(8,128)(2,1)} %get-tuple-element.24.held, bf16[4,256,512]{2,1,0:T(8,128)(2,1)} %collective-permute-done.10.raw, ...), custom_call_target="tpu_custom_call", output_to_operand_aliasing={{0}: (1, {})} | custom-call | flops 939524096 | bytes 2097152 | tf_op jit(solution)/shard_map/pallas_call | solution.py:173
  110.2 53.6 %collective-permute-done.11.first.second = bf16[4,256,256]{2,1,0:T(8,128)(2,1)S(1)} collective-permute-done((bf16[4,256,256]{2,1,0:T(8,128)(2,1)S(1)}, bf16[4,256,256]{2,1,0:T(8,128)(2,1)S(1)}, u32[]{:S(2)}, u32[]{:S(2)}) %collective-permute-start.11) | collective-permute-done | bytes 524320 | tf_op jit(solution)/shard_map/ppermute | solution.py:267
  163.8 1.3 collective-permute-start.16
  165.1 1.5 shard_map.44.held
  166.6 5.3 %collective-permute-done.12.second = bf16[4,256,256]{2,1,0:T(8,128)(2,1)S(1)} collective-permute-done((bf16[4,256,256]{2,1,0:T(8,128)(2,1)S(1)}, bf16[4,256,256]{2,1,0:T(8,128)(2,1)S(1)}, u32[]{:S(2)}, u32[]{:S(2)}) %collective-permute-start.12) | collective-permute-done | bytes 524320 | tf_op jit(solution)/shard_map/ppermute | solution.py:284
  171.9 1.5 shard_map.45.held
  173.4 22.1 %collective-permute-done.13.second = bf16[4,256,256]{2,1,0:T(8,128)(2,1)S(1)} collective-permute-done((bf16[4,256,256]{2,1,0:T(8,128)(2,1)S(1)}, bf16[4,256,256]{2,1,0:T(8,128)(2,1)S(1)}, u32[]{:S(2)}, u32[]{:S(2)}) %collective-permute-start.13) | collective-permute-done | bytes 524320 | tf_op jit(solution)/shard_map/ppermute | solution.py:284
  195.5 1.5 shard_map.46.held
  197.0 0.0 collective-permute-done.14.first
  197.0 0.0 collective-permute-done.15.second
  197.0 2.5 %shard_map.47.held = bf16[48,256,256]{2,1,0:T(8,128)(2,1)} custom-call(s32[2]{0:T(128)S(1)} %pad_add_fusion.info, bf16[48,256,256]{2,1,0:T(8,128)(2,1)} %shard_map.46.held, bf16[48,256,256]{2,1,0:T(8,128)(2,1)S(1)} %bitcast.8, bf16[12,256,256]{2,1,0:T(8,128)(2,1)S(1)} %collective-permute-done.14.first, ...), custom_call_target="tpu_custom_call", output_to_operand_aliasing={{}: (1, {})} | custom-call | flops 786432 | bytes 4718592 | tf_op jit(solution)/shard_map/pallas_call | solution.py:204
  199.4 6.2 %collective-permute-done.16.second = bf16[4,256,256]{2,1,0:T(8,128)(2,1)S(1)} collective-permute-done((bf16[4,256,256]{2,1,0:T(8,128)(2,1)S(1)}, bf16[4,256,256]{2,1,0:T(8,128)(2,1)S(1)}, u32[]{:S(2)}, u32[]{:S(2)}) %collective-permute-start.16) | collective-permute-done | bytes 524320 | tf_op jit(solution)/shard_map/ppermute | solution.py:284
  205.6 1.5 shard_map.48
  (2 shorter events, 0.0 us)
Async XLA Ops:
  1.0 10.0 %collective-permute-start = (bf16[1,256,512]{2,1,0:T(8,128)(2,1)S(1)}, bf16[1,256,512]{2,1,0:T(8,128)(2,1)S(1)}, u32[]{:S(2)}, u32[]{:S(2)}) collective-permute-start(bf16[1,256,512]{2,1,0:T(8,128)(2,1)S(1)} %slice.12), channel_id=1, source_target_pairs={{4,6},{8,10},{12,14},{16,18},{20,22}} | collective-permute-start | bytes 786440 | tf_op jit(solution)/shard_map/ppermute | solution.py:234
  12.0 6.3 %collective-permute-start.1 = (bf16[1,256,512]{2,1,0:T(8,128)(2,1)S(1)}, bf16[1,256,512]{2,1,0:T(8,128)(2,1)S(1)}, u32[]{:S(2)}, u32[]{:S(2)}) collective-permute-start(bf16[1,256,512]{2,1,0:T(8,128)(2,1)S(1)} %broadcast_select_fusion), channel_id=1, source_target_pairs={{4,5},{6,7},{8,9},{10,11},{12,13},{14,15},{16,17},{18,19},{20,21},... | collective-permute-start | bytes 786440 | tf_op jit(solution)/shard_map/ppermute | solution.py:234
  18.3 6.0 %collective-permute-start.2 = (bf16[1,256,512]{2,1,0:T(8,128)(2,1)S(1)}, bf16[1,256,512]{2,1,0:T(8,128)(2,1)S(1)}, u32[]{:S(2)}, u32[]{:S(2)}) collective-permute-start(bf16[1,256,512]{2,1,0:T(8,128)(2,1)S(1)} %broadcast_select_fusion.1), channel_id=1, source_target_pairs={{4,12},{8,0},{12,4},{16,24},{20,28},{5,13},{9,1},{13,5},{17,25},{2... | collective-permute-start | bytes 786440 | tf_op jit(solution)/shard_map/ppermute | solution.py:239
  19.6 7.7 %collective-permute-start.3 = (bf16[1,256,512]{2,1,0:T(8,128)(2,1)S(1)}, bf16[1,256,512]{2,1,0:T(8,128)(2,1)S(1)}, u32[]{:S(2)}, u32[]{:S(2)}) collective-permute-start(bf16[1,256,512]{2,1,0:T(8,128)(2,1)S(1)} %broadcast_select_fusion.1), channel_id=1, source_target_pairs={{4,20},{8,24},{12,28},{16,0},{20,4},{5,21},{9,25},{13,29},{17,1},{... | collective-permute-start | bytes 786440 | tf_op jit(solution)/shard_map/ppermute | solution.py:239
  20.9 12.0 %collective-permute-start.4 = (bf16[1,256,512]{2,1,0:T(8,128)(2,1)S(1)}, bf16[1,256,512]{2,1,0:T(8,128)(2,1)S(1)}, u32[]{:S(2)}, u32[]{:S(2)}) collective-permute-start(bf16[1,256,512]{2,1,0:T(8,128)(2,1)S(1)} %broadcast_select_fusion.1), channel_id=1, source_target_pairs={{4,28},{8,16},{12,20},{16,8},{20,12},{5,29},{9,17},{13,21},{17,9},... | collective-permute-start | bytes 786440 | tf_op jit(solution)/shard_map/ppermute | solution.py:239
  33.0 11.0 %collective-permute-start.5 = (bf16[4,1,256,512]{3,2,1,0:T(8,128)(2,1)S(1)}, bf16[4,1,256,512]{3,2,1,0:T(8,128)(2,1)}, u32[]{:S(2)}, u32[]{:S(2)}) collective-permute-start(bf16[4,1,256,512]{3,2,1,0:T(8,128)(2,1)S(1)} %pad_maximum_fusion.same), channel_id=1, source_target_pairs={{0,4},{4,0},{8,12},{12,8},{16,20},{20,16},{24,28},{28,24},{1,5},{5... | collective-permute-start | bytes 3145736 | tf_op jit(solution)/shard_map/ppermute | solution.py:241
  33.2 59.3 %slice-start = ((s8[6291456]{0:T(1024)(128)(4,1)}), s8[2097152]{0:T(1024)(128)(4,1)S(1)}, s32[]{:S(2)}) async-start(s8[6291456]{0:T(1024)(128)(4,1)} %bitcast.7), calls=%async_computation | async-start | bytes 4194304
  37.0 26.8 %collective-permute-start.6 = (bf16[4,256,512]{2,1,0:T(8,128)(2,1)}, bf16[4,256,512]{2,1,0:T(8,128)(2,1)}, u32[]{:S(2)}, u32[]{:S(2)}) collective-permute-start(bf16[4,256,512]{2,1,0:T(8,128)(2,1)} %get-tuple-element.36), channel_id=1, source_target_pairs={{0,1},{1,0},{2,3},{3,2},{4,5},{5,4},{6,7},{7,6},{8,9},{9,8},{10,11... | collective-permute-start | bytes 3145736 | tf_op jit(solution)/shard_map/ppermute | solution.py:259
  39.4 46.5 %collective-permute-start.7 = (bf16[4,256,512]{2,1,0:T(8,128)(2,1)}, bf16[4,256,512]{2,1,0:T(8,128)(2,1)}, u32[]{:S(2)}, u32[]{:S(2)}) collective-permute-start(bf16[4,256,512]{2,1,0:T(8,128)(2,1)} %get-tuple-element.37), channel_id=1, source_target_pairs={{0,1},{1,0},{2,3},{3,2},{4,5},{5,4},{6,7},{7,6},{8,9},{9,8},{10,11... | collective-permute-start | bytes 3145736 | tf_op jit(solution)/shard_map/ppermute | solution.py:259
  39.5 53.0 %collective-permute-start.8 = (bf16[4,256,512]{2,1,0:T(8,128)(2,1)}, bf16[4,256,512]{2,1,0:T(8,128)(2,1)}, u32[]{:S(2)}, u32[]{:S(2)}) collective-permute-start(bf16[4,256,512]{2,1,0:T(8,128)(2,1)} %get-tuple-element.36), channel_id=1, source_target_pairs={{1,2},{2,1},{5,6},{6,5},{9,10},{10,9},{13,14},{14,13},{17,18},{18,... | collective-permute-start | bytes 3145736 | tf_op jit(solution)/shard_map/ppermute | solution.py:258
  41.2 61.4 %collective-permute-start.9 = (bf16[4,256,512]{2,1,0:T(8,128)(2,1)}, bf16[4,256,512]{2,1,0:T(8,128)(2,1)}, u32[]{:S(2)}, u32[]{:S(2)}) collective-permute-start(bf16[4,256,512]{2,1,0:T(8,128)(2,1)} %get-tuple-element.37), channel_id=1, source_target_pairs={{1,2},{2,1},{5,6},{6,5},{9,10},{10,9},{13,14},{14,13},{17,18},{18,... | collective-permute-start | bytes 3145736 | tf_op jit(solution)/shard_map/ppermute | solution.py:258
  44.0 62.4 %collective-permute-start.10 = (bf16[4,256,512]{2,1,0:T(8,128)(2,1)}, bf16[4,256,512]{2,1,0:T(8,128)(2,1)}, u32[]{:S(2)}, u32[]{:S(2)}) collective-permute-start(bf16[4,256,512]{2,1,0:T(8,128)(2,1)} %get-tuple-element.35), channel_id=1, source_target_pairs={{1,2},{2,1},{5,6},{6,5},{9,10},{10,9},{13,14},{14,13},{17,18},{18,... | collective-permute-start | bytes 3145736 | tf_op jit(solution)/shard_map/ppermute | solution.py:258
  48.2 2.8 %copy-start = (bf16[48,256,256]{2,1,0:T(8,128)(2,1)S(1)}, bf16[48,256,256]{2,1,0:T(8,128)(2,1)}, u32[]{:S(2)}) copy-start(bf16[48,256,256]{2,1,0:T(8,128)(2,1)} %trailing.15) | copy-start | bytes 18874372
  51.0 1.9 copy-start.1
  52.9 39.6 %slice-start.1 = ((s8[6291456]{0:T(1024)(128)(4,1)}), s8[4194304]{0:T(1024)(128)(4,1)S(1)}, s32[]{:S(2)}) async-start(s8[6291456]{0:T(1024)(128)(4,1)} %bitcast.7), calls=%async_computation.1 | async-start | bytes 8388608
  63.7 133.2 %collective-permute-start.14 = (bf16[12,256,256]{2,1,0:T(8,128)(2,1)S(1)}, bf16[12,256,256]{2,1,0:T(8,128)(2,1)S(1)}, u32[]{:S(2)}, u32[]{:S(2)}) collective-permute-start(bf16[12,256,256]{2,1,0:T(8,128)(2,1)S(1)} %get-tuple-element.31), channel_id=1, source_target_pairs={{0,2},{3,1},{4,6},{7,5},{8,10},{11,9},{12,14},{15,13},{16,18},{19,... | collective-permute-start | bytes 4718600 | tf_op jit(solution)/shard_map/ppermute | solution.py:274
  85.9 111.0 %collective-permute-start.15 = (bf16[12,256,256]{2,1,0:T(8,128)(2,1)S(1)}, bf16[12,256,256]{2,1,0:T(8,128)(2,1)S(1)}, u32[]{:S(2)}, u32[]{:S(2)}) collective-permute-start(bf16[12,256,256]{2,1,0:T(8,128)(2,1)S(1)} %get-tuple-element.32), channel_id=1, source_target_pairs={{0,3},{3,0},{4,7},{7,4},{8,11},{11,8},{12,15},{15,12},{16,19},{19,... | collective-permute-start | bytes 4718600 | tf_op jit(solution)/shard_map/ppermute | solution.py:274
  92.5 71.4 %collective-permute-start.11 = (bf16[4,256,256]{2,1,0:T(8,128)(2,1)S(1)}, bf16[4,256,256]{2,1,0:T(8,128)(2,1)S(1)}, u32[]{:S(2)}, u32[]{:S(2)}) collective-permute-start(bf16[4,256,256]{2,1,0:T(8,128)(2,1)S(1)} %get-tuple-element.26), channel_id=1, source_target_pairs={{0,1},{1,0},{2,3},{3,2},{4,5},{5,4},{6,7},{7,6},{8,9},{9,8},{10,11... | collective-permute-start | bytes 1572872 | tf_op jit(solution)/shard_map/ppermute | solution.py:267
  102.6 69.3 %collective-permute-start.12 = (bf16[4,256,256]{2,1,0:T(8,128)(2,1)S(1)}, bf16[4,256,256]{2,1,0:T(8,128)(2,1)S(1)}, u32[]{:S(2)}, u32[]{:S(2)}) collective-permute-start(bf16[4,256,256]{2,1,0:T(8,128)(2,1)S(1)} %get-tuple-element.28), channel_id=1, source_target_pairs={{2,3},{1,0},{6,7},{5,4},{10,11},{9,8},{14,15},{13,12},{18,19},{17,... | collective-permute-start | bytes 1572872 | tf_op jit(solution)/shard_map/ppermute | solution.py:284
  106.4 89.1 %collective-permute-start.13 = (bf16[4,256,256]{2,1,0:T(8,128)(2,1)S(1)}, bf16[4,256,256]{2,1,0:T(8,128)(2,1)S(1)}, u32[]{:S(2)}, u32[]{:S(2)}) collective-permute-start(bf16[4,256,256]{2,1,0:T(8,128)(2,1)S(1)} %get-tuple-element.30), channel_id=1, source_target_pairs={{2,3},{1,0},{6,7},{5,4},{10,11},{9,8},{14,15},{13,12},{18,19},{17,... | collective-permute-start | bytes 1572872 | tf_op jit(solution)/shard_map/ppermute | solution.py:284
  163.8 41.8 %collective-permute-start.16 = (bf16[4,256,256]{2,1,0:T(8,128)(2,1)S(1)}, bf16[4,256,256]{2,1,0:T(8,128)(2,1)S(1)}, u32[]{:S(2)}, u32[]{:S(2)}) collective-permute-start(bf16[4,256,256]{2,1,0:T(8,128)(2,1)S(1)} %get-tuple-element.34), channel_id=1, source_target_pairs={{2,3},{1,0},{6,7},{5,4},{10,11},{9,8},{14,15},{13,12},{18,19},{17,... | collective-permute-start | bytes 1572872 | tf_op jit(solution)/shard_map/ppermute | solution.py:284

commit v3 on v2

v3 whole, which is shorter than its diff:
```python
import functools

import jax
import jax.numpy as jnp
from jax import lax
from jax.experimental import pallas as pl
from jax.experimental.pallas import tpu as pltpu
from jax.sharding import PartitionSpec as P

VMEM_LIMIT = 40 * 1024 * 1024
BF16 = jnp.bfloat16
SMALL_COST = pl.CostEstimate(flops=1024, bytes_accessed=1024, transcendentals=0)


def dot(left, right):
    return jnp.dot(left, right, preferred_element_type=jnp.float32)


def factor_rows(rows, inverses_t, couple_t):
    size = couple_t.shape[0]
    left = dot(rows[:, :size], inverses_t[0]).astype(BF16)
    reduced = (rows[:, size:].astype(jnp.float32) - dot(left, couple_t)).astype(BF16)
    right = dot(reduced, inverses_t[1]).astype(BF16)
    return left, right


def times_key(left, right, key_t):
    size = left.shape[1]
    return dot(left, key_t[:size]) + dot(right, key_t[size:])


def special_source(col, cols):
    return jnp.where(col < cols // 2, cols // 2, cols // 2 - 1)


def keys_body(rows, info, same, other, inverses_t, couple_t, keys_t):
    size = couple_t.shape[0]

    def raw(tile):
        offset = info[0] ^ (tile % rows)
        index, place = offset // 2, tile // rows
        return jnp.where(offset % 2 == 0, same[index, place], other[index, place])

    couple = dot(raw(1)[:, :size], inverses_t[0]).astype(BF16)
    couple_t[...] = couple.astype(jnp.float32).T.astype(BF16)
    for j in range(keys_t.shape[0]):
        left, right = factor_rows(raw(j + 2), inverses_t, couple_t[...])
        keys_t[j, :size] = left.astype(jnp.float32).T.astype(BF16)
        keys_t[j, size:] = right.astype(jnp.float32).T.astype(BF16)


def make_keys(info, same, other, inverses_t, rows, cols):
    size, width = same.shape[2:]
    vmem = pl.BlockSpec(memory_space=pltpu.VMEM)
    return pl.pallas_call(
        functools.partial(keys_body, rows),
        in_specs=[pl.BlockSpec(memory_space=pltpu.SMEM), vmem, vmem, vmem],
        out_specs=[vmem, vmem],
        out_shape=[
            jax.ShapeDtypeStruct((size, size), BF16),
            jax.ShapeDtypeStruct((cols, width, size), BF16),
        ],
        compiler_params=pltpu.CompilerParams(vmem_limit_bytes=VMEM_LIMIT),
        cost_estimate=SMALL_COST,
    )(info, same, other, inverses_t)


def whole(array):
    return pl.BlockSpec(array.shape, lambda t, p: (0,) * array.ndim)


def own_body(cols, info, panel, inverses_t, couple_t, keys_t, trailing, out, *pieces):
    part, size, width = panel.shape
    left, right = factor_rows(panel[...].reshape(part * size, width), inverses_t, couple_t[...])
    total = times_key(left, right, keys_t[info[1]]).reshape(part, size, size)
    out[...] = (trailing[...].astype(jnp.float32) - total).astype(BF16)
    for offset in range(2, cols):
        total = times_key(left, right, keys_t[info[1] ^ offset]).reshape(part, size, size)
        pieces[offset - 2][...] = total.astype(BF16)


def own_tiles(info, panel, inverses_t, couple_t, keys_t, trailing, part, cols):
    tiles, size, width = panel.shape
    parts = tiles // part
    block = (part, size, size)
    mine = pl.BlockSpec(block, lambda t, p: (p[1] * parts + t, 0, 0))
    far = pl.BlockSpec(block, lambda t, p: (t, 0, 0))
    piece = jax.ShapeDtypeStruct((tiles, size, size), BF16)
    return pl.pallas_call(
        functools.partial(own_body, cols),
        grid_spec=pltpu.PrefetchScalarGridSpec(
            num_scalar_prefetch=1,
            grid=(parts,),
            in_specs=[
                pl.BlockSpec((part, size, width), lambda t, p: (t, 0, 0)),
                whole(inverses_t),
                whole(couple_t),
                whole(keys_t),
                mine,
            ],
            out_specs=[mine] + [far] * (cols - 2),
        ),
        out_shape=[jax.ShapeDtypeStruct(trailing.shape, BF16)] + [piece] * (cols - 2),
        compiler_params=pltpu.CompilerParams(vmem_limit_bytes=VMEM_LIMIT),
        cost_estimate=SMALL_COST,
    )(info, panel, inverses_t, couple_t, keys_t, trailing)


def near_body(info, held, after, raw, inverses_t, couple_t, keys_t, trailing, out):
    del held, after
    part, size, width = raw.shape
    left, right = factor_rows(raw[...].reshape(part * size, width), inverses_t, couple_t[...])
    total = times_key(left, right, keys_t[info[1]]).reshape(part, size, size)
    out[...] = (trailing[...].astype(jnp.float32) - total).astype(BF16)


def near_tiles(info, held, after, raw, inverses_t, couple_t, keys_t, trailing, part):
    tiles, size, width = raw.shape
    parts = tiles // part
    anywhere = pl.BlockSpec(memory_space=pl.ANY)
    place = pl.BlockSpec((part, size, size), lambda t, p: ((p[1] ^ 1) * parts + t, 0, 0))
    return pl.pallas_call(
        near_body,
        grid_spec=pltpu.PrefetchScalarGridSpec(
            num_scalar_prefetch=1,
            grid=(parts,),
            in_specs=[
                anywhere,
                anywhere,
                pl.BlockSpec((part, size, width), lambda t, p: (t, 0, 0)),
                whole(inverses_t),
                whole(couple_t),
                whole(keys_t),
                place,
            ],
            out_specs=place,
        ),
        out_shape=jax.ShapeDtypeStruct(trailing.shape, BF16),
        input_output_aliases={1: 0},
        compiler_params=pltpu.CompilerParams(vmem_limit_bytes=VMEM_LIMIT),
        cost_estimate=SMALL_COST,
    )(info, held, after, raw, inverses_t, couple_t, keys_t, trailing)


def gate(pieces, waited):
    anywhere = pl.BlockSpec(memory_space=pl.ANY)
    return pl.pallas_call(
        lambda *refs: None,
        in_specs=[anywhere] * (len(pieces) + len(waited)),
        out_specs=[anywhere] * len(pieces),
        out_shape=[jax.ShapeDtypeStruct(piece.shape, piece.dtype) for piece in pieces],
        input_output_aliases={i: i for i in range(len(pieces))},
        cost_estimate=SMALL_COST,
    )(*pieces, *waited)


def crossed_body(cols, info, after, raw, inverses_t, couple_t, keys_t, *pieces):
    del after
    part, size, width = raw.shape
    left, right = factor_rows(raw[...].reshape(part * size, width), inverses_t, couple_t[...])
    col = info[1]
    for k in range(cols // 2):
        target = jnp.clip(jnp.where(col < cols // 2, col - k, col + k), 0, cols - 1)
        total = times_key(left, right, keys_t[target])
        pieces[k][...] = total.reshape(part, size, size).astype(BF16)


def crossed_tiles(info, after, raw, first, count, inverses_t, couple_t, keys_t, part, cols):
    size, width = raw.shape[1:]
    skipped = first // part
    piece = jax.ShapeDtypeStruct((count, size, size), BF16)
    return pl.pallas_call(
        functools.partial(crossed_body, cols),
        grid_spec=pltpu.PrefetchScalarGridSpec(
            num_scalar_prefetch=1,
            grid=(count // part,),
            in_specs=[
                pl.BlockSpec(memory_space=pl.ANY),
                pl.BlockSpec((part, size, width), lambda t, p: (skipped + t, 0, 0)),
                whole(inverses_t),
                whole(couple_t),
                whole(keys_t),
            ],
            out_specs=[pl.BlockSpec((part, size, size), lambda t, p: (t, 0, 0))] * (cols // 2),
        ),
        out_shape=[piece] * (cols // 2),
        compiler_params=pltpu.CompilerParams(vmem_limit_bytes=VMEM_LIMIT),
        cost_estimate=SMALL_COST,
    )(info, after, raw, inverses_t, couple_t, keys_t)


def update_body(use_second, info, held, trailing, first, second, out):
    del held
    flag = use_second(info[1])

    @pl.when(jnp.logical_not(flag))
    def _():
        out[...] = (trailing[...].astype(jnp.float32) - first[...].astype(jnp.float32)).astype(BF16)

    @pl.when(flag)
    def _():
        out[...] = (trailing[...].astype(jnp.float32) - second[...].astype(jnp.float32)).astype(BF16)


def update(info, held, trailing, first, second, part, start, use_second):
    tiles, size, width = first.shape
    block = (part, size, width)
    place = pl.BlockSpec(block, lambda t, p: (start(p[1]) + t, 0, 0))
    return pl.pallas_call(
        functools.partial(update_body, use_second),
        grid_spec=pltpu.PrefetchScalarGridSpec(
            num_scalar_prefetch=1,
            grid=(tiles // part,),
            in_specs=[
                pl.BlockSpec(memory_space=pl.ANY),
                place,
                pl.BlockSpec(block, lambda t, p: (jnp.where(use_second(p[1]), 0, t), 0, 0)),
                pl.BlockSpec(block, lambda t, p: (jnp.where(use_second(p[1]), t, 0), 0, 0)),
            ],
            out_specs=place,
        ),
        out_shape=jax.ShapeDtypeStruct(trailing.shape, trailing.dtype),
        input_output_aliases={1: 0},
        compiler_params=pltpu.CompilerParams(vmem_limit_bytes=VMEM_LIMIT),
        cost_estimate=SMALL_COST,
    )(info, held, trailing, first, second)


def spread_heads(head, rows, cols):
    wanted = sorted({tile % rows for tile in range(1, cols + 2)})
    col_index = lax.axis_index("col")
    span = cols // 2
    while span:
        pairs = [
            (r * cols + c, r * cols + c + span) for r in wanted for c in range(0, cols, 2 * span)
        ]
        arrived = lax.ppermute(head, ("row", "col"), pairs)
        head = jnp.where(col_index % (2 * span) == span, arrived, head)
        span //= 2
    same = [head]
    for offset in range(2, rows, 2):
        same.append(lax.ppermute(head, "row", [(r, r ^ offset) for r in wanted]))
    same = jnp.stack(same)
    return same, lax.ppermute(same, "row", [(r, r ^ 1) for r in range(rows)])


def shards(panel_cols, inverses, trailing):
    tiles = panel_cols.shape[0]
    rows = lax.axis_size("row")
    cols = lax.axis_size("col")
    low, high = cols // 2 - 1, cols // 2
    part = 3 if tiles % 3 == 0 else 1
    halves = 2 if tiles % (2 * part) == 0 else 1
    half = tiles // halves
    info = jnp.stack([lax.axis_index("row"), lax.axis_index("col")]).astype(jnp.int32)
    inverses_t = jnp.swapaxes(inverses, 1, 2)

    crossed = lax.ppermute(panel_cols, "col", [(low, high), (high, low)])
    next_raw = lax.ppermute(panel_cols, "col", [(c, c ^ 1) for c in range(cols)])

    head_tiles = (cols + 1) // rows + 1
    same, other = spread_heads(panel_cols[:head_tiles], rows, cols)
    couple_t, keys_t = make_keys(info, same, other, inverses_t, rows, cols)
    small = (inverses_t, couple_t, keys_t)

    out, *far = own_tiles(info, panel_cols, *small, trailing, part, cols)
    far = gate(far, [crossed, next_raw])
    arrived = {}
    for offset in range(cols - 1, 1, -1):
        pairs = [
            (c, c ^ offset)
            for c in range(cols)
            if not (c == low and c ^ offset > low) and not (c == high and c ^ offset < high)
        ]
        arrived[offset] = lax.ppermute(far[offset - 2], "col", pairs)

    outward = []
    col_index = lax.axis_index("col")
    after = far[-1]
    for i in range(halves):
        mine, *handed = crossed_tiles(info, after, crossed, i * half, half, *small, part, cols)
        after = mine
        got = [
            lax.ppermute(handed[k], "col", [(high, high + k + 1), (low, low - k - 1)])
            for k in range(cols // 2 - 1)
        ]
        chosen = got[0]
        for k in range(1, len(got)):
            here = (col_index == high + k + 1) | (col_index == low - k - 1)
            chosen = jnp.where(here, got[k], chosen)
        outward.append((mine, chosen))

    out = near_tiles(info, out, after, next_raw, *small, trailing, part)

    for offset in range(2, cols - 1):
        def second(col, offset=offset):
            return (col ^ special_source(col, cols)) <= offset

        def source(col, offset=offset, second=second):
            return (col ^ jnp.where(second(col), offset + 1, offset)) * (tiles // part)

        out = update(
            info, out, trailing, arrived[offset], arrived[offset + 1], part, source, second
        )

    def outer(col):
        return (col != low) & (col != high)

    for i, (mine, got) in enumerate(outward):
        out = update(
            info, out, trailing, mine, got, part,
            lambda col, i=i: (special_source(col, cols) * tiles + i * half) // part, outer,
        )
    return out


def solution(mesh):
    in_specs = (P("col", "row", None), P(), P(None, "row", "col"))
    out_specs = P(None, "row", "col")
    return jax.shard_map(shards, mesh=mesh, in_specs=in_specs, out_specs=out_specs, check_vma=False)
```

time: 208 us -> 212 us (1.019); the launches traced: 207 us -> 208 us
  local copies, waits for them, and re-layouts: 10.5 us -> 17.6 us
  starting transfers between devices: 35.4 us -> 29.3 us
  Pallas kernels: 32.5 us -> 27 us
  waiting for transfers between devices: 127 us -> 132 us
    ppermute x6 -> x2, waiting for transfers between devices: 74.6 us -> 0.01 us  [the longest x1 0.01 us: shards(): lax.ppermute(panel_cols, 'col', [(c, c ^ 1) for c in range(cols)])]
    ppermute x2, waiting for transfers between devices: 10.4 us -> 69.4 us  [spread_heads(): arrived = lax.ppermute(head, ('row', 'col'), pairs)]
    ppermute x2, waiting for transfers between devices: 0.01 us -> 45.3 us  [shards(): arrived[offset] = lax.ppermute(far[offset - 2], 'col', pairs)]
    ppermute x3 -> x2, waiting for transfers between devices: 33.6 us -> 8.52 us  [shards(): lax.ppermute(handed[k], 'col', [(high, high + k + 1), (low, low - k - 1)])]
    unnamed x9 -> x25, local copies, waits for them, and re-layouts: 5.76 us -> 16.6 us
    ppermute x6 -> x2, starting transfers between devices: 7.72 us -> 2.43 us  [the longest x1 1.58 us: shards(): lax.ppermute(panel_cols, 'col', [(c, c ^ 1) for c in range(cols)])]
    slice x1 -> x0, local copies, waits for them, and re-layouts: 3.75 us -> none  [shards(): chunks = [panel_cols[i * part:(i + 1) * part] for i in range(parts)]]
    pallas_call x5 -> x3, Pallas kernels: 8.37 us -> 5.55 us  [update(): pl.pallas_call(functools.partial(update_body, use_second), grid_spec=pltp...]
  transfers between devices with their start and end apart: 17 -> 12, of which waited for: 10 -> 8; matrix products, arithmetic and copies ran while one was open for 2% -> 2% of each run, Pallas kernels for 15% -> 12%
where the time goes in v3:
time: 212 us; the launch traced here: 208 us
  waiting for transfers between devices  132 us (62%)
  starting transfers between devices  29.3 us (14%)
  Pallas kernels  27 us (13%)
  local copies, waits for them, and re-layouts  17.6 us (8%)
  other arithmetic  2.19 us (1%)
    ppermute x2, waiting for transfers between devices, spread_heads(): arrived = lax.ppermute(head, ('row', 'col'), pairs)  69.4 us
    ppermute x2, waiting for transfers between devices, shards(): arrived[offset] = lax.ppermute(far[offset - 2], 'col', pairs)  45.3 us
    unnamed x25, local copies, waits for them, and re-layouts  16.6 us
    ppermute x2, starting transfers between devices, shards(): arrived[offset] = lax.ppermute(far[offset - 2], 'col', pairs)  10.1 us
    ppermute x2, waiting for transfers between devices, shards(): lax.ppermute(handed[k], 'col', [(high, high + k + 1), (low, low - k - 1)])  8.52 us
    ppermute x2, starting transfers between devices, spread_heads(): arrived = lax.ppermute(head, ('row', 'col'), pairs)  8.27 us
    ppermute x3, waiting for transfers between devices, spread_heads(): same.append(lax.ppermute(head, 'row', [(r, r ^ offset) for r in wanted]))  7.02 us
    pallas_call x1, Pallas kernels, near_tiles(): pl.pallas_call(near_body, grid_spec=pltpu.PrefetchScalarGridSpec(num_scal...  6.81 us
  transfers between devices with their start and end apart: 12, of which 8 were waited for; matrix products, arithmetic and copies ran while one was open for 2% of the time, Pallas kernels for 12%

profile of v3, /device:TPU:4, one launch (start us, length us, event | category | flops | bytes accessed | tf_op | source)
XLA Modules:
  0.0 208.3 jit_solution(17350957586112373761)
XLA Ops:
  0.0 1.6 collective-permute-start.7
  1.6 0.9 collective-permute-start.6
  2.4 1.0 slice.3
  3.4 6.3 %collective-permute-start = (bf16[1,256,512]{2,1,0:T(8,128)(2,1)S(1)}, bf16[1,256,512]{2,1,0:T(8,128)(2,1)}, u32[]{:S(2)}, u32[]{:S(2)}) collective-permute-start(bf16[1,256,512]{2,1,0:T(8,128)(2,1)S(1)} %slice.3), channel_id=1, source_target_pairs={{4,6},{8,10},{12,14},{16,18},{20,22}} | collective-permute-start | bytes 786440 | tf_op jit(solution)/shard_map/ppermute | solution.py:237
  9.7 65.1 %collective-permute-done = bf16[1,256,512]{2,1,0:T(8,128)(2,1)} collective-permute-done((bf16[1,256,512]{2,1,0:T(8,128)(2,1)S(1)}, bf16[1,256,512]{2,1,0:T(8,128)(2,1)}, u32[]{:S(2)}, u32[]{:S(2)}) %collective-permute-start) | collective-permute-done | bytes 262176 | tf_op jit(solution)/shard_map/ppermute | solution.py:237
  74.8 1.0 broadcast_select_fusion
  75.8 2.0 collective-permute-start.1
  77.8 4.3 %collective-permute-done.1 = bf16[1,256,512]{2,1,0:T(8,128)(2,1)} collective-permute-done((bf16[1,256,512]{2,1,0:T(8,128)(2,1)S(1)}, bf16[1,256,512]{2,1,0:T(8,128)(2,1)}, u32[]{:S(2)}, u32[]{:S(2)}) %collective-permute-start.1) | collective-permute-done | bytes 262176 | tf_op jit(solution)/shard_map/ppermute | solution.py:237
  82.1 3.3 %collective-permute-start.4 = (bf16[1,256,512]{2,1,0:T(8,128)(2,1)S(1)}, bf16[1,256,512]{2,1,0:T(8,128)(2,1)S(1)}, u32[]{:S(2)}, u32[]{:S(2)}) collective-permute-start(bf16[1,256,512]{2,1,0:T(8,128)(2,1)S(1)} %broadcast_select_fusion.1), channel_id=1, source_target_pairs={{4,28},{8,16},{12,20},{16,8},{20,12},{5,29},{9,17},{13,21},{17,9},... | collective-permute-start | bytes 786440 | tf_op jit(solution)/shard_map/ppermute | solution.py:242
  85.4 1.3 collective-permute-start.3
  86.7 1.3 collective-permute-start.2
  88.1 3.8 %collective-permute-done.4 = bf16[1,256,512]{2,1,0:T(8,128)(2,1)S(1)} collective-permute-done((bf16[1,256,512]{2,1,0:T(8,128)(2,1)S(1)}, bf16[1,256,512]{2,1,0:T(8,128)(2,1)S(1)}, u32[]{:S(2)}, u32[]{:S(2)}) %collective-permute-start.4) | collective-permute-done | bytes 262176 | tf_op jit(solution)/shard_map/ppermute | solution.py:242
  91.9 0.0 collective-permute-done.3
  91.9 3.2 %collective-permute-done.2 = bf16[1,256,512]{2,1,0:T(8,128)(2,1)S(1)} collective-permute-done((bf16[1,256,512]{2,1,0:T(8,128)(2,1)S(1)}, bf16[1,256,512]{2,1,0:T(8,128)(2,1)S(1)}, u32[]{:S(2)}, u32[]{:S(2)}) %collective-permute-start.2) | collective-permute-done | bytes 262176 | tf_op jit(solution)/shard_map/ppermute | solution.py:242
  95.1 1.1 pad_maximum_fusion.same
  96.2 0.0 collective-permute-start.5
  96.2 1.1 copy.10
  97.3 0.1 pad_add_fusion.info
  97.4 1.8 collective-permute-done.5.other
  99.2 2.8 %shard_map.37 = (bf16[256,256]{1,0:T(8,128)(2,1)S(1)}, bf16[4,512,256]{2,1,0:T(8,128)(2,1)S(1)}) custom-call(s32[2]{0:T(128)S(1)} %pad_add_fusion.info, bf16[4,1,256,512]{3,2,1,0:T(8,128)(2,1)} %pad_maximum_fusion.same, bf16[4,1,256,512]{3,2,1,0:T(8,128)(2,1)} %collective-permute-done.5.other, bf16[2,256,256]{2,1,0:T(8,128)(2,1)S(1)} %bitcast.9), custom_call_target="tpu_custom_call" | custom-call | flops 1024 | bytes 1024 | tf_op jit(solution)/shard_map/pallas_call | solution.py:55
  102.0 0.0 copy-start.4
  102.0 0.0 copy-start
  102.0 3.2 %copy-done = bf16[48,256,256]{2,1,0:T(8,128)(2,1)S(1)} copy-done((bf16[48,256,256]{2,1,0:T(8,128)(2,1)S(1)}, bf16[48,256,256]{2,1,0:T(8,128)(2,1)}, u32[]{:S(2)}) %copy-start) | copy-done | bytes 6291480
  105.1 0.0 copy-start.8
  105.1 1.9 copy-done.8
  107.0 6.6 %shard_map.38 = (bf16[48,256,256]{2,1,0:T(8,128)(2,1)}, bf16[12,256,256]{2,1,0:T(8,128)(2,1)S(1)}, bf16[12,256,256]{2,1,0:T(8,128)(2,1)S(1)}) custom-call(s32[2]{0:T(128)S(1)} %pad_add_fusion.info, bf16[12,256,512]{2,1,0:T(8,128)(2,1)S(1)} %copy-done.8, bf16[2,256,256]{2,1,0:T(8,128)(2,1)S(1)} %bitcast.10, bf16[256,256]{1,0:T(8,128)(2,1)S(1)} %get-tuple-element.16.couple_t, ...), custom_call_target="tpu_custom_call" | custom-call | flops 1024 | bytes 1024 | tf_op jit(solution)/shard_map/pallas_call | solution.py:89
  113.7 0.0 copy-done.4
  113.7 0.0 copy-start.6
  113.7 1.2 copy-done.6
  114.9 0.0 copy-start.9
  114.9 1.1 copy-done.9
  116.1 0.0 collective-permute-done.7.refs_3_.raw
  116.1 0.0 collective-permute-done.6.refs_2_.raw
  116.1 0.0 copy-start.1
  116.1 1.7 copy-done.1
  117.8 5.5 %collective-permute-start.8 = (bf16[12,256,256]{2,1,0:T(8,128)(2,1)}, bf16[12,256,256]{2,1,0:T(8,128)(2,1)S(1)}, u32[]{:S(2)}, u32[]{:S(2)}) collective-permute-start(bf16[12,256,256]{2,1,0:T(8,128)(2,1)} %get-tuple-element.24), channel_id=1, source_target_pairs={{0,2},{3,1},{4,6},{7,5},{8,10},{11,9},{12,14},{15,13},{16,18},{19,... | collective-permute-start | bytes 4718600 | tf_op jit(solution)/shard_map/ppermute | solution.py:275
  123.3 0.0 slice-start
  123.3 0.0 slice-start.1
  123.3 4.6 %collective-permute-start.9 = (bf16[12,256,256]{2,1,0:T(8,128)(2,1)}, bf16[12,256,256]{2,1,0:T(8,128)(2,1)S(1)}, u32[]{:S(2)}, u32[]{:S(2)}) collective-permute-start(bf16[12,256,256]{2,1,0:T(8,128)(2,1)} %get-tuple-element.21.after), channel_id=1, source_target_pairs={{0,3},{3,0},{4,7},{7,4},{8,11},{11,8},{12,15},{15,12},{16,19},{19,... | collective-permute-start | bytes 4718600 | tf_op jit(solution)/shard_map/ppermute | solution.py:275
  127.9 0.0 copy-start.2
  127.9 1.9 copy-done.2
  129.7 0.0 copy-start.5
  129.7 1.2 copy-done.5
  131.0 0.0 copy-start.7
  131.0 1.4 copy-done.7
  132.4 2.6 %shard_map.40 = (bf16[6,256,256]{2,1,0:T(8,128)(2,1)S(1)}, bf16[6,256,256]{2,1,0:T(8,128)(2,1)S(1)}) custom-call(s32[2]{0:T(128)S(1)} %pad_add_fusion.info, bf16[12,256,256]{2,1,0:T(8,128)(2,1)S(1)} %copy-done.7, bf16[12,256,512]{2,1,0:T(8,128)(2,1)S(1)} %copy-done.2, bf16[2,256,256]{2,1,0:T(8,128)(2,1)S(1)} %bitcast.11, ...), custom_call_target="tpu_custom_call" | custom-call | flops 1024 | bytes 1024 | tf_op jit(solution)/shard_map/pallas_call | solution.py:172
  135.0 1.3 collective-permute-start.10
  136.3 0.0 copy-start.3
  136.3 1.9 copy-done.3
  138.2 2.6 %shard_map.41 = (bf16[6,256,256]{2,1,0:T(8,128)(2,1)S(1)}, bf16[6,256,256]{2,1,0:T(8,128)(2,1)S(1)}) custom-call(s32[2]{0:T(128)S(1)} %pad_add_fusion.info, bf16[6,256,256]{2,1,0:T(8,128)(2,1)S(1)} %get-tuple-element.22.after.first, bf16[12,256,512]{2,1,0:T(8,128)(2,1)S(1)} %copy-done.3, bf16[2,256,256]{2,1,0:T(8,128)(2,1)S(1)} %bitcast.12, ...), custom_call_target="tpu_custom_call" | custom-call | flops 1024 | bytes 1024 | tf_op jit(solution)/shard_map/pallas_call | solution.py:172
  140.8 1.3 collective-permute-start.11
  142.1 0.0 slice-done
  142.1 0.0 slice-done.1
  142.1 6.8 %shard_map.42.held = bf16[48,256,256]{2,1,0:T(8,128)(2,1)} custom-call(s32[2]{0:T(128)S(1)} %pad_add_fusion.info, bf16[48,256,256]{2,1,0:T(8,128)(2,1)} %get-tuple-element.18.held, bf16[6,256,256]{2,1,0:T(8,128)(2,1)S(1)} %get-tuple-element.23.after.first, bf16[12,256,512]{2,1,0:T(8,128)(2,1)} %collective-permute-done.7.refs_3_.raw, ...), custom_call_target="tpu_custom_call", output_to_operand_aliasing={{}: (1, {})} | custom-call | flops 1024 | bytes 1024 | tf_op jit(solution)/shard_map/pallas_call | solution.py:122
  148.9 9.3 %collective-permute-done.8.first = bf16[12,256,256]{2,1,0:T(8,128)(2,1)S(1)} collective-permute-done((bf16[12,256,256]{2,1,0:T(8,128)(2,1)}, bf16[12,256,256]{2,1,0:T(8,128)(2,1)S(1)}, u32[]{:S(2)}, u32[]{:S(2)}) %collective-permute-start.8) | collective-permute-done | bytes 1572896 | tf_op jit(solution)/shard_map/ppermute | solution.py:275
  158.2 36.0 %collective-permute-done.9.second = bf16[12,256,256]{2,1,0:T(8,128)(2,1)S(1)} collective-permute-done((bf16[12,256,256]{2,1,0:T(8,128)(2,1)}, bf16[12,256,256]{2,1,0:T(8,128)(2,1)S(1)}, u32[]{:S(2)}, u32[]{:S(2)}) %collective-permute-start.9) | collective-permute-done | bytes 1572896 | tf_op jit(solution)/shard_map/ppermute | solution.py:275
  194.2 2.4 %shard_map.43.held = bf16[48,256,256]{2,1,0:T(8,128)(2,1)} custom-call(s32[2]{0:T(128)S(1)} %pad_add_fusion.info, bf16[48,256,256]{2,1,0:T(8,128)(2,1)} %shard_map.42.held, bf16[48,256,256]{2,1,0:T(8,128)(2,1)S(1)} %bitcast.8, bf16[12,256,256]{2,1,0:T(8,128)(2,1)S(1)} %collective-permute-done.8.first, ...), custom_call_target="tpu_custom_call", output_to_operand_aliasing={{}: (1, {})} | custom-call | flops 1024 | bytes 1024 | tf_op jit(solution)/shard_map/pallas_call | solution.py:209
  196.6 0.0 collective-permute-done.10.second
  196.6 1.6 shard_map.44.held
  198.2 8.5 %collective-permute-done.11.second = bf16[6,256,256]{2,1,0:T(8,128)(2,1)S(1)} collective-permute-done((bf16[6,256,256]{2,1,0:T(8,128)(2,1)S(1)}, bf16[6,256,256]{2,1,0:T(8,128)(2,1)S(1)}, u32[]{:S(2)}, u32[]{:S(2)}) %collective-permute-start.11) | collective-permute-done | bytes 786464 | tf_op jit(solution)/shard_map/ppermute | solution.py:284
  206.7 1.6 shard_map.45
  (3 shorter events, 0.0 us)
Async XLA Ops:
  0.0 116.1 %collective-permute-start.7 = (bf16[12,256,512]{2,1,0:T(8,128)(2,1)}, bf16[12,256,512]{2,1,0:T(8,128)(2,1)}, u32[]{:S(2)}, u32[]{:S(2)}) collective-permute-start(bf16[12,256,512]{2,1,0:T(8,128)(2,1)} %panel.1), channel_id=1, source_target_pairs={{0,1},{1,0},{2,3},{3,2},{4,5},{5,4},{6,7},{7,6},{8,9},{9,8},{10,11... | collective-permute-start | bytes 9437192 | tf_op jit(solution)/shard_map/ppermute | solution.py:259
  1.6 114.5 %collective-permute-start.6 = (bf16[12,256,512]{2,1,0:T(8,128)(2,1)}, bf16[12,256,512]{2,1,0:T(8,128)(2,1)S(1)}, u32[]{:S(2)}, u32[]{:S(2)}) collective-permute-start(bf16[12,256,512]{2,1,0:T(8,128)(2,1)} %panel.1), channel_id=1, source_target_pairs={{1,2},{2,1},{5,6},{6,5},{9,10},{10,9},{13,14},{14,13},{17,18},{18,... | collective-permute-start | bytes 9437192 | tf_op jit(solution)/shard_map/ppermute | solution.py:258
  3.4 71.4 %collective-permute-start = (bf16[1,256,512]{2,1,0:T(8,128)(2,1)S(1)}, bf16[1,256,512]{2,1,0:T(8,128)(2,1)}, u32[]{:S(2)}, u32[]{:S(2)}) collective-permute-start(bf16[1,256,512]{2,1,0:T(8,128)(2,1)S(1)} %slice.3), channel_id=1, source_target_pairs={{4,6},{8,10},{12,14},{16,18},{20,22}} | collective-permute-start | bytes 786440 | tf_op jit(solution)/shard_map/ppermute | solution.py:237
  75.8 6.3 %collective-permute-start.1 = (bf16[1,256,512]{2,1,0:T(8,128)(2,1)S(1)}, bf16[1,256,512]{2,1,0:T(8,128)(2,1)}, u32[]{:S(2)}, u32[]{:S(2)}) collective-permute-start(bf16[1,256,512]{2,1,0:T(8,128)(2,1)S(1)} %broadcast_select_fusion), channel_id=1, source_target_pairs={{4,5},{6,7},{8,9},{10,11},{12,13},{14,15},{16,17},{18,19},{20,21},... | collective-permute-start | bytes 786440 | tf_op jit(solution)/shard_map/ppermute | solution.py:237
  82.1 9.8 %collective-permute-start.4 = (bf16[1,256,512]{2,1,0:T(8,128)(2,1)S(1)}, bf16[1,256,512]{2,1,0:T(8,128)(2,1)S(1)}, u32[]{:S(2)}, u32[]{:S(2)}) collective-permute-start(bf16[1,256,512]{2,1,0:T(8,128)(2,1)S(1)} %broadcast_select_fusion.1), channel_id=1, source_target_pairs={{4,28},{8,16},{12,20},{16,8},{20,12},{5,29},{9,17},{13,21},{17,9},... | collective-permute-start | bytes 786440 | tf_op jit(solution)/shard_map/ppermute | solution.py:242
  85.4 6.5 %collective-permute-start.3 = (bf16[1,256,512]{2,1,0:T(8,128)(2,1)S(1)}, bf16[1,256,512]{2,1,0:T(8,128)(2,1)S(1)}, u32[]{:S(2)}, u32[]{:S(2)}) collective-permute-start(bf16[1,256,512]{2,1,0:T(8,128)(2,1)S(1)} %broadcast_select_fusion.1), channel_id=1, source_target_pairs={{4,20},{8,24},{12,28},{16,0},{20,4},{5,21},{9,25},{13,29},{17,1},{... | collective-permute-start | bytes 786440 | tf_op jit(solution)/shard_map/ppermute | solution.py:242
  86.7 8.3 %collective-permute-start.2 = (bf16[1,256,512]{2,1,0:T(8,128)(2,1)S(1)}, bf16[1,256,512]{2,1,0:T(8,128)(2,1)S(1)}, u32[]{:S(2)}, u32[]{:S(2)}) collective-permute-start(bf16[1,256,512]{2,1,0:T(8,128)(2,1)S(1)} %broadcast_select_fusion.1), channel_id=1, source_target_pairs={{4,12},{8,0},{12,4},{16,24},{20,28},{5,13},{9,1},{13,5},{17,25},{2... | collective-permute-start | bytes 786440 | tf_op jit(solution)/shard_map/ppermute | solution.py:242
  96.2 3.0 %collective-permute-start.5 = (bf16[4,1,256,512]{3,2,1,0:T(8,128)(2,1)}, bf16[4,1,256,512]{3,2,1,0:T(8,128)(2,1)}, u32[]{:S(2)}, u32[]{:S(2)}) collective-permute-start(bf16[4,1,256,512]{3,2,1,0:T(8,128)(2,1)} %pad_maximum_fusion.same), channel_id=1, source_target_pairs={{0,4},{4,0},{8,12},{12,8},{16,20},{20,16},{24,28},{28,24},{1,5},{5... | collective-permute-start | bytes 3145736 | tf_op jit(solution)/shard_map/ppermute | solution.py:244
  102.0 11.7 %copy-start.4 = (bf16[4,512,256]{2,1,0:T(8,128)(2,1)}, bf16[4,512,256]{2,1,0:T(8,128)(2,1)S(1)}, u32[]{:S(2)}) copy-start(bf16[4,512,256]{2,1,0:T(8,128)(2,1)S(1)} %get-tuple-element.17.keys_t) | copy-start | bytes 3145732
  102.0 3.2 %copy-start = (bf16[48,256,256]{2,1,0:T(8,128)(2,1)S(1)}, bf16[48,256,256]{2,1,0:T(8,128)(2,1)}, u32[]{:S(2)}) copy-start(bf16[48,256,256]{2,1,0:T(8,128)(2,1)} %trailing.9) | copy-start | bytes 18874372
  105.1 1.9 copy-start.8
  113.7 1.2 copy-start.6
  114.9 1.1 copy-start.9
  116.1 1.7 copy-start.1
  117.8 40.5 %collective-permute-start.8 = (bf16[12,256,256]{2,1,0:T(8,128)(2,1)}, bf16[12,256,256]{2,1,0:T(8,128)(2,1)S(1)}, u32[]{:S(2)}, u32[]{:S(2)}) collective-permute-start(bf16[12,256,256]{2,1,0:T(8,128)(2,1)} %get-tuple-element.24), channel_id=1, source_target_pairs={{0,2},{3,1},{4,6},{7,5},{8,10},{11,9},{12,14},{15,13},{16,18},{19,... | collective-permute-start | bytes 4718600 | tf_op jit(solution)/shard_map/ppermute | solution.py:275
  123.3 18.8 %slice-start = ((s8[6291456]{0:T(1024)(128)(4,1)}), s8[4194304]{0:T(1024)(128)(4,1)S(1)}, s32[]{:S(2)}) async-start(s8[6291456]{0:T(1024)(128)(4,1)} %bitcast.7), calls=%async_computation | async-start | bytes 8388608
  123.3 18.8 %slice-start.1 = ((s8[6291456]{0:T(1024)(128)(4,1)}), s8[2097152]{0:T(1024)(128)(4,1)S(1)}, s32[]{:S(2)}) async-start(s8[6291456]{0:T(1024)(128)(4,1)} %bitcast.7), calls=%async_computation.1 | async-start | bytes 4194304
  123.3 70.9 %collective-permute-start.9 = (bf16[12,256,256]{2,1,0:T(8,128)(2,1)}, bf16[12,256,256]{2,1,0:T(8,128)(2,1)S(1)}, u32[]{:S(2)}, u32[]{:S(2)}) collective-permute-start(bf16[12,256,256]{2,1,0:T(8,128)(2,1)} %get-tuple-element.21.after), channel_id=1, source_target_pairs={{0,3},{3,0},{4,7},{7,4},{8,11},{11,8},{12,15},{15,12},{16,19},{19,... | collective-permute-start | bytes 4718600 | tf_op jit(solution)/shard_map/ppermute | solution.py:275
  127.9 1.9 copy-start.2
  129.7 1.2 copy-start.5
  131.0 1.4 copy-start.7
  135.0 61.6 %collective-permute-start.10 = (bf16[6,256,256]{2,1,0:T(8,128)(2,1)S(1)}, bf16[6,256,256]{2,1,0:T(8,128)(2,1)S(1)}, u32[]{:S(2)}, u32[]{:S(2)}) collective-permute-start(bf16[6,256,256]{2,1,0:T(8,128)(2,1)S(1)} %get-tuple-element.25), channel_id=1, source_target_pairs={{2,3},{1,0},{6,7},{5,4},{10,11},{9,8},{14,15},{13,12},{18,19},{17,... | collective-permute-start | bytes 2359304 | tf_op jit(solution)/shard_map/ppermute | solution.py:284
  136.3 1.9 copy-start.3
  140.8 65.9 %collective-permute-start.11 = (bf16[6,256,256]{2,1,0:T(8,128)(2,1)S(1)}, bf16[6,256,256]{2,1,0:T(8,128)(2,1)S(1)}, u32[]{:S(2)}, u32[]{:S(2)}) collective-permute-start(bf16[6,256,256]{2,1,0:T(8,128)(2,1)S(1)} %get-tuple-element.26), channel_id=1, source_target_pairs={{2,3},{1,0},{6,7},{5,4},{10,11},{9,8},{14,15},{13,12},{18,19},{17,... | collective-permute-start | bytes 2359304 | tf_op jit(solution)/shard_map/ppermute | solution.py:284

commit v4 on v3

v4 whole, which is shorter than its diff:
```python
import functools

import jax
import jax.numpy as jnp
from jax import lax
from jax.experimental import pallas as pl
from jax.experimental.pallas import tpu as pltpu
from jax.sharding import PartitionSpec as P

BF16 = jnp.bfloat16
SMALL_COST = pl.CostEstimate(flops=1024, bytes_accessed=1024, transcendentals=0)


def vmem_limit():
    return (8 + 3 * lax.axis_size("col")) * 1024 * 1024


def dot(left, right):
    return jnp.dot(left, right, preferred_element_type=jnp.float32)


def factor_rows(rows, inverses_t, couple_t):
    size = couple_t.shape[0]
    left = dot(rows[:, :size], inverses_t[0]).astype(BF16)
    reduced = (rows[:, size:].astype(jnp.float32) - dot(left, couple_t)).astype(BF16)
    right = dot(reduced, inverses_t[1]).astype(BF16)
    return left, right


def times_key(left, right, key_t):
    size = left.shape[1]
    return dot(left, key_t[:size]) + dot(right, key_t[size:])


def special_source(col, cols):
    return cols // 2 - (col >= cols // 2)


def keys_body(rows, info, same, other, inverses_t, couple_t, keys_t):
    size = couple_t.shape[0]

    def raw(tile):
        offset = info[0] ^ (tile % rows)
        index, place = offset // 2, tile // rows
        return jnp.where(offset % 2 == 0, same[index, place], other[index, place])

    couple = dot(raw(1)[:, :size], inverses_t[0]).astype(BF16)
    couple_t[...] = couple.astype(jnp.float32).T.astype(BF16)
    for j in range(keys_t.shape[0]):
        left, right = factor_rows(raw(j + 2), inverses_t, couple_t[...])
        keys_t[j, :size] = left.astype(jnp.float32).T.astype(BF16)
        keys_t[j, size:] = right.astype(jnp.float32).T.astype(BF16)


def make_keys(info, same, other, inverses_t, rows, cols):
    size, width = same.shape[2:]
    vmem = pl.BlockSpec(memory_space=pltpu.VMEM)
    return pl.pallas_call(
        functools.partial(keys_body, rows),
        in_specs=[pl.BlockSpec(memory_space=pltpu.SMEM), vmem, vmem, vmem],
        out_specs=[vmem, vmem],
        out_shape=[
            jax.ShapeDtypeStruct((size, size), BF16),
            jax.ShapeDtypeStruct((cols, width, size), BF16),
        ],
        compiler_params=pltpu.CompilerParams(vmem_limit_bytes=vmem_limit()),
        cost_estimate=SMALL_COST,
    )(info, same, other, inverses_t)


def whole(array):
    return pl.BlockSpec(array.shape, lambda t, p: (0,) * array.ndim)


def own_body(info, panel, inverses_t, couple_t, keys_t, trailing, out, factored):
    part, size, width = panel.shape
    left, right = factor_rows(panel[...].reshape(part * size, width), inverses_t, couple_t[...])
    total = times_key(left, right, keys_t[info[1]]).reshape(part, size, size)
    out[...] = (trailing[...].astype(jnp.float32) - total).astype(BF16)
    factored[:, :, :size] = left.reshape(part, size, size)
    factored[:, :, size:] = right.reshape(part, size, size)


def own_tiles(info, panel, inverses_t, couple_t, keys_t, trailing, part):
    tiles, size, width = panel.shape
    parts = tiles // part
    rows = pl.BlockSpec((part, size, width), lambda t, p: (t, 0, 0))
    mine = pl.BlockSpec((part, size, size), lambda t, p: (p[1] * parts + t, 0, 0))
    return pl.pallas_call(
        own_body,
        grid_spec=pltpu.PrefetchScalarGridSpec(
            num_scalar_prefetch=1,
            grid=(parts,),
            in_specs=[rows, whole(inverses_t), whole(couple_t), whole(keys_t), mine],
            out_specs=[mine, rows],
        ),
        out_shape=[
            jax.ShapeDtypeStruct(trailing.shape, BF16),
            jax.ShapeDtypeStruct(panel.shape, BF16),
        ],
        compiler_params=pltpu.CompilerParams(vmem_limit_bytes=vmem_limit()),
        cost_estimate=SMALL_COST,
    )(info, panel, inverses_t, couple_t, keys_t, trailing)


def far_body(offset, info, after, factored, keys_t, piece):
    del after
    part, size, width = factored.shape
    rows = factored[...].reshape(part * size, width)
    total = dot(rows, keys_t[info[1] ^ offset])
    piece[...] = total.reshape(part, size, size).astype(BF16)


def far_product(info, after, factored, keys_t, offset, part):
    tiles, size, width = factored.shape
    return pl.pallas_call(
        functools.partial(far_body, offset),
        grid_spec=pltpu.PrefetchScalarGridSpec(
            num_scalar_prefetch=1,
            grid=(tiles // part,),
            in_specs=[
                pl.BlockSpec(memory_space=pl.ANY),
                pl.BlockSpec((part, size, width), lambda t, p: (t, 0, 0)),
                whole(keys_t),
            ],
            out_specs=pl.BlockSpec((part, size, size), lambda t, p: (t, 0, 0)),
        ),
        out_shape=jax.ShapeDtypeStruct((tiles, size, size), BF16),
        compiler_params=pltpu.CompilerParams(vmem_limit_bytes=vmem_limit()),
        cost_estimate=SMALL_COST,
    )(info, after, factored, keys_t)


def near_body(info, held, after, raw, inverses_t, couple_t, keys_t, trailing, out):
    del held, after
    part, size, width = raw.shape
    left, right = factor_rows(raw[...].reshape(part * size, width), inverses_t, couple_t[...])
    total = times_key(left, right, keys_t[info[1]]).reshape(part, size, size)
    out[...] = (trailing[...].astype(jnp.float32) - total).astype(BF16)


def near_tiles(info, held, after, raw, inverses_t, couple_t, keys_t, trailing, part):
    count, size, width = raw.shape
    parts = trailing.shape[0] // part // lax.axis_size("col")
    place = pl.BlockSpec((part, size, size), lambda t, p: ((p[1] ^ 1) * parts + t, 0, 0))
    return pl.pallas_call(
        near_body,
        grid_spec=pltpu.PrefetchScalarGridSpec(
            num_scalar_prefetch=1,
            grid=(count // part,),
            in_specs=[
                pl.BlockSpec(memory_space=pl.ANY),
                pl.BlockSpec(memory_space=pl.ANY),
                pl.BlockSpec((part, size, width), lambda t, p: (t, 0, 0)),
                whole(inverses_t),
                whole(couple_t),
                whole(keys_t),
                place,
            ],
            out_specs=place,
        ),
        out_shape=jax.ShapeDtypeStruct(trailing.shape, BF16),
        input_output_aliases={1: 0},
        compiler_params=pltpu.CompilerParams(vmem_limit_bytes=vmem_limit()),
        cost_estimate=SMALL_COST,
    )(info, held, after, raw, inverses_t, couple_t, keys_t, trailing)


def copy_after(panel, part, after):
    def body(after, tiles, out):
        del after
        out[...] = tiles[...]

    block = pl.BlockSpec((part,) + panel.shape[1:], lambda t: (t, 0, 0))
    return pl.pallas_call(
        body,
        grid=(panel.shape[0] // part,),
        in_specs=[pl.BlockSpec(memory_space=pl.ANY), block],
        out_specs=block,
        out_shape=jax.ShapeDtypeStruct(panel.shape, panel.dtype),
        compiler_params=pltpu.CompilerParams(vmem_limit_bytes=vmem_limit()),
        cost_estimate=SMALL_COST,
    )(after, panel)


def crossed_body(cols, info, after, raw, inverses_t, couple_t, keys_t, *pieces):
    del after
    part, size, width = raw.shape
    left, right = factor_rows(raw[...].reshape(part * size, width), inverses_t, couple_t[...])
    col = info[1]
    for k in range(cols // 2):
        target = jnp.clip(jnp.where(col < cols // 2, col - k, col + k), 0, cols - 1)
        total = times_key(left, right, keys_t[target])
        pieces[k][...] = total.reshape(part, size, size).astype(BF16)


def crossed_tiles(info, after, raw, first, count, inverses_t, couple_t, keys_t, part, cols):
    size, width = raw.shape[1:]
    skipped = first // part
    piece = jax.ShapeDtypeStruct((count, size, size), BF16)
    return pl.pallas_call(
        functools.partial(crossed_body, cols),
        grid_spec=pltpu.PrefetchScalarGridSpec(
            num_scalar_prefetch=1,
            grid=(count // part,),
            in_specs=[
                pl.BlockSpec(memory_space=pl.ANY),
                pl.BlockSpec((part, size, width), lambda t, p: (skipped + t, 0, 0)),
                whole(inverses_t),
                whole(couple_t),
                whole(keys_t),
            ],
            out_specs=[pl.BlockSpec((part, size, size), lambda t, p: (t, 0, 0))] * (cols // 2),
        ),
        out_shape=[piece] * (cols // 2),
        compiler_params=pltpu.CompilerParams(vmem_limit_bytes=vmem_limit()),
        cost_estimate=SMALL_COST,
    )(info, after, raw, inverses_t, couple_t, keys_t)


def update_body(which, info, held, trailing, *refs):
    del held
    *pieces, out = refs
    for i, piece in enumerate(pieces):
        @pl.when(which(info[1]) == i)
        def _(piece=piece):
            total = trailing[...].astype(jnp.float32) - piece[...].astype(jnp.float32)
            out[...] = total.astype(BF16)


def update(info, held, trailing, pieces, count, part, start, which):
    block = (part,) + trailing.shape[1:]
    place = pl.BlockSpec(block, lambda t, p: (start(p[1]) + t, 0, 0))

    def chosen(i, first):
        skipped = first // part
        return pl.BlockSpec(
            block, lambda t, p: (skipped + jnp.where(which(p[1]) == i, t, 0), 0, 0)
        )

    return pl.pallas_call(
        functools.partial(update_body, which),
        grid_spec=pltpu.PrefetchScalarGridSpec(
            num_scalar_prefetch=1,
            grid=(count // part,),
            in_specs=[pl.BlockSpec(memory_space=pl.ANY), place]
            + [chosen(i, first) for i, (_, first) in enumerate(pieces)],
            out_specs=place,
        ),
        out_shape=jax.ShapeDtypeStruct(trailing.shape, trailing.dtype),
        input_output_aliases={1: 0},
        compiler_params=pltpu.CompilerParams(vmem_limit_bytes=vmem_limit()),
        cost_estimate=SMALL_COST,
    )(info, held, trailing, *[array for array, _ in pieces])


def spread_down(head, wanted, cols):
    steps = []
    col_index = lax.axis_index("col")
    span = cols // 2
    while span:
        pairs = [
            (r * cols + c, r * cols + c + span) for r in wanted for c in range(0, cols, 2 * span)
        ]
        arrived = lax.ppermute(head, ("row", "col"), pairs)
        head = jnp.where(col_index % (2 * span) == span, arrived, head)
        steps.append(head)
        span //= 2
    return head, steps[0]


def spread_across(head, wanted, rows):
    same = [head]
    for offset in range(2, rows, 2):
        same.append(lax.ppermute(head, "row", [(r, r ^ offset) for r in wanted]))
    same = jnp.stack(same)
    return same, lax.ppermute(same, "row", [(r, r ^ 1) for r in range(rows)])


def shards(panel_cols, inverses, trailing):
    tiles = panel_cols.shape[0]
    rows = lax.axis_size("row")
    cols = lax.axis_size("col")
    low, high = cols // 2 - 1, cols // 2
    part = 3 if tiles % 3 == 0 else 1
    parts = tiles // part
    halves = 2 if parts % 2 == 0 else 1
    half = tiles // halves
    info = jnp.stack([lax.axis_index("row"), lax.axis_index("col")]).astype(jnp.int32)
    inverses_t = jnp.swapaxes(inverses, 1, 2)

    crossed = lax.ppermute(panel_cols, "col", [(low, high), (high, low)])

    wanted = sorted({tile % rows for tile in range(1, cols + 2)})
    head, first_step = spread_down(panel_cols[:(cols + 1) // rows + 1], wanted, cols)
    beside = [(c, c ^ 1) for c in range(cols)]
    next_raw = lax.ppermute(copy_after(panel_cols, part, first_step), "col", beside)
    same, other = spread_across(head, wanted, rows)
    couple_t, keys_t = make_keys(info, same, other, inverses_t, rows, cols)
    small = (inverses_t, couple_t, keys_t)

    out, factored = own_tiles(info, panel_cols, *small, trailing, part)
    arrived = {}
    after = out
    for offset in range(cols - 1, 1, -1):
        pairs = [
            (c, c ^ offset)
            for c in range(cols)
            if not (c == low and c ^ offset > low) and not (c == high and c ^ offset < high)
        ]
        after = far_product(info, after, factored, keys_t, offset, part)
        arrived[offset] = lax.ppermute(after, "col", pairs)

    outward = []
    col_index = lax.axis_index("col")
    for i in range(halves):
        mine, *handed = crossed_tiles(info, after, crossed, i * half, half, *small, part, cols)
        after = mine
        got = [
            lax.ppermute(handed[k], "col", [(high, high + k + 1), (low, low - k - 1)])
            for k in range(cols // 2 - 1)
        ]
        chosen = got[0]
        for k in range(1, len(got)):
            here = (col_index == high + k + 1) | (col_index == low - k - 1)
            chosen = jnp.where(here, got[k], chosen)
        outward.append((mine, chosen))

    out = near_tiles(info, out, after, next_raw, *small, trailing, part)

    def far_offset(col, slot):
        return slot + ((col ^ special_source(col, cols)) <= slot)

    def inner(col):
        return (col == low) | (col == high)

    for slot in range(3, cols - 1):
        out = update(
            info, out, trailing, [(arrived[slot], 0), (arrived[slot + 1], 0)], tiles, part,
            lambda col, slot=slot: (col ^ far_offset(col, slot)) * parts,
            lambda col, slot=slot: far_offset(col, slot) - slot,
        )

    outer_far = sorted({far_offset(c, 2) for c in range(cols) if not inner(c)})

    def far_place(col):
        return (col ^ far_offset(col, 2)) * parts

    for i, (mine, _) in enumerate(outward):
        out = update(
            info, out, trailing,
            [(mine, 0)] + [(arrived[offset], i * half) for offset in outer_far], half, part,
            lambda col, i=i: i * half // part
            + jnp.where(inner(col), special_source(col, cols) * parts, far_place(col)),
            lambda col: jnp.where(inner(col), 0, far_offset(col, 2) - outer_far[0] + 1),
        )
    for i, (_, got) in enumerate(outward):
        out = update(
            info, out, trailing, [(got, 0), (arrived[2], i * half)], half, part,
            lambda col, i=i: i * half // part
            + jnp.where(inner(col), far_place(col), special_source(col, cols) * parts),
            lambda col: jnp.where(inner(col), 1, 0),
        )
    return out


def solution(mesh):
    in_specs = (P("col", "row", None), P(), P(None, "row", "col"))
    out_specs = P(None, "row", "col")
    return jax.shard_map(shards, mesh=mesh, in_specs=in_specs, out_specs=out_specs, check_vma=False)
```

time: 212 us -> 160 us (0.75)
  the two profiles are of different devices: /device:TPU:4 before, /device:TPU:10 now
where the time goes in v4:
time: 160 us
  waiting for transfers between devices  88.4 us (55%)
  Pallas kernels  35.1 us (22%)
  starting transfers between devices  23.3 us (15%)
  local copies, waits for them, and re-layouts  9.52 us (6%)
  other arithmetic  3.16 us (2%)
    ppermute x2, waiting for transfers between devices, shards(): arrived[offset] = lax.ppermute(after, 'col', pairs)  57.9 us
    ppermute x1, waiting for transfers between devices, shards(): crossed = lax.ppermute(panel_cols, 'col', [(low, high), (high, low)])  20.5 us
    unnamed x13, local copies, waits for them, and re-layouts  8.55 us
    pallas_call x2, Pallas kernels, crossed_tiles(): pl.pallas_call(functools.partial(crossed_body, cols), grid_spec=pltpu.Pre...  7.5 us
    ppermute x3, waiting for transfers between devices, spread_across(): same.append(lax.ppermute(head, 'row', [(r, r ^ offset) for r in wanted]))  6.86 us
    pallas_call x1, Pallas kernels, near_tiles(): pl.pallas_call(near_body, grid_spec=pltpu.PrefetchScalarGridSpec(num_scal...  6.83 us
    ppermute x1, starting transfers between devices, shards(): lax.ppermute(copy_after(panel_cols, part, first_step), 'col', beside)  6.38 us
    pallas_call x4, Pallas kernels, update(): pl.pallas_call(functools.partial(update_body, which), grid_spec=pltpu.Pre...  6.36 us
  transfers between devices with their start and end apart: 12, of which 6 were waited for; matrix products, arithmetic and copies ran while one was open for 3% of the time, Pallas kernels for 21%

profile of v4, /device:TPU:10, one launch (start us, length us, event | category | flops | bytes accessed | tf_op | source)
XLA Modules:
  0.0 159.7 jit_solution(6831675003298508458)
XLA Ops:
  0.0 1.0 slice.3
  1.0 0.7 collective-permute-start
  1.7 4.1 %collective-permute-start.6 = (bf16[12,256,512]{2,1,0:T(8,128)(2,1)}, bf16[12,256,512]{2,1,0:T(8,128)(2,1)}, u32[]{:S(2)}, u32[]{:S(2)}) collective-permute-start(bf16[12,256,512]{2,1,0:T(8,128)(2,1)} %tiles.1), channel_id=1, source_target_pairs={{1,2},{2,1},{5,6},{6,5},{9,10},{10,9},{13,14},{14,13},{17,18},{18,... | collective-permute-start | bytes 9437192 | tf_op jit(solution)/shard_map/ppermute | solution.py:292
  5.8 0.0 collective-permute-done
  5.8 1.0 broadcast_select_fusion.after
  6.8 1.3 collective-permute-start.1
  8.1 0.0 copy-start.2
  8.1 1.9 %copy-done.2 = bf16[12,256,512]{2,1,0:T(8,128)(2,1)S(1)} copy-done((bf16[12,256,512]{2,1,0:T(8,128)(2,1)S(1)}, bf16[12,256,512]{2,1,0:T(8,128)(2,1)}, u32[]{:S(2)}) %copy-start.2) | copy-done | bytes 3145752
  10.0 2.2 %shard_map.43 = bf16[12,256,512]{2,1,0:T(8,128)(2,1)} custom-call(bf16[1,256,512]{2,1,0:T(8,128)(2,1)S(1)} %broadcast_select_fusion.after, bf16[12,256,512]{2,1,0:T(8,128)(2,1)S(1)} %copy-done.2), custom_call_target="tpu_custom_call" | custom-call | flops 1024 | bytes 1024 | tf_op jit(solution)/shard_map/pallas_call | solution.py:175
  12.2 0.0 copy-start.3
  12.2 6.4 %collective-permute-start.7 = (bf16[12,256,512]{2,1,0:T(8,128)(2,1)}, bf16[12,256,512]{2,1,0:T(8,128)(2,1)}, u32[]{:S(2)}, u32[]{:S(2)}) collective-permute-start(bf16[12,256,512]{2,1,0:T(8,128)(2,1)} %shard_map.43), channel_id=1, source_target_pairs={{0,1},{1,0},{2,3},{3,2},{4,5},{5,4},{6,7},{7,6},{8,9},{9,8},{10,11... | collective-permute-start | bytes 9437192 | tf_op jit(solution)/shard_map/ppermute | solution.py:297
  18.6 1.3 collective-permute-done.1
  19.9 1.0 broadcast_select_fusion.1
  20.8 3.4 %collective-permute-start.4 = (bf16[1,256,512]{2,1,0:T(8,128)(2,1)S(1)}, bf16[1,256,512]{2,1,0:T(8,128)(2,1)S(1)}, u32[]{:S(2)}, u32[]{:S(2)}) collective-permute-start(bf16[1,256,512]{2,1,0:T(8,128)(2,1)S(1)} %broadcast_select_fusion.1), channel_id=1, source_target_pairs={{4,28},{8,16},{12,20},{16,8},{20,12},{5,29},{9,17},{13,21},{17,9},... | collective-permute-start | bytes 786440 | tf_op jit(solution)/shard_map/ppermute | solution.py:275
  24.3 1.3 collective-permute-start.3
  25.6 1.3 collective-permute-start.2
  26.9 5.9 %collective-permute-done.4 = bf16[1,256,512]{2,1,0:T(8,128)(2,1)S(1)} collective-permute-done((bf16[1,256,512]{2,1,0:T(8,128)(2,1)S(1)}, bf16[1,256,512]{2,1,0:T(8,128)(2,1)S(1)}, u32[]{:S(2)}, u32[]{:S(2)}) %collective-permute-start.4) | collective-permute-done | bytes 262176 | tf_op jit(solution)/shard_map/ppermute | solution.py:275
  32.8 0.0 collective-permute-done.3
  32.8 0.9 collective-permute-done.2
  33.7 1.1 pad_maximum_fusion.same
  34.8 0.0 collective-permute-start.5
  34.8 1.1 copy.9
  35.9 0.1 pad_add_fusion.info
  36.0 1.8 %collective-permute-done.5.other = bf16[4,1,256,512]{3,2,1,0:T(8,128)(2,1)} collective-permute-done((bf16[4,1,256,512]{3,2,1,0:T(8,128)(2,1)}, bf16[4,1,256,512]{3,2,1,0:T(8,128)(2,1)}, u32[]{:S(2)}, u32[]{:S(2)}) %collective-permute-start.5) | collective-permute-done | bytes 1048608 | tf_op jit(solution)/shard_map/ppermute | solution.py:277
  37.8 2.8 %shard_map.37 = (bf16[256,256]{1,0:T(8,128)(2,1)S(1)}, bf16[4,512,256]{2,1,0:T(8,128)(2,1)S(1)}) custom-call(s32[2]{0:T(128)S(1)} %pad_add_fusion.info, bf16[4,1,256,512]{3,2,1,0:T(8,128)(2,1)} %pad_maximum_fusion.same, bf16[4,1,256,512]{3,2,1,0:T(8,128)(2,1)} %collective-permute-done.5.other, bf16[2,256,256]{2,1,0:T(8,128)(2,1)S(1)} %bitcast.9), custom_call_target="tpu_custom_call" | custom-call | flops 1024 | bytes 1024 | tf_op jit(solution)/shard_map/pallas_call | solution.py:58
  40.6 0.0 copy-done.3
  40.6 0.0 copy-start
  40.6 2.8 %copy-done = bf16[48,256,256]{2,1,0:T(8,128)(2,1)S(1)} copy-done((bf16[48,256,256]{2,1,0:T(8,128)(2,1)S(1)}, bf16[48,256,256]{2,1,0:T(8,128)(2,1)}, u32[]{:S(2)}) %copy-start) | copy-done | bytes 6291480
  43.4 5.4 %shard_map.38 = (bf16[48,256,256]{2,1,0:T(8,128)(2,1)}, bf16[12,256,512]{2,1,0:T(8,128)(2,1)S(1)}) custom-call(s32[2]{0:T(128)S(1)} %pad_add_fusion.info, bf16[12,256,512]{2,1,0:T(8,128)(2,1)S(1)} %copy-done.3, bf16[2,256,256]{2,1,0:T(8,128)(2,1)S(1)} %bitcast.10, bf16[256,256]{1,0:T(8,128)(2,1)S(1)} %get-tuple-element.13.couple_t, ...), custom_call_target="tpu_custom_call" | custom-call | flops 1024 | bytes 1024 | tf_op jit(solution)/shard_map/pallas_call | solution.py:89
  48.8 0.0 copy-start.1
  48.8 2.8 %copy-done.1 = bf16[48,256,256]{2,1,0:T(8,128)(2,1)S(1)} copy-done((bf16[48,256,256]{2,1,0:T(8,128)(2,1)S(1)}, bf16[48,256,256]{2,1,0:T(8,128)(2,1)}, u32[]{:S(2)}) %copy-start.1) | copy-done | bytes 6291480
  51.6 2.0 %shard_map.39.after = bf16[12,256,256]{2,1,0:T(8,128)(2,1)S(1)} custom-call(s32[2]{0:T(128)S(1)} %pad_add_fusion.info, bf16[48,256,256]{2,1,0:T(8,128)(2,1)S(1)} %copy-done.1, bf16[12,256,512]{2,1,0:T(8,128)(2,1)S(1)} %get-tuple-element.16.factored, bf16[4,512,256]{2,1,0:T(8,128)(2,1)S(1)} %get-tuple-element.14.keys_t), custom_call_target="tpu_custom_call" | custom-call | flops 1024 | bytes 1024 | tf_op jit(solution)/shard_map/pallas_call | solution.py:116
  53.6 0.8 collective-permute-start.8
  54.4 0.0 slice-start
  54.4 2.0 %shard_map.40.after = bf16[12,256,256]{2,1,0:T(8,128)(2,1)S(1)} custom-call(s32[2]{0:T(128)S(1)} %pad_add_fusion.info, bf16[12,256,256]{2,1,0:T(8,128)(2,1)S(1)} %shard_map.39.after, bf16[12,256,512]{2,1,0:T(8,128)(2,1)S(1)} %get-tuple-element.16.factored, bf16[4,512,256]{2,1,0:T(8,128)(2,1)S(1)} %get-tuple-element.14.keys_t), custom_call_target="tpu_custom_call" | custom-call | flops 1024 | bytes 1024 | tf_op jit(solution)/shard_map/pallas_call | solution.py:116
  56.4 0.0 slice-start.1
  56.5 1.4 collective-permute-start.10
  57.9 20.5 %collective-permute-done.6.raw = bf16[12,256,512]{2,1,0:T(8,128)(2,1)} collective-permute-done((bf16[12,256,512]{2,1,0:T(8,128)(2,1)}, bf16[12,256,512]{2,1,0:T(8,128)(2,1)}, u32[]{:S(2)}, u32[]{:S(2)}) %collective-permute-start.6) | collective-permute-done | bytes 3145760 | tf_op jit(solution)/shard_map/ppermute | solution.py:292
  78.4 3.7 %shard_map.41 = (bf16[6,256,256]{2,1,0:T(8,128)(2,1)S(1)}, bf16[6,256,256]{2,1,0:T(8,128)(2,1)S(1)}) custom-call(s32[2]{0:T(128)S(1)} %pad_add_fusion.info, bf16[12,256,256]{2,1,0:T(8,128)(2,1)S(1)} %shard_map.40.after, bf16[12,256,512]{2,1,0:T(8,128)(2,1)} %collective-permute-done.6.raw, bf16[2,256,256]{2,1,0:T(8,128)(2,1)S(1)} %bitcast.11, ...), custom_call_target="tpu_custom_call" | custom-call | flops 1024 | bytes 1024 | tf_op jit(solution)/shard_map/pallas_call | solution.py:201
  82.2 1.3 collective-permute-start.9
  83.5 3.8 %shard_map.42 = (bf16[6,256,256]{2,1,0:T(8,128)(2,1)S(1)}, bf16[6,256,256]{2,1,0:T(8,128)(2,1)S(1)}) custom-call(s32[2]{0:T(128)S(1)} %pad_add_fusion.info, bf16[6,256,256]{2,1,0:T(8,128)(2,1)S(1)} %get-tuple-element.17.after.refs_0_, bf16[12,256,512]{2,1,0:T(8,128)(2,1)} %collective-permute-done.6.raw, bf16[2,256,256]{2,1,0:T(8,128)(2,1)S(1)} %bitcast.12, ...), custom_call_target="tpu_custom_call" | custom-call | flops 1024 | bytes 1024 | tf_op jit(solution)/shard_map/pallas_call | solution.py:201
  87.3 1.3 collective-permute-start.11
  88.6 0.0 collective-permute-done.7.raw
  88.6 0.0 slice-done
  88.7 0.0 slice-done.1
  88.7 6.8 %shard_map.44.held = bf16[48,256,256]{2,1,0:T(8,128)(2,1)} custom-call(s32[2]{0:T(128)S(1)} %pad_add_fusion.info, bf16[48,256,256]{2,1,0:T(8,128)(2,1)} %get-tuple-element.15.after.held, bf16[6,256,256]{2,1,0:T(8,128)(2,1)S(1)} %get-tuple-element.18.after.refs_0_, bf16[12,256,512]{2,1,0:T(8,128)(2,1)} %collective-permute-done.7.raw, ...), custom_call_target="tpu_custom_call", output_to_operand_aliasing={{}: (1, {})} | custom-call | flops 1024 | bytes 1024 | tf_op jit(solution)/shard_map/pallas_call | solution.py:146
  95.5 0.0 collective-permute-done.8.refs_1_
  95.5 1.6 shard_map.45.held
  97.1 1.6 shard_map.46.held
  98.7 57.9 %collective-permute-done.10.refs_1_ = bf16[12,256,256]{2,1,0:T(8,128)(2,1)S(1)} collective-permute-done((bf16[12,256,256]{2,1,0:T(8,128)(2,1)S(1)}, bf16[12,256,256]{2,1,0:T(8,128)(2,1)S(1)}, u32[]{:S(2)}, u32[]{:S(2)}) %collective-permute-start.10) | collective-permute-done | bytes 1572896 | tf_op jit(solution)/shard_map/ppermute | solution.py:312
  156.5 0.0 collective-permute-done.9.refs_0_
  156.6 1.6 shard_map.47.held
  158.1 0.0 collective-permute-done.11.refs_0_
  158.1 1.6 shard_map.48
  (1 shorter events, 0.0 us)
Async XLA Ops:
  1.0 4.8 %collective-permute-start = (bf16[1,256,512]{2,1,0:T(8,128)(2,1)S(1)}, bf16[1,256,512]{2,1,0:T(8,128)(2,1)S(1)}, u32[]{:S(2)}, u32[]{:S(2)}) collective-permute-start(bf16[1,256,512]{2,1,0:T(8,128)(2,1)S(1)} %slice.3), channel_id=1, source_target_pairs={{4,6},{8,10},{12,14},{16,18},{20,22}} | collective-permute-start | bytes 786440 | tf_op jit(solution)/shard_map/ppermute | solution.py:265
  1.7 76.8 %collective-permute-start.6 = (bf16[12,256,512]{2,1,0:T(8,128)(2,1)}, bf16[12,256,512]{2,1,0:T(8,128)(2,1)}, u32[]{:S(2)}, u32[]{:S(2)}) collective-permute-start(bf16[12,256,512]{2,1,0:T(8,128)(2,1)} %tiles.1), channel_id=1, source_target_pairs={{1,2},{2,1},{5,6},{6,5},{9,10},{10,9},{13,14},{14,13},{17,18},{18,... | collective-permute-start | bytes 9437192 | tf_op jit(solution)/shard_map/ppermute | solution.py:292
  6.8 13.1 %collective-permute-start.1 = (bf16[1,256,512]{2,1,0:T(8,128)(2,1)S(1)}, bf16[1,256,512]{2,1,0:T(8,128)(2,1)}, u32[]{:S(2)}, u32[]{:S(2)}) collective-permute-start(bf16[1,256,512]{2,1,0:T(8,128)(2,1)S(1)} %broadcast_select_fusion.after), channel_id=1, source_target_pairs={{4,5},{6,7},{8,9},{10,11},{12,13},{14,15},{16,17},{18,19},{20,21},... | collective-permute-start | bytes 786440 | tf_op jit(solution)/shard_map/ppermute | solution.py:265
  8.1 1.9 %copy-start.2 = (bf16[12,256,512]{2,1,0:T(8,128)(2,1)S(1)}, bf16[12,256,512]{2,1,0:T(8,128)(2,1)}, u32[]{:S(2)}) copy-start(bf16[12,256,512]{2,1,0:T(8,128)(2,1)} %tiles.1) | copy-start | bytes 9437188
  12.2 28.4 %copy-start.3 = (bf16[12,256,512]{2,1,0:T(8,128)(2,1)S(1)}, bf16[12,256,512]{2,1,0:T(8,128)(2,1)}, u32[]{:S(2)}) copy-start(bf16[12,256,512]{2,1,0:T(8,128)(2,1)} %tiles.1) | copy-start | bytes 9437188
  12.2 76.5 %collective-permute-start.7 = (bf16[12,256,512]{2,1,0:T(8,128)(2,1)}, bf16[12,256,512]{2,1,0:T(8,128)(2,1)}, u32[]{:S(2)}, u32[]{:S(2)}) collective-permute-start(bf16[12,256,512]{2,1,0:T(8,128)(2,1)} %shard_map.43), channel_id=1, source_target_pairs={{0,1},{1,0},{2,3},{3,2},{4,5},{5,4},{6,7},{7,6},{8,9},{9,8},{10,11... | collective-permute-start | bytes 9437192 | tf_op jit(solution)/shard_map/ppermute | solution.py:297
  20.8 11.9 %collective-permute-start.4 = (bf16[1,256,512]{2,1,0:T(8,128)(2,1)S(1)}, bf16[1,256,512]{2,1,0:T(8,128)(2,1)S(1)}, u32[]{:S(2)}, u32[]{:S(2)}) collective-permute-start(bf16[1,256,512]{2,1,0:T(8,128)(2,1)S(1)} %broadcast_select_fusion.1), channel_id=1, source_target_pairs={{4,28},{8,16},{12,20},{16,8},{20,12},{5,29},{9,17},{13,21},{17,9},... | collective-permute-start | bytes 786440 | tf_op jit(solution)/shard_map/ppermute | solution.py:275
  24.3 8.5 %collective-permute-start.3 = (bf16[1,256,512]{2,1,0:T(8,128)(2,1)S(1)}, bf16[1,256,512]{2,1,0:T(8,128)(2,1)S(1)}, u32[]{:S(2)}, u32[]{:S(2)}) collective-permute-start(bf16[1,256,512]{2,1,0:T(8,128)(2,1)S(1)} %broadcast_select_fusion.1), channel_id=1, source_target_pairs={{4,20},{8,24},{12,28},{16,0},{20,4},{5,21},{9,25},{13,29},{17,1},{... | collective-permute-start | bytes 786440 | tf_op jit(solution)/shard_map/ppermute | solution.py:275
  25.6 8.2 %collective-permute-start.2 = (bf16[1,256,512]{2,1,0:T(8,128)(2,1)S(1)}, bf16[1,256,512]{2,1,0:T(8,128)(2,1)S(1)}, u32[]{:S(2)}, u32[]{:S(2)}) collective-permute-start(bf16[1,256,512]{2,1,0:T(8,128)(2,1)S(1)} %broadcast_select_fusion.1), channel_id=1, source_target_pairs={{4,12},{8,0},{12,4},{16,24},{20,28},{5,13},{9,1},{13,5},{17,25},{2... | collective-permute-start | bytes 786440 | tf_op jit(solution)/shard_map/ppermute | solution.py:275
  34.8 3.0 %collective-permute-start.5 = (bf16[4,1,256,512]{3,2,1,0:T(8,128)(2,1)}, bf16[4,1,256,512]{3,2,1,0:T(8,128)(2,1)}, u32[]{:S(2)}, u32[]{:S(2)}) collective-permute-start(bf16[4,1,256,512]{3,2,1,0:T(8,128)(2,1)} %pad_maximum_fusion.same), channel_id=1, source_target_pairs={{0,4},{4,0},{8,12},{12,8},{16,20},{20,16},{24,28},{28,24},{1,5},{5... | collective-permute-start | bytes 3145736 | tf_op jit(solution)/shard_map/ppermute | solution.py:277
  40.6 2.8 %copy-start = (bf16[48,256,256]{2,1,0:T(8,128)(2,1)S(1)}, bf16[48,256,256]{2,1,0:T(8,128)(2,1)}, u32[]{:S(2)}) copy-start(bf16[48,256,256]{2,1,0:T(8,128)(2,1)} %trailing.11) | copy-start | bytes 18874372
  48.8 2.8 %copy-start.1 = (bf16[48,256,256]{2,1,0:T(8,128)(2,1)S(1)}, bf16[48,256,256]{2,1,0:T(8,128)(2,1)}, u32[]{:S(2)}) copy-start(bf16[48,256,256]{2,1,0:T(8,128)(2,1)} %get-tuple-element.15.after.held) | copy-start | bytes 18874372
  53.6 41.9 %collective-permute-start.8 = (bf16[12,256,256]{2,1,0:T(8,128)(2,1)S(1)}, bf16[12,256,256]{2,1,0:T(8,128)(2,1)S(1)}, u32[]{:S(2)}, u32[]{:S(2)}) collective-permute-start(bf16[12,256,256]{2,1,0:T(8,128)(2,1)S(1)} %shard_map.39.after), channel_id=1, source_target_pairs={{0,3},{3,0},{4,7},{7,4},{8,11},{11,8},{12,15},{15,12},{16,19},{19,... | collective-permute-start | bytes 4718600 | tf_op jit(solution)/shard_map/ppermute | solution.py:312
  54.4 34.3 %slice-start = ((s8[6291456]{0:T(1024)(128)(4,1)}), s8[4194304]{0:T(1024)(128)(4,1)S(1)}, s32[]{:S(2)}) async-start(s8[6291456]{0:T(1024)(128)(4,1)} %bitcast.7), calls=%async_computation | async-start | bytes 8388608
  56.4 32.2 %slice-start.1 = ((s8[6291456]{0:T(1024)(128)(4,1)}), s8[2097152]{0:T(1024)(128)(4,1)S(1)}, s32[]{:S(2)}) async-start(s8[6291456]{0:T(1024)(128)(4,1)} %bitcast.7), calls=%async_computation.1 | async-start | bytes 4194304
  56.5 100.1 %collective-permute-start.10 = (bf16[12,256,256]{2,1,0:T(8,128)(2,1)S(1)}, bf16[12,256,256]{2,1,0:T(8,128)(2,1)S(1)}, u32[]{:S(2)}, u32[]{:S(2)}) collective-permute-start(bf16[12,256,256]{2,1,0:T(8,128)(2,1)S(1)} %shard_map.40.after), channel_id=1, source_target_pairs={{0,2},{3,1},{4,6},{7,5},{8,10},{11,9},{12,14},{15,13},{16,18},{19,... | collective-permute-start | bytes 4718600 | tf_op jit(solution)/shard_map/ppermute | solution.py:312
  82.2 74.4 %collective-permute-start.9 = (bf16[6,256,256]{2,1,0:T(8,128)(2,1)S(1)}, bf16[6,256,256]{2,1,0:T(8,128)(2,1)S(1)}, u32[]{:S(2)}, u32[]{:S(2)}) collective-permute-start(bf16[6,256,256]{2,1,0:T(8,128)(2,1)S(1)} %get-tuple-element.19), channel_id=1, source_target_pairs={{2,3},{1,0},{6,7},{5,4},{10,11},{9,8},{14,15},{13,12},{18,19},{17,... | collective-permute-start | bytes 2359304 | tf_op jit(solution)/shard_map/ppermute | solution.py:320
  87.3 70.9 %collective-permute-start.11 = (bf16[6,256,256]{2,1,0:T(8,128)(2,1)S(1)}, bf16[6,256,256]{2,1,0:T(8,128)(2,1)S(1)}, u32[]{:S(2)}, u32[]{:S(2)}) collective-permute-start(bf16[6,256,256]{2,1,0:T(8,128)(2,1)S(1)} %get-tuple-element.20), channel_id=1, source_target_pairs={{2,3},{1,0},{6,7},{5,4},{10,11},{9,8},{14,15},{13,12},{18,19},{17,... | collective-permute-start | bytes 2359304 | tf_op jit(solution)/shard_map/ppermute | solution.py:320

commit v5 on v0

v5 whole, which is shorter than its diff:
```python
import functools

import jax
import jax.numpy as jnp
from jax import lax
from jax.experimental import pallas as pl
from jax.experimental.pallas import tpu as pltpu
from jax.sharding import PartitionSpec as P

BF16 = jnp.bfloat16
SMALL_FLOPS, OWN_FLOPS = 1024, 5 * 10**9
ANYWHERE = pl.BlockSpec(memory_space=pl.ANY)


def call(body, grid, in_specs, out_specs, out_shape, held=False, flops=SMALL_FLOPS):
    return pl.pallas_call(
        body,
        grid_spec=pltpu.PrefetchScalarGridSpec(
            num_scalar_prefetch=1, grid=grid, in_specs=in_specs, out_specs=out_specs
        ),
        out_shape=out_shape,
        input_output_aliases={1: 0} if held else {},
        compiler_params=pltpu.CompilerParams(
            vmem_limit_bytes=(8 + 3 * lax.axis_size("col")) * 1024 * 1024
        ),
        cost_estimate=pl.CostEstimate(flops=flops, bytes_accessed=1024, transcendentals=0),
    )


def whole(array):
    return pl.BlockSpec(array.shape, lambda t, p: (0,) * array.ndim)


def tiles_at(array, count, start):
    shape = tuple(pl.Element(extent) for extent in (count,) + array.shape[1:])
    return pl.BlockSpec(shape, lambda t, p: (start(t, p[1]), 0, 0))


def step_of(count):
    return max(step for step in range(1, 6) if count % step == 0)


def shape_of(count, size, width=None):
    return jax.ShapeDtypeStruct((count, size, width or size), BF16)


def dot(left, right):
    return jnp.dot(left, right, preferred_element_type=jnp.float32)


def factor_rows(rows, inverses_t, couple_t):
    size = couple_t.shape[0]
    left = dot(rows[:, :size], inverses_t[0]).astype(BF16)
    reduced = (rows[:, size:].astype(jnp.float32) - dot(left, couple_t)).astype(BF16)
    right = dot(reduced, inverses_t[1]).astype(BF16)
    return left, right


def factor_tiles(tiles, inverses_t, couple_t):
    count, size, width = tiles.shape
    return factor_rows(tiles[...].reshape(count * size, width), inverses_t, couple_t[...])


def times_key(left, right, key_t):
    size = left.shape[1]
    total = dot(left, key_t[:size]) + dot(right, key_t[size:])
    return total.reshape(-1, size, size)


def subtract(trailing, total):
    return (trailing[...].astype(jnp.float32) - total).astype(BF16)


def keys_body(rows, info, same, other, inverses_t, couple_t, keys_t):
    size = couple_t.shape[0]

    def raw(tile):
        offset = info[0] ^ (tile % rows)
        index, place = offset // 2, tile // rows
        return jnp.where(offset % 2 == 0, same[index, place], other[index, place])

    couple = dot(raw(1)[:, :size], inverses_t[0]).astype(BF16)
    couple_t[...] = couple.astype(jnp.float32).T.astype(BF16)
    for j in range(keys_t.shape[0]):
        left, right = factor_rows(raw(j + 2), inverses_t, couple_t[...])
        keys_t[j, :size] = left.astype(jnp.float32).T.astype(BF16)
        keys_t[j, size:] = right.astype(jnp.float32).T.astype(BF16)


def make_keys(info, same, other, inverses_t, rows, cols):
    size, width = same.shape[2:]
    couple_t = jax.ShapeDtypeStruct((size, size), BF16)
    keys_t = jax.ShapeDtypeStruct((cols, width, size), BF16)
    return call(
        functools.partial(keys_body, rows),
        (1,),
        [whole(same), whole(other), whole(inverses_t)],
        [whole(couple_t), whole(keys_t)],
        [couple_t, keys_t],
    )(info, same, other, inverses_t)


def own_body(info, panel, inverses_t, couple_t, keys_t, trailing, out, factored):
    left, right = factor_tiles(panel, inverses_t, couple_t)
    out[...] = subtract(trailing, times_key(left, right, keys_t[info[1]]))
    count, size = panel.shape[:2]
    factored[:, :, :size] = left.reshape(count, size, size)
    factored[:, :, size:] = right.reshape(count, size, size)


def own_tiles(info, panel, small, trailing):
    tiles = panel.shape[0]
    step = step_of(tiles)
    rows = tiles_at(panel, step, lambda t, col: t * step)
    mine = tiles_at(trailing, step, lambda t, col: col * tiles + t * step)
    return call(
        own_body,
        (tiles // step,),
        [rows, *map(whole, small), mine],
        [mine, rows],
        [
            jax.ShapeDtypeStruct(trailing.shape, BF16),
            jax.ShapeDtypeStruct(panel.shape, BF16),
        ],
        flops=OWN_FLOPS,
    )(info, panel, *small, trailing)


def products_body(offset, first, info, after, factored, keys_t, piece):
    del after
    tiles, size, width = factored.shape
    key_t = keys_t[info[1] ^ offset]
    middle = first + (tiles - first) // 2
    for start, stop in ((first, middle), (middle, tiles)):
        rows = factored[start:stop].reshape((stop - start) * size, width)
        total = dot(rows, key_t).reshape(stop - start, size, size)
        piece[start - first:stop - first] = total.astype(BF16)


def products(info, after, factored, keys_t, offset, first):
    tiles, size, _ = factored.shape
    piece = shape_of(tiles - first, size)
    return call(
        functools.partial(products_body, offset, first),
        (1,),
        [ANYWHERE, whole(factored), whole(keys_t)],
        whole(piece),
        piece,
    )(info, after, factored, keys_t)


def raw_body(info, held, after, raw, inverses_t, couple_t, keys_t, trailing, out):
    del held, after
    left, right = factor_tiles(raw, inverses_t, couple_t)
    out[...] = subtract(trailing, times_key(left, right, keys_t[info[1]]))


def raw_tiles(info, held, after, raw, small, trailing, place):
    count = raw.shape[0]
    step = step_of(count)
    spot = tiles_at(trailing, step, lambda t, col: place(col) + t * step)
    return call(
        raw_body,
        (count // step,),
        [
            ANYWHERE,
            ANYWHERE,
            tiles_at(raw, step, lambda t, col: t * step),
            *map(whole, small),
            spot,
        ],
        spot,
        jax.ShapeDtypeStruct(trailing.shape, BF16),
        held=True,
    )(info, held, after, raw, *small, trailing)


def crossed_body(cols, info, after, raw, inverses_t, couple_t, keys_t, *pieces):
    del after
    left, right = factor_tiles(raw, inverses_t, couple_t)
    col = info[1]
    for k in range(cols // 2):
        target = jnp.clip(jnp.where(col < cols // 2, col - k, col + k), 0, cols - 1)
        pieces[k][...] = times_key(left, right, keys_t[target]).astype(BF16)


def crossed_tiles(info, after, raw, first, count, small, cols):
    step = step_of(count)
    piece = shape_of(count, raw.shape[1])
    return call(
        functools.partial(crossed_body, cols),
        (count // step,),
        [ANYWHERE, tiles_at(raw, step, lambda t, col: first + t * step), *map(whole, small)],
        [tiles_at(piece, step, lambda t, col: t * step)] * (cols // 2),
        [piece] * (cols // 2),
    )(info, after, raw, *small)


def update_body(which, info, held, trailing, *refs):
    del held
    *pieces, out = refs
    for i, piece in enumerate(pieces):
        @pl.when(which(info[1]) == i)
        def _(piece=piece):
            out[...] = subtract(trailing, piece[...].astype(jnp.float32))


def update(info, held, trailing, count, pieces, which):
    step = step_of(count)

    def place(col):
        spot = pieces[0][2](col)
        for i, (_, _, start) in enumerate(pieces[1:], 1):
            spot = jnp.where(which(col) == i, start(col), spot)
        return spot

    def chosen(i, array, first):
        return tiles_at(
            array, step, lambda t, col: first + jnp.where(which(col) == i, t * step, 0)
        )

    spot = tiles_at(trailing, step, lambda t, col: place(col) + t * step)
    return call(
        functools.partial(update_body, which),
        (count // step,),
        [ANYWHERE, spot] + [chosen(i, array, first) for i, (array, first, _) in enumerate(pieces)],
        spot,
        jax.ShapeDtypeStruct(trailing.shape, BF16),
        held=True,
    )(info, held, trailing, *[array for array, _, _ in pieces])


def copy_after(panel, first, waited):
    count, size, width = panel.shape[0] - first, *panel.shape[1:]
    step = step_of(count)

    def body(*refs):
        *_, tiles, out = refs
        out[...] = tiles[...]

    shape = shape_of(count, size, width)
    return call(
        body,
        (count // step,),
        [ANYWHERE] * len(waited) + [tiles_at(panel, step, lambda t, col: first + t * step)],
        tiles_at(shape, step, lambda t, col: t * step),
        shape,
    )(jnp.zeros((2,), jnp.int32), *waited, panel)


def spread_ends(first, cols):
    col = lax.axis_index("col")
    kept = first
    span = cols // 2
    while span > 1:
        pairs = []
        for c in range(0, cols, 2 * span):
            pairs += [(c, c + span), (cols - 1 - c, cols - 1 - c - span)]
        arrived = lax.ppermute(kept, "col", pairs)
        reached = (col % (2 * span) == span) | ((cols - 1 - col) % (2 * span) == span)
        kept = jnp.where(reached, arrived, kept)
        span //= 2
    return kept


def spread_across(head, wanted, rows):
    same = [head]
    for offset in range(2, rows, 2):
        same.append(lax.ppermute(head, "row", [(r, r ^ offset) for r in wanted]))
    same = jnp.stack(same)
    return same, lax.ppermute(same, "row", [(r, r ^ 1) for r in range(rows)])


def special_source(col, cols):
    return cols // 2 - (col >= cols // 2)


def shards(panel_cols, inverses, trailing):
    tiles = panel_cols.shape[0]
    rows = lax.axis_size("row")
    cols = lax.axis_size("col")
    col_index = lax.axis_index("col")
    low, high = cols // 2 - 1, cols // 2
    info = jnp.stack([lax.axis_index("row"), col_index]).astype(jnp.int32)
    inverses_t = jnp.swapaxes(inverses, 1, 2)

    head_tiles = (cols + 1) // rows + 1
    beside = [(c, c ^ 1) for c in range(cols)]
    inside = [(c, c ^ 1) for c in range(1, cols - 1)]

    crossed = lax.ppermute(panel_cols, "col", [(low, high), (high, low)])
    kept = spread_ends(panel_cols[:head_tiles], cols)
    near_first = lax.ppermute(panel_cols[:head_tiles], "col", beside)
    passed = lax.ppermute(kept, "col", inside)
    near_last = lax.ppermute(copy_after(panel_cols, head_tiles, [kept, near_first]), "col", beside)
    from_end = (col_index == 1) | (col_index == cols - 2)
    passed = jnp.where(from_end, near_first, passed)
    even = col_index % 2 == 0
    head = jnp.where(even, kept, passed)

    wanted = sorted({tile % rows for tile in range(1, cols + 2)})
    same, other = spread_across(head, wanted, rows)
    couple_t, keys_t = make_keys(info, same, other, inverses_t, rows, cols)
    small = (inverses_t, couple_t, keys_t)
    out, factored = own_tiles(info, panel_cols, small, trailing)

    sends = {
        offset: [
            (c, c ^ offset)
            for c in range(cols)
            if not (c == low and c ^ offset > low) and not (c == high and c ^ offset < high)
        ]
        for offset in range(cols - 1, 1, -1)
    }
    ends_only = all(c in (0, cols - 1) for pairs in sends.values() for c, _ in pairs)
    skipped = head_tiles if ends_only else 0
    arrived = {}
    after = out
    for offset, pairs in sends.items():
        after = products(info, after, factored, keys_t, offset, skipped)
        arrived[offset] = lax.ppermute(after, "col", pairs)

    out = raw_tiles(
        info, out, after, near_last, small, trailing, lambda col: (col ^ 1) * tiles + head_tiles
    )
    half = tiles // 2 if tiles % 2 == 0 else tiles
    mine, got = [], []
    after = out
    for first in range(0, tiles, half):
        after, *handed = crossed_tiles(info, after, crossed, first, half, small, cols)
        mine.append(after)
        handed = [
            lax.ppermute(piece, "col", [(high, high + k), (low, low - k)])
            for k, piece in enumerate(handed, 1)
        ]
        got.append(handed[0])
        for k, piece in enumerate(handed[1:], 2):
            here = (col_index == high + k) | (col_index == low - k)
            got[-1] = jnp.where(here, piece, got[-1])

    out = raw_tiles(info, out, after, near_first, small, trailing, lambda col: (col ^ 1) * tiles)
    if ends_only:
        far_head = jnp.where((col_index <= low) == even, passed, kept)
        out = raw_tiles(
            info, out, after, far_head, small, trailing,
            lambda col: jnp.where(col <= low, (cols - 1) * tiles, 0),
        )

    def far_offset(col, slot=2):
        return slot + ((col ^ special_source(col, cols)) <= slot)

    def inner(col):
        return (col == low) | (col == high)

    def special(array, i):
        return array, 0, lambda col: special_source(col, cols) * tiles + i * half

    def far(offset, i):
        first = min(i * half, tiles - skipped - half)
        return arrived[offset], first, lambda col: (col ^ offset) * tiles + skipped + first

    for slot in range(3, cols - 1):
        for i in range(tiles // half):
            out = update(
                info, out, trailing, half, [far(slot, i), far(slot + 1, i)],
                lambda col, slot=slot: far_offset(col, slot) - slot,
            )
    outer_far = sorted({far_offset(c) for c in range(cols) if not inner(c)})
    for i in range(tiles // half):
        out = update(
            info, out, trailing, half,
            [special(mine[i], i)] + [far(offset, i) for offset in outer_far],
            lambda col: jnp.where(inner(col), 0, far_offset(col) - outer_far[0] + 1),
        )
    for i in range(tiles // half):
        out = update(
            info, out, trailing, half, [special(got[i], i), far(2, i)],
            lambda col: jnp.where(inner(col), 1, 0),
        )
    return out


def solution(mesh):
    in_specs = (P("col", "row", None), P(), P(None, "row", "col"))
    out_specs = P(None, "row", "col")
    return jax.shard_map(shards, mesh=mesh, in_specs=in_specs, out_specs=out_specs, check_vma=False)
```

time: 439 us -> 158 us (0.36)
  waiting for transfers between devices: 397 us -> 68.5 us
  Pallas kernels: 0 us -> 42.5 us
  starting transfers between devices: 0.09 us -> 25.1 us
  matrix products: 18.9 us -> 0 us
  between operations: 13.1 us -> 0.19 us
  local copies, waits for them, and re-layouts: 2.8 us -> 15 us
    all_gather x1 -> x0, waiting for transfers between devices: 217 us -> none  [shards(): whole_panel = lax.all_gather(factored, 'col', axis=0, tiled=True)]
    psum x2 -> x0, waiting for transfers between devices: 180 us -> none  [broadcast(): return lax.psum(kept, axis)]
    ppermute x0 -> x13, waiting for transfers between devices: none -> 68.5 us  [the longest x2 30.8 us: shards(): arrived[offset] = lax.ppermute(after, 'col', pairs)]
    pallas_call x0 -> x14, Pallas kernels: none -> 42.5 us  [the longest x3 14.8 us: raw_tiles(): call(raw_body, (count // step,), [ANYWHERE, ANYWHERE, tiles_at(raw, step,...]
    ppermute x0 -> x13, starting transfers between devices: none -> 25.1 us  [the longest x3 8.06 us: spread_across(): same.append(lax.ppermute(head, 'row', [(r, r ^ offset) for r in wanted]))]
    dot_general x3 -> x0, matrix products: 18.9 us -> none  [the longest x1 12.6 us: shards(): jnp.einsum('tak,bk->tab', whole_panel, key_tile, preferred_element_type=j...]
    unnamed x4 -> x21, local copies, waits for them, and re-layouts: 0.01 us -> 13.3 us
  transfers between devices with their start and end apart: 3 -> 13, of which waited for: 3 -> 10; matrix products, arithmetic and copies ran while one was open for 0% -> 4% of each run, Pallas kernels for 0% -> 26%
where the time goes in v5:
time: 158 us; the launch traced here: 156 us
  waiting for transfers between devices  68.5 us (43%)
  Pallas kernels  42.5 us (27%)
  starting transfers between devices  25.1 us (16%)
  local copies, waits for them, and re-layouts  15 us (9%)
  other arithmetic  4.61 us (3%)
    ppermute x2, waiting for transfers between devices, shards(): arrived[offset] = lax.ppermute(after, 'col', pairs)  30.8 us
    ppermute x1, waiting for transfers between devices, shards(): lax.ppermute(copy_after(panel_cols, head_tiles, [kept, near_first]), 'col...  19.1 us
    pallas_call x3, Pallas kernels, raw_tiles(): call(raw_body, (count // step,), [ANYWHERE, ANYWHERE, tiles_at(raw, step,...  14.8 us
    unnamed x21, local copies, waits for them, and re-layouts  13.3 us
    ppermute x3, starting transfers between devices, spread_across(): same.append(lax.ppermute(head, 'row', [(r, r ^ offset) for r in wanted]))  8.06 us
    ppermute x3, waiting for transfers between devices, spread_across(): same.append(lax.ppermute(head, 'row', [(r, r ^ offset) for r in wanted]))  6.86 us
    pallas_call x4, Pallas kernels, update(): call(functools.partial(update_body, which), (count // step,), [ANYWHERE,...  6.33 us
    ppermute x1, waiting for transfers between devices, spread_ends(): arrived = lax.ppermute(kept, 'col', pairs)  5.42 us
  transfers between devices with their start and end apart: 13, of which 10 were waited for; matrix products, arithmetic and copies ran while one was open for 4% of the time, Pallas kernels for 26%

profile of v5, /device:TPU:4, one launch (start us, length us, event | category | flops | bytes accessed | tf_op | source)
XLA Modules:
  0.0 156.0 jit_solution(15818337817578324930)
XLA Ops:
  0.0 1.7 %slice.4 = bf16[1,256,512]{2,1,0:T(8,128)(2,1)} slice(bf16[12,256,512]{2,1,0:T(8,128)(2,1)} %refs_3_.1), slice={[0:1], [0:256], [0:512]} | slice | bytes 524288 | tf_op jit(solution)/shard_map/slice | solution.py:292
  1.7 5.2 %collective-permute-start = (bf16[1,256,512]{2,1,0:T(8,128)(2,1)}, bf16[1,256,512]{2,1,0:T(8,128)(2,1)}, u32[]{:S(2)}, u32[]{:S(2)}) collective-permute-start(bf16[1,256,512]{2,1,0:T(8,128)(2,1)} %slice.4), channel_id=1, source_target_pairs={{0,2},{3,1},{4,6},{7,5},{8,10},{11,9},{12,14},{15,13},{16,18},{19,... | collective-permute-start | bytes 786440 | tf_op jit(solution)/shard_map/ppermute | solution.py:259
  6.9 0.0 collective-permute-start.1
  6.9 0.9 collective-permute-start.8
  7.7 5.4 %collective-permute-done = bf16[1,256,512]{2,1,0:T(8,128)(2,1)} collective-permute-done((bf16[1,256,512]{2,1,0:T(8,128)(2,1)}, bf16[1,256,512]{2,1,0:T(8,128)(2,1)}, u32[]{:S(2)}, u32[]{:S(2)}) %collective-permute-start) | collective-permute-done | bytes 262176 | tf_op jit(solution)/shard_map/ppermute | solution.py:259
  13.2 1.7 %broadcast_select_fusion.2.refs_1_ = bf16[1,256,512]{2,1,0:T(8,128)(2,1)} fusion(bf16[1,256,512]{2,1,0:T(8,128)(2,1)} %collective-permute-done, pred[]{:T(512)S(6)} %or.6, bf16[12,256,512]{2,1,0:T(8,128)(2,1)} %refs_3_.1), kind=kLoop, calls=%fused_computation.3 | loop fusion | flops 131072 | bytes 786433 | tf_op jit(solution)/shard_map/jit(_where)/select_n | solution.py:261
  14.8 1.3 collective-permute-start.2
  16.1 1.5 collective-permute-done.1.refs_2_.raw
  17.6 0.0 copy-start.5
  17.6 0.0 copy-start.3
  17.6 2.0 %copy-done.3 = bf16[12,256,512]{2,1,0:T(8,128)(2,1)S(1)} copy-done((bf16[12,256,512]{2,1,0:T(8,128)(2,1)S(1)}, bf16[12,256,512]{2,1,0:T(8,128)(2,1)}, u32[]{:S(2)}) %copy-start.3) | copy-done | bytes 3145752
  19.6 4.9 %shard_map.41 = bf16[11,256,512]{2,1,0:T(8,128)(2,1)} custom-call(s32[2]{0:T(128)S(1)} %broadcast_1_refs_0_.2.refs_0_, bf16[1,256,512]{2,1,0:T(8,128)(2,1)} %broadcast_select_fusion.2.refs_1_, bf16[1,256,512]{2,1,0:T(8,128)(2,1)S(1)} %collective-permute-done.1.refs_2_.raw, bf16[12,256,512]{2,1,0:T(8,128)(2,1)S(1)} %copy-done.3), custom_call_target="tpu_custom_call" | custom-call | flops 1024 | bytes 1024 | tf_op jit(solution)/shard_map/pallas_call | solution.py:242
  24.5 2.4 %collective-permute-start.7 = (bf16[11,256,512]{2,1,0:T(8,128)(2,1)}, bf16[11,256,512]{2,1,0:T(8,128)(2,1)}, u32[]{:S(2)}, u32[]{:S(2)}) collective-permute-start(bf16[11,256,512]{2,1,0:T(8,128)(2,1)} %shard_map.41), channel_id=1, source_target_pairs={{0,1},{1,0},{2,3},{3,2},{4,5},{5,4},{6,7},{7,6},{8,9},{9,8},{10,11... | collective-permute-start | bytes 8650760 | tf_op jit(solution)/shard_map/ppermute | solution.py:295
  26.9 0.0 collective-permute-done.2
  26.9 0.0 copy-done.5
  26.9 1.8 %broadcast_select_fusion = (bf16[1,256,512]{2,1,0:T(8,128)(2,1)}, bf16[1,256,512]{2,1,0:T(8,128)(2,1)S(1)}) fusion(bf16[1,256,512]{2,1,0:T(8,128)(2,1)} %broadcast_select_fusion.2.refs_1_, pred[]{:T(512)S(6)} %eq.27, bf16[1,256,512]{2,1,0:T(8,128)(2,1)S(1)} %collective-permute-done.1.refs_2_.raw, bf16[1,256,512]{2,1,0:T(8,128)(2,1)} %collective-permute-done.2, ...), kind=kLoop, calls=%fused_computation.1 | loop fusion | flops 393216 | bytes 1310723 | tf_op jit(solution)/shard_map/jit(_where)/select_n | solution.py:343
  28.7 3.4 %collective-permute-start.3 = (bf16[1,256,512]{2,1,0:T(8,128)(2,1)S(1)}, bf16[1,256,512]{2,1,0:T(8,128)(2,1)S(1)}, u32[]{:S(2)}, u32[]{:S(2)}) collective-permute-start(bf16[1,256,512]{2,1,0:T(8,128)(2,1)S(1)} %get-tuple-element.22), channel_id=1, source_target_pairs={{4,12},{8,0},{12,4},{16,24},{20,28},{5,13},{9,1},{13,5},{17,25},{2... | collective-permute-start | bytes 786440 | tf_op jit(solution)/shard_map/ppermute | solution.py:269
  32.1 1.3 collective-permute-start.4
  33.4 3.4 %collective-permute-start.5 = (bf16[1,256,512]{2,1,0:T(8,128)(2,1)S(1)}, bf16[1,256,512]{2,1,0:T(8,128)(2,1)S(1)}, u32[]{:S(2)}, u32[]{:S(2)}) collective-permute-start(bf16[1,256,512]{2,1,0:T(8,128)(2,1)S(1)} %get-tuple-element.22), channel_id=1, source_target_pairs={{4,28},{8,16},{12,20},{16,8},{20,12},{5,29},{9,17},{13,21},{17,9},... | collective-permute-start | bytes 786440 | tf_op jit(solution)/shard_map/ppermute | solution.py:269
  36.8 0.8 collective-permute-done.3
  37.6 1.0 collective-permute-done.4
  38.6 5.0 %collective-permute-done.5 = bf16[1,256,512]{2,1,0:T(8,128)(2,1)S(1)} collective-permute-done((bf16[1,256,512]{2,1,0:T(8,128)(2,1)S(1)}, bf16[1,256,512]{2,1,0:T(8,128)(2,1)S(1)}, u32[]{:S(2)}, u32[]{:S(2)}) %collective-permute-start.5) | collective-permute-done | bytes 262176 | tf_op jit(solution)/shard_map/ppermute | solution.py:269
  43.6 1.1 pad_maximum_fusion.same
  44.7 0.0 collective-permute-start.6
  44.7 1.1 copy.11
  45.8 0.1 pad_add_fusion.info
  45.9 1.8 %collective-permute-done.6.other = bf16[4,1,256,512]{3,2,1,0:T(8,128)(2,1)} collective-permute-done((bf16[4,1,256,512]{3,2,1,0:T(8,128)(2,1)}, bf16[4,1,256,512]{3,2,1,0:T(8,128)(2,1)}, u32[]{:S(2)}, u32[]{:S(2)}) %collective-permute-start.6) | collective-permute-done | bytes 1048608 | tf_op jit(solution)/shard_map/ppermute | solution.py:271
  47.7 3.3 %shard_map.37 = (bf16[256,256]{1,0:T(8,128)(2,1)S(1)}, bf16[4,512,256]{2,1,0:T(8,128)(2,1)S(1)}) custom-call(s32[2]{0:T(128)S(1)} %pad_add_fusion.info, bf16[4,1,256,512]{3,2,1,0:T(8,128)(2,1)} %pad_maximum_fusion.same, bf16[4,1,256,512]{3,2,1,0:T(8,128)(2,1)} %collective-permute-done.6.other, bf16[2,256,256]{2,1,0:T(8,128)(2,1)S(1)} %bitcast.9), custom_call_target="tpu_custom_call" | custom-call | flops 1024 | bytes 1024 | tf_op jit(solution)/shard_map/pallas_call | solution.py:94
  51.0 0.0 copy-start.2
  51.0 2.8 %copy-done.2 = bf16[48,256,256]{2,1,0:T(8,128)(2,1)S(1)} copy-done((bf16[48,256,256]{2,1,0:T(8,128)(2,1)S(1)}, bf16[48,256,256]{2,1,0:T(8,128)(2,1)}, u32[]{:S(2)}) %copy-start.2) | copy-done | bytes 6291480
  53.8 0.0 copy-start.4
  53.8 1.9 %copy-done.4 = bf16[12,256,512]{2,1,0:T(8,128)(2,1)S(1)} copy-done((bf16[12,256,512]{2,1,0:T(8,128)(2,1)S(1)}, bf16[12,256,512]{2,1,0:T(8,128)(2,1)}, u32[]{:S(2)}) %copy-start.4) | copy-done | bytes 3145752
  55.7 0.0 slice-start
  55.7 5.1 %shard_map.38 = (bf16[48,256,256]{2,1,0:T(8,128)(2,1)}, bf16[12,256,512]{2,1,0:T(8,128)(2,1)S(1)}) custom-call(s32[2]{0:T(128)S(1)} %pad_add_fusion.info, bf16[12,256,512]{2,1,0:T(8,128)(2,1)S(1)} %copy-done.4, bf16[2,256,256]{2,1,0:T(8,128)(2,1)S(1)} %bitcast.10, bf16[256,256]{1,0:T(8,128)(2,1)S(1)} %get-tuple-element.13.couple_t, ...), custom_call_target="tpu_custom_call" | custom-call | flops 5000000000 | bytes 1024 | tf_op jit(solution)/shard_map/pallas_call | solution.py:116
  60.8 0.0 copy-start
  60.8 2.8 %copy-done = bf16[48,256,256]{2,1,0:T(8,128)(2,1)S(1)} copy-done((bf16[48,256,256]{2,1,0:T(8,128)(2,1)S(1)}, bf16[48,256,256]{2,1,0:T(8,128)(2,1)}, u32[]{:S(2)}) %copy-start) | copy-done | bytes 6291480
  63.6 1.5 shard_map.39.after
  65.1 3.3 %collective-permute-start.9 = (bf16[11,256,256]{2,1,0:T(8,128)(2,1)S(1)}, bf16[11,256,256]{2,1,0:T(8,128)(2,1)S(1)}, u32[]{:S(2)}, u32[]{:S(2)}) collective-permute-start(bf16[11,256,256]{2,1,0:T(8,128)(2,1)S(1)} %shard_map.39.after), channel_id=1, source_target_pairs={{0,3},{3,0},{4,7},{7,4},{8,11},{11,8},{12,15},{15,12},{16,19},{19,... | collective-permute-start | bytes 4325384 | tf_op jit(solution)/shard_map/ppermute | solution.py:321
  68.3 1.5 shard_map.40.after
  69.8 1.4 collective-permute-start.11
  71.2 19.1 %collective-permute-done.7.raw = bf16[11,256,512]{2,1,0:T(8,128)(2,1)} collective-permute-done((bf16[11,256,512]{2,1,0:T(8,128)(2,1)}, bf16[11,256,512]{2,1,0:T(8,128)(2,1)}, u32[]{:S(2)}, u32[]{:S(2)}) %collective-permute-start.7) | collective-permute-done | bytes 2883616 | tf_op jit(solution)/shard_map/ppermute | solution.py:295
  90.2 0.0 slice-done
  90.2 0.0 slice-done.1
  90.2 11.1 %shard_map.42.after.held = bf16[48,256,256]{2,1,0:T(8,128)(2,1)} custom-call(s32[2]{0:T(128)S(1)} %pad_add_fusion.info, bf16[48,256,256]{2,1,0:T(8,128)(2,1)} %get-tuple-element.15.after.held, bf16[11,256,256]{2,1,0:T(8,128)(2,1)S(1)} %shard_map.40.after, bf16[11,256,512]{2,1,0:T(8,128)(2,1)} %collective-permute-done.7.raw, ...), custom_call_target="tpu_custom_call", output_to_operand_aliasing={{}: (1, {})} | custom-call | flops 1024 | bytes 1024 | tf_op jit(solution)/shard_map/pallas_call | solution.py:162
  101.4 0.0 collective-permute-done.8.raw
  101.4 2.8 %copy-done.1 = bf16[48,256,256]{2,1,0:T(8,128)(2,1)S(1)} copy-done((bf16[48,256,256]{2,1,0:T(8,128)(2,1)S(1)}, bf16[48,256,256]{2,1,0:T(8,128)(2,1)}, u32[]{:S(2)}) %copy-start.1) | copy-done | bytes 6291480
  104.1 2.6 %shard_map.43 = (bf16[6,256,256]{2,1,0:T(8,128)(2,1)S(1)}, bf16[6,256,256]{2,1,0:T(8,128)(2,1)S(1)}) custom-call(s32[2]{0:T(128)S(1)} %pad_add_fusion.info, bf16[48,256,256]{2,1,0:T(8,128)(2,1)S(1)} %copy-done.1, bf16[12,256,512]{2,1,0:T(8,128)(2,1)S(1)} %collective-permute-done.8.raw, bf16[2,256,256]{2,1,0:T(8,128)(2,1)S(1)} %bitcast.12, ...), custom_call_target="tpu_custom_call" | custom-call | flops 1024 | bytes 1024 | tf_op jit(solution)/shard_map/pallas_call | solution.py:190
  106.8 0.0 copy-start.6
  106.8 1.4 collective-permute-start.10
  108.2 2.6 %shard_map.44 = (bf16[6,256,256]{2,1,0:T(8,128)(2,1)S(1)}, bf16[6,256,256]{2,1,0:T(8,128)(2,1)S(1)}) custom-call(s32[2]{0:T(128)S(1)} %pad_add_fusion.info, bf16[6,256,256]{2,1,0:T(8,128)(2,1)S(1)} %get-tuple-element.17.after.refs_0_, bf16[12,256,512]{2,1,0:T(8,128)(2,1)S(1)} %collective-permute-done.8.raw, bf16[2,256,256]{2,1,0:T(8,128)(2,1)S(1)} %bitcast.13, ...), custom_call_target="tpu_custom_call" | custom-call | flops 1024 | bytes 1024 | tf_op jit(solution)/shard_map/pallas_call | solution.py:190
  110.8 1.3 collective-permute-start.12
  112.1 0.0 copy-done.6
  112.1 0.0 copy-start.7
  112.1 1.8 %shard_map.45.held = bf16[48,256,256]{2,1,0:T(8,128)(2,1)} custom-call(s32[2]{0:T(128)S(1)} %pad_add_fusion.info, bf16[48,256,256]{2,1,0:T(8,128)(2,1)} %shard_map.42.after.held, bf16[6,256,256]{2,1,0:T(8,128)(2,1)S(1)} %get-tuple-element.18.after.refs_0_, bf16[1,256,512]{2,1,0:T(8,128)(2,1)S(1)} %copy-done.6, ...), custom_call_target="tpu_custom_call", output_to_operand_aliasing={{}: (1, {})} | custom-call | flops 1024 | bytes 1024 | tf_op jit(solution)/shard_map/pallas_call | solution.py:162
  114.0 0.0 copy-done.7
  114.0 1.8 %shard_map.46.held = bf16[48,256,256]{2,1,0:T(8,128)(2,1)} custom-call(s32[2]{0:T(128)S(1)} %pad_add_fusion.info, bf16[48,256,256]{2,1,0:T(8,128)(2,1)} %shard_map.45.held, bf16[6,256,256]{2,1,0:T(8,128)(2,1)S(1)} %get-tuple-element.18.after.refs_0_, bf16[1,256,512]{2,1,0:T(8,128)(2,1)S(1)} %copy-done.7, ...), custom_call_target="tpu_custom_call", output_to_operand_aliasing={{}: (1, {})} | custom-call | flops 1024 | bytes 1024 | tf_op jit(solution)/shard_map/pallas_call | solution.py:162
  115.8 7.4 %collective-permute-done.9.refs_1_ = bf16[11,256,256]{2,1,0:T(8,128)(2,1)S(1)} collective-permute-done((bf16[11,256,256]{2,1,0:T(8,128)(2,1)S(1)}, bf16[11,256,256]{2,1,0:T(8,128)(2,1)S(1)}, u32[]{:S(2)}, u32[]{:S(2)}) %collective-permute-start.9) | collective-permute-done | bytes 1441824 | tf_op jit(solution)/shard_map/ppermute | solution.py:321
  123.2 1.6 %shard_map.47.held = bf16[48,256,256]{2,1,0:T(8,128)(2,1)} custom-call(s32[2]{0:T(128)S(1)} %pad_add_fusion.info, bf16[48,256,256]{2,1,0:T(8,128)(2,1)} %shard_map.46.held, bf16[48,256,256]{2,1,0:T(8,128)(2,1)S(1)} %bitcast.8, bf16[6,256,256]{2,1,0:T(8,128)(2,1)S(1)} %get-tuple-element.17.after.refs_0_, ...), custom_call_target="tpu_custom_call", output_to_operand_aliasing={{}: (1, {})} | custom-call | flops 1024 | bytes 1024 | tf_op jit(solution)/shard_map/pallas_call | solution.py:223
  124.8 1.6 %shard_map.48.held = bf16[48,256,256]{2,1,0:T(8,128)(2,1)} custom-call(s32[2]{0:T(128)S(1)} %pad_add_fusion.info, bf16[48,256,256]{2,1,0:T(8,128)(2,1)} %shard_map.47.held, bf16[48,256,256]{2,1,0:T(8,128)(2,1)S(1)} %bitcast.8, bf16[6,256,256]{2,1,0:T(8,128)(2,1)S(1)} %get-tuple-element.18.after.refs_0_, ...), custom_call_target="tpu_custom_call", output_to_operand_aliasing={{}: (1, {})} | custom-call | flops 1024 | bytes 1024 | tf_op jit(solution)/shard_map/pallas_call | solution.py:223
  126.4 23.4 %collective-permute-done.11.refs_1_ = bf16[11,256,256]{2,1,0:T(8,128)(2,1)S(1)} collective-permute-done((bf16[11,256,256]{2,1,0:T(8,128)(2,1)S(1)}, bf16[11,256,256]{2,1,0:T(8,128)(2,1)S(1)}, u32[]{:S(2)}, u32[]{:S(2)}) %collective-permute-start.11) | collective-permute-done | bytes 1441824 | tf_op jit(solution)/shard_map/ppermute | solution.py:321
  149.8 0.0 collective-permute-done.10.refs_0_
  149.8 1.6 %shard_map.49.held = bf16[48,256,256]{2,1,0:T(8,128)(2,1)} custom-call(s32[2]{0:T(128)S(1)} %pad_add_fusion.info, bf16[48,256,256]{2,1,0:T(8,128)(2,1)} %shard_map.48.held, bf16[48,256,256]{2,1,0:T(8,128)(2,1)S(1)} %bitcast.8, bf16[6,256,256]{2,1,0:T(8,128)(2,1)S(1)} %collective-permute-done.10.refs_0_, ...), custom_call_target="tpu_custom_call", output_to_operand_aliasing={{}: (1, {})} | custom-call | flops 1024 | bytes 1024 | tf_op jit(solution)/shard_map/pallas_call | solution.py:223
  151.4 3.0 %collective-permute-done.12.refs_0_ = bf16[6,256,256]{2,1,0:T(8,128)(2,1)S(1)} collective-permute-done((bf16[6,256,256]{2,1,0:T(8,128)(2,1)S(1)}, bf16[6,256,256]{2,1,0:T(8,128)(2,1)S(1)}, u32[]{:S(2)}, u32[]{:S(2)}) %collective-permute-start.12) | collective-permute-done | bytes 786464 | tf_op jit(solution)/shard_map/ppermute | solution.py:333
  154.4 1.6 %shard_map.50 = bf16[48,256,256]{2,1,0:T(8,128)(2,1)} custom-call(s32[2]{0:T(128)S(1)} %pad_add_fusion.info, bf16[48,256,256]{2,1,0:T(8,128)(2,1)} %shard_map.49.held, bf16[48,256,256]{2,1,0:T(8,128)(2,1)S(1)} %bitcast.8, bf16[6,256,256]{2,1,0:T(8,128)(2,1)S(1)} %collective-permute-done.12.refs_0_, ...), custom_call_target="tpu_custom_call", output_to_operand_aliasing={{}: (1, {})} | custom-call | flops 1024 | bytes 1024 | tf_op jit(solution)/shard_map/pallas_call | solution.py:223
  (4 shorter events, 0.0 us)
Async XLA Ops:
  1.7 11.5 %collective-permute-start = (bf16[1,256,512]{2,1,0:T(8,128)(2,1)}, bf16[1,256,512]{2,1,0:T(8,128)(2,1)}, u32[]{:S(2)}, u32[]{:S(2)}) collective-permute-start(bf16[1,256,512]{2,1,0:T(8,128)(2,1)} %slice.4), channel_id=1, source_target_pairs={{0,2},{3,1},{4,6},{7,5},{8,10},{11,9},{12,14},{15,13},{16,18},{19,... | collective-permute-start | bytes 786440 | tf_op jit(solution)/shard_map/ppermute | solution.py:259
  6.9 10.8 %collective-permute-start.1 = (bf16[1,256,512]{2,1,0:T(8,128)(2,1)}, bf16[1,256,512]{2,1,0:T(8,128)(2,1)S(1)}, u32[]{:S(2)}, u32[]{:S(2)}) collective-permute-start(bf16[1,256,512]{2,1,0:T(8,128)(2,1)} %slice.4), channel_id=1, source_target_pairs={{0,1},{1,0},{2,3},{3,2},{4,5},{5,4},{6,7},{7,6},{8,9},{9,8},{10,11... | collective-permute-start | bytes 786440 | tf_op jit(solution)/shard_map/ppermute | solution.py:293
  6.9 94.5 %collective-permute-start.8 = (bf16[12,256,512]{2,1,0:T(8,128)(2,1)}, bf16[12,256,512]{2,1,0:T(8,128)(2,1)S(1)}, u32[]{:S(2)}, u32[]{:S(2)}) collective-permute-start(bf16[12,256,512]{2,1,0:T(8,128)(2,1)} %refs_3_.1), channel_id=1, source_target_pairs={{1,2},{2,1},{5,6},{6,5},{9,10},{10,9},{13,14},{14,13},{17,18},{18,... | collective-permute-start | bytes 9437192 | tf_op jit(solution)/shard_map/ppermute | solution.py:291
  14.8 12.1 %collective-permute-start.2 = (bf16[1,256,512]{2,1,0:T(8,128)(2,1)}, bf16[1,256,512]{2,1,0:T(8,128)(2,1)}, u32[]{:S(2)}, u32[]{:S(2)}) collective-permute-start(bf16[1,256,512]{2,1,0:T(8,128)(2,1)} %broadcast_select_fusion.2.refs_1_), channel_id=1, source_target_pairs={{1,0},{2,3},{5,4},{6,7},{9,8},{10,11},{13,12},{14,15},{17,16},{18,... | collective-permute-start | bytes 786440 | tf_op jit(solution)/shard_map/ppermute | solution.py:294
  17.6 9.3 %copy-start.5 = (bf16[1,256,512]{2,1,0:T(8,128)(2,1)}, bf16[1,256,512]{2,1,0:T(8,128)(2,1)S(1)}, u32[]{:S(2)}) copy-start(bf16[1,256,512]{2,1,0:T(8,128)(2,1)S(1)} %collective-permute-done.1.refs_2_.raw) | copy-start | bytes 786436
  17.6 2.0 %copy-start.3 = (bf16[12,256,512]{2,1,0:T(8,128)(2,1)S(1)}, bf16[12,256,512]{2,1,0:T(8,128)(2,1)}, u32[]{:S(2)}) copy-start(bf16[12,256,512]{2,1,0:T(8,128)(2,1)} %refs_3_.1) | copy-start | bytes 9437188
  24.5 65.7 %collective-permute-start.7 = (bf16[11,256,512]{2,1,0:T(8,128)(2,1)}, bf16[11,256,512]{2,1,0:T(8,128)(2,1)}, u32[]{:S(2)}, u32[]{:S(2)}) collective-permute-start(bf16[11,256,512]{2,1,0:T(8,128)(2,1)} %shard_map.41), channel_id=1, source_target_pairs={{0,1},{1,0},{2,3},{3,2},{4,5},{5,4},{6,7},{7,6},{8,9},{9,8},{10,11... | collective-permute-start | bytes 8650760 | tf_op jit(solution)/shard_map/ppermute | solution.py:295
  28.7 8.9 %collective-permute-start.3 = (bf16[1,256,512]{2,1,0:T(8,128)(2,1)S(1)}, bf16[1,256,512]{2,1,0:T(8,128)(2,1)S(1)}, u32[]{:S(2)}, u32[]{:S(2)}) collective-permute-start(bf16[1,256,512]{2,1,0:T(8,128)(2,1)S(1)} %get-tuple-element.22), channel_id=1, source_target_pairs={{4,12},{8,0},{12,4},{16,24},{20,28},{5,13},{9,1},{13,5},{17,25},{2... | collective-permute-start | bytes 786440 | tf_op jit(solution)/shard_map/ppermute | solution.py:269
  32.1 6.5 %collective-permute-start.4 = (bf16[1,256,512]{2,1,0:T(8,128)(2,1)S(1)}, bf16[1,256,512]{2,1,0:T(8,128)(2,1)S(1)}, u32[]{:S(2)}, u32[]{:S(2)}) collective-permute-start(bf16[1,256,512]{2,1,0:T(8,128)(2,1)S(1)} %get-tuple-element.22), channel_id=1, source_target_pairs={{4,20},{8,24},{12,28},{16,0},{20,4},{5,21},{9,25},{13,29},{17,1},{... | collective-permute-start | bytes 786440 | tf_op jit(solution)/shard_map/ppermute | solution.py:269
  33.4 10.2 %collective-permute-start.5 = (bf16[1,256,512]{2,1,0:T(8,128)(2,1)S(1)}, bf16[1,256,512]{2,1,0:T(8,128)(2,1)S(1)}, u32[]{:S(2)}, u32[]{:S(2)}) collective-permute-start(bf16[1,256,512]{2,1,0:T(8,128)(2,1)S(1)} %get-tuple-element.22), channel_id=1, source_target_pairs={{4,28},{8,16},{12,20},{16,8},{20,12},{5,29},{9,17},{13,21},{17,9},... | collective-permute-start | bytes 786440 | tf_op jit(solution)/shard_map/ppermute | solution.py:269
  44.7 3.0 %collective-permute-start.6 = (bf16[4,1,256,512]{3,2,1,0:T(8,128)(2,1)}, bf16[4,1,256,512]{3,2,1,0:T(8,128)(2,1)}, u32[]{:S(2)}, u32[]{:S(2)}) collective-permute-start(bf16[4,1,256,512]{3,2,1,0:T(8,128)(2,1)} %pad_maximum_fusion.same), channel_id=1, source_target_pairs={{0,4},{4,0},{8,12},{12,8},{16,20},{20,16},{24,28},{28,24},{1,5},{5... | collective-permute-start | bytes 3145736 | tf_op jit(solution)/shard_map/ppermute | solution.py:271
  51.0 2.8 %copy-start.2 = (bf16[48,256,256]{2,1,0:T(8,128)(2,1)S(1)}, bf16[48,256,256]{2,1,0:T(8,128)(2,1)}, u32[]{:S(2)}) copy-start(bf16[48,256,256]{2,1,0:T(8,128)(2,1)} %trailing.15) | copy-start | bytes 18874372
  53.8 1.9 %copy-start.4 = (bf16[12,256,512]{2,1,0:T(8,128)(2,1)S(1)}, bf16[12,256,512]{2,1,0:T(8,128)(2,1)}, u32[]{:S(2)}) copy-start(bf16[12,256,512]{2,1,0:T(8,128)(2,1)} %refs_3_.1) | copy-start | bytes 9437188
  55.7 34.5 %slice-start = ((s8[6291456]{0:T(1024)(128)(4,1)}), s8[2097152]{0:T(1024)(128)(4,1)S(1)}, s32[]{:S(2)}) async-start(s8[6291456]{0:T(1024)(128)(4,1)} %bitcast.7), calls=%async_computation | async-start | bytes 4194304
  60.8 2.8 %copy-start = (bf16[48,256,256]{2,1,0:T(8,128)(2,1)S(1)}, bf16[48,256,256]{2,1,0:T(8,128)(2,1)}, u32[]{:S(2)}) copy-start(bf16[48,256,256]{2,1,0:T(8,128)(2,1)} %get-tuple-element.15.after.held) | copy-start | bytes 18874372
  63.6 26.6 %slice-start.1 = ((s8[6291456]{0:T(1024)(128)(4,1)}), s8[4194304]{0:T(1024)(128)(4,1)S(1)}, s32[]{:S(2)}) async-start(s8[6291456]{0:T(1024)(128)(4,1)} %bitcast.7), calls=%async_computation.1 | async-start | bytes 8388608
  65.1 58.1 %collective-permute-start.9 = (bf16[11,256,256]{2,1,0:T(8,128)(2,1)S(1)}, bf16[11,256,256]{2,1,0:T(8,128)(2,1)S(1)}, u32[]{:S(2)}, u32[]{:S(2)}) collective-permute-start(bf16[11,256,256]{2,1,0:T(8,128)(2,1)S(1)} %shard_map.39.after), channel_id=1, source_target_pairs={{0,3},{3,0},{4,7},{7,4},{8,11},{11,8},{12,15},{15,12},{16,19},{19,... | collective-permute-start | bytes 4325384 | tf_op jit(solution)/shard_map/ppermute | solution.py:321
  69.8 80.0 %collective-permute-start.11 = (bf16[11,256,256]{2,1,0:T(8,128)(2,1)S(1)}, bf16[11,256,256]{2,1,0:T(8,128)(2,1)S(1)}, u32[]{:S(2)}, u32[]{:S(2)}) collective-permute-start(bf16[11,256,256]{2,1,0:T(8,128)(2,1)S(1)} %shard_map.40.after), channel_id=1, source_target_pairs={{0,2},{3,1},{4,6},{7,5},{8,10},{11,9},{12,14},{15,13},{16,18},{19,... | collective-permute-start | bytes 4325384 | tf_op jit(solution)/shard_map/ppermute | solution.py:321
  101.4 2.8 %copy-start.1 = (bf16[48,256,256]{2,1,0:T(8,128)(2,1)S(1)}, bf16[48,256,256]{2,1,0:T(8,128)(2,1)}, u32[]{:S(2)}) copy-start(bf16[48,256,256]{2,1,0:T(8,128)(2,1)} %shard_map.42.after.held) | copy-start | bytes 18874372
  106.8 5.4 %copy-start.6 = (bf16[1,256,512]{2,1,0:T(8,128)(2,1)S(1)}, bf16[1,256,512]{2,1,0:T(8,128)(2,1)}, u32[]{:S(2)}) copy-start(bf16[1,256,512]{2,1,0:T(8,128)(2,1)} %copy-done.5) | copy-start | bytes 786436
  106.8 43.0 %collective-permute-start.10 = (bf16[6,256,256]{2,1,0:T(8,128)(2,1)S(1)}, bf16[6,256,256]{2,1,0:T(8,128)(2,1)S(1)}, u32[]{:S(2)}, u32[]{:S(2)}) collective-permute-start(bf16[6,256,256]{2,1,0:T(8,128)(2,1)S(1)} %get-tuple-element.19), channel_id=1, source_target_pairs={{2,3},{1,0},{6,7},{5,4},{10,11},{9,8},{14,15},{13,12},{18,19},{17,... | collective-permute-start | bytes 2359304 | tf_op jit(solution)/shard_map/ppermute | solution.py:333
  110.8 43.6 %collective-permute-start.12 = (bf16[6,256,256]{2,1,0:T(8,128)(2,1)S(1)}, bf16[6,256,256]{2,1,0:T(8,128)(2,1)S(1)}, u32[]{:S(2)}, u32[]{:S(2)}) collective-permute-start(bf16[6,256,256]{2,1,0:T(8,128)(2,1)S(1)} %get-tuple-element.20), channel_id=1, source_target_pairs={{2,3},{1,0},{6,7},{5,4},{10,11},{9,8},{14,15},{13,12},{18,19},{17,... | collective-permute-start | bytes 2359304 | tf_op jit(solution)/shard_map/ppermute | solution.py:333
  112.1 1.9 %copy-start.7 = (bf16[1,256,512]{2,1,0:T(8,128)(2,1)S(1)}, bf16[1,256,512]{2,1,0:T(8,128)(2,1)}, u32[]{:S(2)}) copy-start(bf16[1,256,512]{2,1,0:T(8,128)(2,1)} %get-tuple-element.21.raw) | copy-start | bytes 786436

commit v6 on v5

--- a/solution.py
+++ b/solution.py
@@ -36,8 +36,12 @@
     return pl.BlockSpec(shape, lambda t, p: (start(t, p[1]), 0, 0))
 
 
-def step_of(count):
-    return max(step for step in range(1, 6) if count % step == 0)
+def steps_of(count):
+    steps = -(-count // 4)
+    step = -(-count // steps)
+    if count % step == 0:
+        return step, steps, lambda t: t * step
+    return step, steps, lambda t: jnp.minimum(t * step, count - step)
 
 
 def shape_of(count, size, width=None):
@@ -110,12 +114,12 @@
 
 def own_tiles(info, panel, small, trailing):
     tiles = panel.shape[0]
-    step = step_of(tiles)
-    rows = tiles_at(panel, step, lambda t, col: t * step)
-    mine = tiles_at(trailing, step, lambda t, col: col * tiles + t * step)
+    step, steps, at = steps_of(tiles)
+    rows = tiles_at(panel, step, lambda t, col: at(t))
+    mine = tiles_at(trailing, step, lambda t, col: col * tiles + at(t))
     return call(
         own_body,
-        (tiles // step,),
+        (steps,),
         [rows, *map(whole, small), mine],
         [mine, rows],
         [
@@ -149,28 +153,30 @@
     )(info, after, factored, keys_t)
 
 
-def raw_body(info, held, after, raw, inverses_t, couple_t, keys_t, trailing, out):
+def raw_body(info, held, after, raw, inverses_t, couple_t, keys_t, trailing, out, done):
     del held, after
+    done[...] = jnp.zeros_like(done)
     left, right = factor_tiles(raw, inverses_t, couple_t)
     out[...] = subtract(trailing, times_key(left, right, keys_t[info[1]]))
 
 
 def raw_tiles(info, held, after, raw, small, trailing, place):
     count = raw.shape[0]
-    step = step_of(count)
-    spot = tiles_at(trailing, step, lambda t, col: place(col) + t * step)
+    step, steps, at = steps_of(count)
+    spot = tiles_at(trailing, step, lambda t, col: place(col) + at(t))
+    done = jax.ShapeDtypeStruct((8, 128), jnp.float32)
     return call(
         raw_body,
-        (count // step,),
+        (steps,),
         [
             ANYWHERE,
             ANYWHERE,
-            tiles_at(raw, step, lambda t, col: t * step),
+            tiles_at(raw, step, lambda t, col: at(t)),
             *map(whole, small),
             spot,
         ],
-        spot,
-        jax.ShapeDtypeStruct(trailing.shape, BF16),
+        [spot, whole(done)],
+        [jax.ShapeDtypeStruct(trailing.shape, BF16), done],
         held=True,
     )(info, held, after, raw, *small, trailing)
 
@@ -185,13 +191,13 @@
 
 
 def crossed_tiles(info, after, raw, first, count, small, cols):
-    step = step_of(count)
+    step, steps, at = steps_of(count)
     piece = shape_of(count, raw.shape[1])
     return call(
         functools.partial(crossed_body, cols),
-        (count // step,),
-        [ANYWHERE, tiles_at(raw, step, lambda t, col: first + t * step), *map(whole, small)],
-        [tiles_at(piece, step, lambda t, col: t * step)] * (cols // 2),
+        (steps,),
+        [ANYWHERE, tiles_at(raw, step, lambda t, col: first + at(t)), *map(whole, small)],
+        [tiles_at(piece, step, lambda t, col: at(t))] * (cols // 2),
         [piece] * (cols // 2),
     )(info, after, raw, *small)
 
@@ -206,7 +212,7 @@
 
 
 def update(info, held, trailing, count, pieces, which):
-    step = step_of(count)
+    step, steps, at = steps_of(count)
 
     def place(col):
         spot = pieces[0][2](col)
@@ -216,13 +222,13 @@
 
     def chosen(i, array, first):
         return tiles_at(
-            array, step, lambda t, col: first + jnp.where(which(col) == i, t * step, 0)
+            array, step, lambda t, col: first + jnp.where(which(col) == i, at(t), 0)
         )
 
-    spot = tiles_at(trailing, step, lambda t, col: place(col) + t * step)
+    spot = tiles_at(trailing, step, lambda t, col: place(col) + at(t))
     return call(
         functools.partial(update_body, which),
-        (count // step,),
+        (steps,),
         [ANYWHERE, spot] + [chosen(i, array, first) for i, (array, first, _) in enumerate(pieces)],
         spot,
         jax.ShapeDtypeStruct(trailing.shape, BF16),
@@ -230,22 +236,15 @@
     )(info, held, trailing, *[array for array, _, _ in pieces])
 
 
-def copy_after(panel, first, waited):
-    count, size, width = panel.shape[0] - first, *panel.shape[1:]
-    step = step_of(count)
-
-    def body(*refs):
-        *_, tiles, out = refs
-        out[...] = tiles[...]
-
-    shape = shape_of(count, size, width)
-    return call(
-        body,
-        (count // step,),
-        [ANYWHERE] * len(waited) + [tiles_at(panel, step, lambda t, col: first + t * step)],
-        tiles_at(shape, step, lambda t, col: t * step),
-        shape,
-    )(jnp.zeros((2,), jnp.int32), *waited, panel)
+def gate(array, waited):
+    return call(
+        lambda *refs: None,
+        (1,),
+        [ANYWHERE] * (1 + len(waited)),
+        ANYWHERE,
+        jax.ShapeDtypeStruct(array.shape, array.dtype),
+        held=True,
+    )(jnp.zeros((2,), jnp.int32), array, *waited)
 
 
 def spread_ends(first, cols):
@@ -291,8 +290,10 @@
     crossed = lax.ppermute(panel_cols, "col", [(low, high), (high, low)])
     kept = spread_ends(panel_cols[:head_tiles], cols)
     near_first = lax.ppermute(panel_cols[:head_tiles], "col", beside)
+    rest = panel_cols[head_tiles:]
+    kept = gate(kept, [rest])
     passed = lax.ppermute(kept, "col", inside)
-    near_last = lax.ppermute(copy_after(panel_cols, head_tiles, [kept, near_first]), "col", beside)
+    near_last = lax.ppermute(gate(rest, [kept, near_first]), "col", beside)
     from_end = (col_index == 1) | (col_index == cols - 2)
     passed = jnp.where(from_end, near_first, passed)
     even = col_index % 2 == 0
@@ -315,17 +316,16 @@
     ends_only = all(c in (0, cols - 1) for pairs in sends.values() for c, _ in pairs)
     skipped = head_tiles if ends_only else 0
     arrived = {}
-    after = out
+    after = factored
     for offset, pairs in sends.items():
         after = products(info, after, factored, keys_t, offset, skipped)
         arrived[offset] = lax.ppermute(after, "col", pairs)
 
-    out = raw_tiles(
+    out, after = raw_tiles(
         info, out, after, near_last, small, trailing, lambda col: (col ^ 1) * tiles + head_tiles
     )
     half = tiles // 2 if tiles % 2 == 0 else tiles
     mine, got = [], []
-    after = out
     for first in range(0, tiles, half):
         after, *handed = crossed_tiles(info, after, crossed, first, half, small, cols)
         mine.append(after)
@@ -338,10 +338,12 @@
             here = (col_index == high + k) | (col_index == low - k)
             got[-1] = jnp.where(here, piece, got[-1])
 
-    out = raw_tiles(info, out, after, near_first, small, trailing, lambda col: (col ^ 1) * tiles)
+    out, after = raw_tiles(
+        info, out, after, near_first, small, trailing, lambda col: (col ^ 1) * tiles
+    )
     if ends_only:
         far_head = jnp.where((col_index <= low) == even, passed, kept)
-        out = raw_tiles(
+        out, after = raw_tiles(
             info, out, after, far_head, small, trailing,
             lambda col: jnp.where(col <= low, (cols - 1) * tiles, 0),
         )

time: 158 us -> 153 us (0.968)
  Pallas kernels: 42.5 us -> 36.3 us
  local copies, waits for them, and re-layouts: 15 us -> 9.57 us
  waiting for transfers between devices: 68.5 us -> 73.2 us
  starting transfers between devices: 25.1 us -> 27.9 us
    ppermute x1, waiting for transfers between devices: 19.1 us -> 49.6 us  [shards(): near_last = lax.ppermute(gate(rest, [kept, near_first]), 'col', beside)]
    ppermute x2, waiting for transfers between devices: 30.8 us -> 2.94 us  [shards(): arrived[offset] = lax.ppermute(after, 'col', pairs)]
    unnamed x21 -> x11, local copies, waits for them, and re-layouts: 13.3 us -> 5.76 us
    pallas_call x11 -> x12, Pallas kernels: 36.3 us -> 30.1 us  [the longest x3 10.2 us: raw_tiles(): call(raw_body, (steps,), [ANYWHERE, ANYWHERE, tiles_at(raw, step, lambda...]
    ppermute x1, waiting for transfers between devices: 0.01 us -> 4.97 us  [shards(): passed = lax.ppermute(kept, 'col', inside)]
    ppermute x1, waiting for transfers between devices: 5.42 us -> 1.83 us  [spread_ends(): arrived = lax.ppermute(kept, 'col', pairs)]
    slice x0 -> x1, local copies, waits for them, and re-layouts: none -> 2.14 us  [shards(): rest = panel_cols[head_tiles:]]
  transfers between devices with their start and end apart: 13 -> 13, of which waited for: 10 -> 9; matrix products, arithmetic and copies ran while one was open for 4% -> 5% of each run, Pallas kernels for 26% -> 23%
where the time goes in v6:
time: 153 us; the launch traced here: 151 us
  waiting for transfers between devices  73.2 us (48%)
  Pallas kernels  36.3 us (24%)
  starting transfers between devices  27.9 us (18%)
  local copies, waits for them, and re-layouts  9.57 us (6%)
  other arithmetic  3.85 us (3%)
    ppermute x1, waiting for transfers between devices, shards(): near_last = lax.ppermute(gate(rest, [kept, near_first]), 'col', beside)  49.6 us
    pallas_call x3, Pallas kernels, raw_tiles(): call(raw_body, (steps,), [ANYWHERE, ANYWHERE, tiles_at(raw, step, lambda...  10.2 us
    ppermute x3, starting transfers between devices, spread_across(): same.append(lax.ppermute(head, 'row', [(r, r ^ offset) for r in wanted]))  8.06 us
    pallas_call x2, Pallas kernels, crossed_tiles(): call(functools.partial(crossed_body, cols), (steps,), [ANYWHERE, tiles_at...  7.5 us
    pallas_call x4, Pallas kernels, update(): call(functools.partial(update_body, which), (steps,), [ANYWHERE, spot] +...  6.31 us
    ppermute x2, starting transfers between devices, shards(): arrived[offset] = lax.ppermute(after, 'col', pairs)  6.06 us
    ppermute x3, waiting for transfers between devices, spread_across(): same.append(lax.ppermute(head, 'row', [(r, r ^ offset) for r in wanted]))  5.79 us
    unnamed x11, local copies, waits for them, and re-layouts  5.76 us
  transfers between devices with their start and end apart: 13, of which 9 were waited for; matrix products, arithmetic and copies ran while one was open for 5% of the time, Pallas kernels for 23%

profile of v6, /device:TPU:4, one launch (start us, length us, event | category | flops | bytes accessed | tf_op | source)
XLA Modules:
  0.0 151.1 jit_solution(6078576542018667265)
XLA Ops:
  0.0 1.7 %slice.7 = bf16[1,256,512]{2,1,0:T(8,128)(2,1)} slice(bf16[12,256,512]{2,1,0:T(8,128)(2,1)} %panel.1), slice={[0:1], [0:256], [0:512]} | slice | bytes 524288 | tf_op jit(solution)/shard_map/slice | solution.py:291
  1.7 5.2 %collective-permute-start = (bf16[1,256,512]{2,1,0:T(8,128)(2,1)}, bf16[1,256,512]{2,1,0:T(8,128)(2,1)}, u32[]{:S(2)}, u32[]{:S(2)}) collective-permute-start(bf16[1,256,512]{2,1,0:T(8,128)(2,1)} %slice.7), channel_id=1, source_target_pairs={{0,2},{3,1},{4,6},{7,5},{8,10},{11,9},{12,14},{15,13},{16,18},{19,... | collective-permute-start | bytes 786440 | tf_op jit(solution)/shard_map/ppermute | solution.py:258
  6.9 0.0 collective-permute-start.1
  6.9 2.3 %collective-permute-start.8 = (bf16[12,256,512]{2,1,0:T(8,128)(2,1)}, bf16[12,256,512]{2,1,0:T(8,128)(2,1)}, u32[]{:S(2)}, u32[]{:S(2)}) collective-permute-start(bf16[12,256,512]{2,1,0:T(8,128)(2,1)} %panel.1), channel_id=1, source_target_pairs={{1,2},{2,1},{5,6},{6,5},{9,10},{10,9},{13,14},{14,13},{17,18},{18,... | collective-permute-start | bytes 9437192 | tf_op jit(solution)/shard_map/ppermute | solution.py:290
  9.2 2.1 %slice.8.refs_2_.refs_1_ = bf16[11,256,512]{2,1,0:T(8,128)(2,1)S(1)} slice(bf16[12,256,512]{2,1,0:T(8,128)(2,1)} %panel.1), slice={[1:12], [0:256], [0:512]} | slice | bytes 5767168 | tf_op jit(solution)/shard_map/slice | solution.py:293
  11.3 1.8 %collective-permute-done = bf16[1,256,512]{2,1,0:T(8,128)(2,1)} collective-permute-done((bf16[1,256,512]{2,1,0:T(8,128)(2,1)}, bf16[1,256,512]{2,1,0:T(8,128)(2,1)}, u32[]{:S(2)}, u32[]{:S(2)}) %collective-permute-start) | collective-permute-done | bytes 262176 | tf_op jit(solution)/shard_map/ppermute | solution.py:258
  13.2 1.0 broadcast_select_fusion.2.refs_1_
  14.2 0.5 shard_map.37.refs_2_
  14.7 1.3 collective-permute-start.2
  16.0 1.6 %collective-permute-done.1.refs_3_.raw = bf16[1,256,512]{2,1,0:T(8,128)(2,1)S(1)} collective-permute-done((bf16[1,256,512]{2,1,0:T(8,128)(2,1)}, bf16[1,256,512]{2,1,0:T(8,128)(2,1)S(1)}, u32[]{:S(2)}, u32[]{:S(2)}) %collective-permute-start.1) | collective-permute-done | bytes 262176 | tf_op jit(solution)/shard_map/ppermute | solution.py:292
  17.6 0.5 shard_map.42
  18.2 2.4 %collective-permute-start.7 = (bf16[11,256,512]{2,1,0:T(8,128)(2,1)S(1)}, bf16[11,256,512]{2,1,0:T(8,128)(2,1)}, u32[]{:S(2)}, u32[]{:S(2)}) collective-permute-start(bf16[11,256,512]{2,1,0:T(8,128)(2,1)S(1)} %shard_map.42), channel_id=1, source_target_pairs={{0,1},{1,0},{2,3},{3,2},{4,5},{5,4},{6,7},{7,6},{8,9},{9,8},{10,11... | collective-permute-start | bytes 8650760 | tf_op jit(solution)/shard_map/ppermute | solution.py:296
  20.6 5.0 %collective-permute-done.2 = bf16[1,256,512]{2,1,0:T(8,128)(2,1)} collective-permute-done((bf16[1,256,512]{2,1,0:T(8,128)(2,1)S(1)}, bf16[1,256,512]{2,1,0:T(8,128)(2,1)}, u32[]{:S(2)}, u32[]{:S(2)}) %collective-permute-start.2) | collective-permute-done | bytes 262176 | tf_op jit(solution)/shard_map/ppermute | solution.py:295
  25.6 1.7 %broadcast_select_fusion = (bf16[1,256,512]{2,1,0:T(8,128)(2,1)}, bf16[1,256,512]{2,1,0:T(8,128)(2,1)S(1)}) fusion(bf16[1,256,512]{2,1,0:T(8,128)(2,1)S(1)} %shard_map.37.refs_2_, pred[]{:T(512)S(6)} %eq.27, bf16[1,256,512]{2,1,0:T(8,128)(2,1)S(1)} %collective-permute-done.1.refs_3_.raw, bf16[1,256,512]{2,1,0:T(8,128)(2,1)} %collective-permute-done.2, ...), kind=kLoop, calls=%fused_computation.1 | loop fusion | flops 393216 | bytes 1310723 | tf_op jit(solution)/shard_map/jit(_where)/select_n | solution.py:345
  27.3 3.4 %collective-permute-start.3 = (bf16[1,256,512]{2,1,0:T(8,128)(2,1)S(1)}, bf16[1,256,512]{2,1,0:T(8,128)(2,1)S(1)}, u32[]{:S(2)}, u32[]{:S(2)}) collective-permute-start(bf16[1,256,512]{2,1,0:T(8,128)(2,1)S(1)} %get-tuple-element.32), channel_id=1, source_target_pairs={{4,12},{8,0},{12,4},{16,24},{20,28},{5,13},{9,1},{13,5},{17,25},{2... | collective-permute-start | bytes 786440 | tf_op jit(solution)/shard_map/ppermute | solution.py:268
  30.7 1.3 collective-permute-start.4
  32.0 3.4 %collective-permute-start.5 = (bf16[1,256,512]{2,1,0:T(8,128)(2,1)S(1)}, bf16[1,256,512]{2,1,0:T(8,128)(2,1)S(1)}, u32[]{:S(2)}, u32[]{:S(2)}) collective-permute-start(bf16[1,256,512]{2,1,0:T(8,128)(2,1)S(1)} %get-tuple-element.32), channel_id=1, source_target_pairs={{4,28},{8,16},{12,20},{16,8},{20,12},{5,29},{9,17},{13,21},{17,9},... | collective-permute-start | bytes 786440 | tf_op jit(solution)/shard_map/ppermute | solution.py:268
  35.4 0.0 collective-permute-done.3
  35.4 0.5 collective-permute-done.4
  35.9 5.3 %collective-permute-done.5 = bf16[1,256,512]{2,1,0:T(8,128)(2,1)S(1)} collective-permute-done((bf16[1,256,512]{2,1,0:T(8,128)(2,1)S(1)}, bf16[1,256,512]{2,1,0:T(8,128)(2,1)S(1)}, u32[]{:S(2)}, u32[]{:S(2)}) %collective-permute-start.5) | collective-permute-done | bytes 262176 | tf_op jit(solution)/shard_map/ppermute | solution.py:268
  41.2 1.1 pad_maximum_fusion.same
  42.3 0.0 collective-permute-start.6
  42.3 1.1 copy.13
  43.4 0.1 pad_add_fusion.info
  43.4 1.8 %collective-permute-done.6.other = bf16[4,1,256,512]{3,2,1,0:T(8,128)(2,1)} collective-permute-done((bf16[4,1,256,512]{3,2,1,0:T(8,128)(2,1)}, bf16[4,1,256,512]{3,2,1,0:T(8,128)(2,1)}, u32[]{:S(2)}, u32[]{:S(2)}) %collective-permute-start.6) | collective-permute-done | bytes 1048608 | tf_op jit(solution)/shard_map/ppermute | solution.py:270
  45.3 3.3 %shard_map.38 = (bf16[256,256]{1,0:T(8,128)(2,1)S(1)}, bf16[4,512,256]{2,1,0:T(8,128)(2,1)S(1)}) custom-call(s32[2]{0:T(128)S(1)} %pad_add_fusion.info, bf16[4,1,256,512]{3,2,1,0:T(8,128)(2,1)} %pad_maximum_fusion.same, bf16[4,1,256,512]{3,2,1,0:T(8,128)(2,1)} %collective-permute-done.6.other, bf16[2,256,256]{2,1,0:T(8,128)(2,1)S(1)} %bitcast.9), custom_call_target="tpu_custom_call" | custom-call | flops 1024 | bytes 1024 | tf_op jit(solution)/shard_map/pallas_call | solution.py:98
  48.6 0.0 copy-start
  48.6 2.8 %copy-done = bf16[48,256,256]{2,1,0:T(8,128)(2,1)S(1)} copy-done((bf16[48,256,256]{2,1,0:T(8,128)(2,1)S(1)}, bf16[48,256,256]{2,1,0:T(8,128)(2,1)}, u32[]{:S(2)}) %copy-start) | copy-done | bytes 6291480
  51.4 0.0 copy-start.1
  51.4 1.9 %copy-done.1 = bf16[12,256,512]{2,1,0:T(8,128)(2,1)S(1)} copy-done((bf16[12,256,512]{2,1,0:T(8,128)(2,1)S(1)}, bf16[12,256,512]{2,1,0:T(8,128)(2,1)}, u32[]{:S(2)}) %copy-start.1) | copy-done | bytes 3145752
  53.3 5.1 %shard_map.39 = (bf16[48,256,256]{2,1,0:T(8,128)(2,1)}, bf16[12,256,512]{2,1,0:T(8,128)(2,1)S(1)}) custom-call(s32[2]{0:T(128)S(1)} %pad_add_fusion.info, bf16[12,256,512]{2,1,0:T(8,128)(2,1)S(1)} %copy-done.1, bf16[2,256,256]{2,1,0:T(8,128)(2,1)S(1)} %bitcast.10, bf16[256,256]{1,0:T(8,128)(2,1)S(1)} %get-tuple-element.18.couple_t, ...), custom_call_target="tpu_custom_call" | custom-call | flops 5000000000 | bytes 1024 | tf_op jit(solution)/shard_map/pallas_call | solution.py:120
  58.3 0.0 slice-start
  58.3 0.0 slice-start.1
  58.3 1.5 shard_map.40.after
  59.8 4.7 %collective-permute-start.9 = (bf16[11,256,256]{2,1,0:T(8,128)(2,1)S(1)}, bf16[11,256,256]{2,1,0:T(8,128)(2,1)S(1)}, u32[]{:S(2)}, u32[]{:S(2)}) collective-permute-start(bf16[11,256,256]{2,1,0:T(8,128)(2,1)S(1)} %shard_map.40.after), channel_id=1, source_target_pairs={{0,3},{3,0},{4,7},{7,4},{8,11},{11,8},{12,15},{15,12},{16,19},{19,... | collective-permute-start | bytes 4325384 | tf_op jit(solution)/shard_map/ppermute | solution.py:322
  64.5 1.5 shard_map.41.after
  66.0 1.4 collective-permute-start.11
  67.3 49.6 %collective-permute-done.7.raw = bf16[11,256,512]{2,1,0:T(8,128)(2,1)} collective-permute-done((bf16[11,256,512]{2,1,0:T(8,128)(2,1)S(1)}, bf16[11,256,512]{2,1,0:T(8,128)(2,1)}, u32[]{:S(2)}, u32[]{:S(2)}) %collective-permute-start.7) | collective-permute-done | bytes 2883616 | tf_op jit(solution)/shard_map/ppermute | solution.py:296
  117.0 0.0 slice-done
  117.0 0.0 slice-done.1
  117.0 6.5 %shard_map.43 = (bf16[48,256,256]{2,1,0:T(8,128)(2,1)}, f32[8,128]{1,0:T(8,128)S(1)}) custom-call(s32[2]{0:T(128)S(1)} %pad_add_fusion.info, bf16[48,256,256]{2,1,0:T(8,128)(2,1)} %get-tuple-element.20.held, bf16[11,256,256]{2,1,0:T(8,128)(2,1)S(1)} %shard_map.41.after, ...), custom_call_target="tpu_custom_call", output_to_operand_aliasing={{0}: (1, {})} | custom-call | flops 1024 | bytes 1024 | tf_op jit(solution)/shard_map/pallas_call | solution.py:168
  123.5 0.0 collective-permute-done.8.raw
  123.5 3.7 %shard_map.44 = (bf16[6,256,256]{2,1,0:T(8,128)(2,1)S(1)}, bf16[6,256,256]{2,1,0:T(8,128)(2,1)S(1)}) custom-call(s32[2]{0:T(128)S(1)} %pad_add_fusion.info, f32[8,128]{1,0:T(8,128)S(1)} %get-tuple-element.23.after, bf16[12,256,512]{2,1,0:T(8,128)(2,1)} %collective-permute-done.8.raw, bf16[2,256,256]{2,1,0:T(8,128)(2,1)S(1)} %bitcast.12, ...), custom_call_target="tpu_custom_call" | custom-call | flops 1024 | bytes 1024 | tf_op jit(solution)/shard_map/pallas_call | solution.py:196
  127.2 1.3 collective-permute-start.10
  128.5 3.8 %shard_map.45 = (bf16[6,256,256]{2,1,0:T(8,128)(2,1)S(1)}, bf16[6,256,256]{2,1,0:T(8,128)(2,1)S(1)}) custom-call(s32[2]{0:T(128)S(1)} %pad_add_fusion.info, bf16[6,256,256]{2,1,0:T(8,128)(2,1)S(1)} %get-tuple-element.24.after.refs_0_, bf16[12,256,512]{2,1,0:T(8,128)(2,1)} %collective-permute-done.8.raw, bf16[2,256,256]{2,1,0:T(8,128)(2,1)S(1)} %bitcast.13, ...), custom_call_target="tpu_custom_call" | custom-call | flops 1024 | bytes 1024 | tf_op jit(solution)/shard_map/pallas_call | solution.py:196
  132.3 1.3 collective-permute-start.12
  133.6 0.0 copy-start.2
  133.6 1.8 %shard_map.46 = (bf16[48,256,256]{2,1,0:T(8,128)(2,1)}, f32[8,128]{1,0:T(8,128)S(1)}) custom-call(s32[2]{0:T(128)S(1)} %pad_add_fusion.info, bf16[48,256,256]{2,1,0:T(8,128)(2,1)} %get-tuple-element.22.held, bf16[6,256,256]{2,1,0:T(8,128)(2,1)S(1)} %get-tuple-element.25.after.refs_0_, ...), custom_call_target="tpu_custom_call", output_to_operand_aliasing={{0}: (1, {})} | custom-call | flops 1024 | bytes 1024 | tf_op jit(solution)/shard_map/pallas_call | solution.py:168
  135.4 0.0 copy-done.2
  135.4 1.8 %shard_map.47 = (bf16[48,256,256]{2,1,0:T(8,128)(2,1)}, f32[8,128]{1,0:T(8,128)}) custom-call(s32[2]{0:T(128)S(1)} %pad_add_fusion.info, bf16[48,256,256]{2,1,0:T(8,128)(2,1)} %get-tuple-element.26.held, f32[8,128]{1,0:T(8,128)S(1)} %get-tuple-element.27.after, bf16[1,256,512]{2,1,0:T(8,128)(2,1)S(1)} %copy-done.2, ...), custom_call_target="tpu_custom_call", output_to_operand_aliasing={{0}: (1, {})} | custom-call | flops 1024 | bytes 1024 | tf_op jit(solution)/shard_map/pallas_call | solution.py:168
  137.3 0.0 collective-permute-done.9.refs_1_
  137.3 1.6 %shard_map.48.held = bf16[48,256,256]{2,1,0:T(8,128)(2,1)} custom-call(s32[2]{0:T(128)S(1)} %pad_add_fusion.info, bf16[48,256,256]{2,1,0:T(8,128)(2,1)} %get-tuple-element.28.held, bf16[48,256,256]{2,1,0:T(8,128)(2,1)S(1)} %bitcast.8, bf16[6,256,256]{2,1,0:T(8,128)(2,1)S(1)} %get-tuple-element.24.after.refs_0_, ...), custom_call_target="tpu_custom_call", output_to_operand_aliasing={{}: (1, {})} | custom-call | flops 1024 | bytes 1024 | tf_op jit(solution)/shard_map/pallas_call | solution.py:229
  138.9 1.6 %shard_map.49.held = bf16[48,256,256]{2,1,0:T(8,128)(2,1)} custom-call(s32[2]{0:T(128)S(1)} %pad_add_fusion.info, bf16[48,256,256]{2,1,0:T(8,128)(2,1)} %shard_map.48.held, bf16[48,256,256]{2,1,0:T(8,128)(2,1)S(1)} %bitcast.8, bf16[6,256,256]{2,1,0:T(8,128)(2,1)S(1)} %get-tuple-element.25.after.refs_0_, ...), custom_call_target="tpu_custom_call", output_to_operand_aliasing={{}: (1, {})} | custom-call | flops 1024 | bytes 1024 | tf_op jit(solution)/shard_map/pallas_call | solution.py:229
  140.5 2.9 %collective-permute-done.11.refs_1_ = bf16[11,256,256]{2,1,0:T(8,128)(2,1)S(1)} collective-permute-done((bf16[11,256,256]{2,1,0:T(8,128)(2,1)S(1)}, bf16[11,256,256]{2,1,0:T(8,128)(2,1)S(1)}, u32[]{:S(2)}, u32[]{:S(2)}) %collective-permute-start.11) | collective-permute-done | bytes 1441824 | tf_op jit(solution)/shard_map/ppermute | solution.py:322
  143.4 0.0 collective-permute-done.10.refs_0_
  143.4 1.6 %shard_map.50.held = bf16[48,256,256]{2,1,0:T(8,128)(2,1)} custom-call(s32[2]{0:T(128)S(1)} %pad_add_fusion.info, bf16[48,256,256]{2,1,0:T(8,128)(2,1)} %shard_map.49.held, bf16[48,256,256]{2,1,0:T(8,128)(2,1)S(1)} %bitcast.8, bf16[6,256,256]{2,1,0:T(8,128)(2,1)S(1)} %collective-permute-done.10.refs_0_, ...), custom_call_target="tpu_custom_call", output_to_operand_aliasing={{}: (1, {})} | custom-call | flops 1024 | bytes 1024 | tf_op jit(solution)/shard_map/pallas_call | solution.py:229
  145.0 4.6 %collective-permute-done.12.refs_0_ = bf16[6,256,256]{2,1,0:T(8,128)(2,1)S(1)} collective-permute-done((bf16[6,256,256]{2,1,0:T(8,128)(2,1)S(1)}, bf16[6,256,256]{2,1,0:T(8,128)(2,1)S(1)}, u32[]{:S(2)}, u32[]{:S(2)}) %collective-permute-start.12) | collective-permute-done | bytes 786464 | tf_op jit(solution)/shard_map/ppermute | solution.py:333
  149.5 1.6 %shard_map.51 = bf16[48,256,256]{2,1,0:T(8,128)(2,1)} custom-call(s32[2]{0:T(128)S(1)} %pad_add_fusion.info, bf16[48,256,256]{2,1,0:T(8,128)(2,1)} %shard_map.50.held, bf16[48,256,256]{2,1,0:T(8,128)(2,1)S(1)} %bitcast.8, bf16[6,256,256]{2,1,0:T(8,128)(2,1)S(1)} %collective-permute-done.12.refs_0_, ...), custom_call_target="tpu_custom_call", output_to_operand_aliasing={{}: (1, {})} | custom-call | flops 1024 | bytes 1024 | tf_op jit(solution)/shard_map/pallas_call | solution.py:229
  (2 shorter events, 0.0 us)
Async XLA Ops:
  1.7 11.5 %collective-permute-start = (bf16[1,256,512]{2,1,0:T(8,128)(2,1)}, bf16[1,256,512]{2,1,0:T(8,128)(2,1)}, u32[]{:S(2)}, u32[]{:S(2)}) collective-permute-start(bf16[1,256,512]{2,1,0:T(8,128)(2,1)} %slice.7), channel_id=1, source_target_pairs={{0,2},{3,1},{4,6},{7,5},{8,10},{11,9},{12,14},{15,13},{16,18},{19,... | collective-permute-start | bytes 786440 | tf_op jit(solution)/shard_map/ppermute | solution.py:258
  6.9 10.8 %collective-permute-start.1 = (bf16[1,256,512]{2,1,0:T(8,128)(2,1)}, bf16[1,256,512]{2,1,0:T(8,128)(2,1)S(1)}, u32[]{:S(2)}, u32[]{:S(2)}) collective-permute-start(bf16[1,256,512]{2,1,0:T(8,128)(2,1)} %slice.7), channel_id=1, source_target_pairs={{0,1},{1,0},{2,3},{3,2},{4,5},{5,4},{6,7},{7,6},{8,9},{9,8},{10,11... | collective-permute-start | bytes 786440 | tf_op jit(solution)/shard_map/ppermute | solution.py:292
  6.9 116.6 %collective-permute-start.8 = (bf16[12,256,512]{2,1,0:T(8,128)(2,1)}, bf16[12,256,512]{2,1,0:T(8,128)(2,1)}, u32[]{:S(2)}, u32[]{:S(2)}) collective-permute-start(bf16[12,256,512]{2,1,0:T(8,128)(2,1)} %panel.1), channel_id=1, source_target_pairs={{1,2},{2,1},{5,6},{6,5},{9,10},{10,9},{13,14},{14,13},{17,18},{18,... | collective-permute-start | bytes 9437192 | tf_op jit(solution)/shard_map/ppermute | solution.py:290
  14.7 10.9 %collective-permute-start.2 = (bf16[1,256,512]{2,1,0:T(8,128)(2,1)S(1)}, bf16[1,256,512]{2,1,0:T(8,128)(2,1)}, u32[]{:S(2)}, u32[]{:S(2)}) collective-permute-start(bf16[1,256,512]{2,1,0:T(8,128)(2,1)S(1)} %shard_map.37.refs_2_), channel_id=1, source_target_pairs={{1,0},{2,3},{5,4},{6,7},{9,8},{10,11},{13,12},{14,15},{17,16},{18,... | collective-permute-start | bytes 786440 | tf_op jit(solution)/shard_map/ppermute | solution.py:295
  18.2 98.8 %collective-permute-start.7 = (bf16[11,256,512]{2,1,0:T(8,128)(2,1)S(1)}, bf16[11,256,512]{2,1,0:T(8,128)(2,1)}, u32[]{:S(2)}, u32[]{:S(2)}) collective-permute-start(bf16[11,256,512]{2,1,0:T(8,128)(2,1)S(1)} %shard_map.42), channel_id=1, source_target_pairs={{0,1},{1,0},{2,3},{3,2},{4,5},{5,4},{6,7},{7,6},{8,9},{9,8},{10,11... | collective-permute-start | bytes 8650760 | tf_op jit(solution)/shard_map/ppermute | solution.py:296
  27.3 8.1 %collective-permute-start.3 = (bf16[1,256,512]{2,1,0:T(8,128)(2,1)S(1)}, bf16[1,256,512]{2,1,0:T(8,128)(2,1)S(1)}, u32[]{:S(2)}, u32[]{:S(2)}) collective-permute-start(bf16[1,256,512]{2,1,0:T(8,128)(2,1)S(1)} %get-tuple-element.32), channel_id=1, source_target_pairs={{4,12},{8,0},{12,4},{16,24},{20,28},{5,13},{9,1},{13,5},{17,25},{2... | collective-permute-start | bytes 786440 | tf_op jit(solution)/shard_map/ppermute | solution.py:268
  30.7 5.2 %collective-permute-start.4 = (bf16[1,256,512]{2,1,0:T(8,128)(2,1)S(1)}, bf16[1,256,512]{2,1,0:T(8,128)(2,1)S(1)}, u32[]{:S(2)}, u32[]{:S(2)}) collective-permute-start(bf16[1,256,512]{2,1,0:T(8,128)(2,1)S(1)} %get-tuple-element.32), channel_id=1, source_target_pairs={{4,20},{8,24},{12,28},{16,0},{20,4},{5,21},{9,25},{13,29},{17,1},{... | collective-permute-start | bytes 786440 | tf_op jit(solution)/shard_map/ppermute | solution.py:268
  32.0 9.2 %collective-permute-start.5 = (bf16[1,256,512]{2,1,0:T(8,128)(2,1)S(1)}, bf16[1,256,512]{2,1,0:T(8,128)(2,1)S(1)}, u32[]{:S(2)}, u32[]{:S(2)}) collective-permute-start(bf16[1,256,512]{2,1,0:T(8,128)(2,1)S(1)} %get-tuple-element.32), channel_id=1, source_target_pairs={{4,28},{8,16},{12,20},{16,8},{20,12},{5,29},{9,17},{13,21},{17,9},... | collective-permute-start | bytes 786440 | tf_op jit(solution)/shard_map/ppermute | solution.py:268
  42.3 3.0 %collective-permute-start.6 = (bf16[4,1,256,512]{3,2,1,0:T(8,128)(2,1)}, bf16[4,1,256,512]{3,2,1,0:T(8,128)(2,1)}, u32[]{:S(2)}, u32[]{:S(2)}) collective-permute-start(bf16[4,1,256,512]{3,2,1,0:T(8,128)(2,1)} %pad_maximum_fusion.same), channel_id=1, source_target_pairs={{0,4},{4,0},{8,12},{12,8},{16,20},{20,16},{24,28},{28,24},{1,5},{5... | collective-permute-start | bytes 3145736 | tf_op jit(solution)/shard_map/ppermute | solution.py:270
  48.6 2.8 %copy-start = (bf16[48,256,256]{2,1,0:T(8,128)(2,1)S(1)}, bf16[48,256,256]{2,1,0:T(8,128)(2,1)}, u32[]{:S(2)}) copy-start(bf16[48,256,256]{2,1,0:T(8,128)(2,1)} %trailing.15) | copy-start | bytes 18874372
  51.4 1.9 %copy-start.1 = (bf16[12,256,512]{2,1,0:T(8,128)(2,1)S(1)}, bf16[12,256,512]{2,1,0:T(8,128)(2,1)}, u32[]{:S(2)}) copy-start(bf16[12,256,512]{2,1,0:T(8,128)(2,1)} %panel.1) | copy-start | bytes 9437188
  58.3 58.6 %slice-start = ((s8[6291456]{0:T(1024)(128)(4,1)}), s8[4194304]{0:T(1024)(128)(4,1)S(1)}, s32[]{:S(2)}) async-start(s8[6291456]{0:T(1024)(128)(4,1)} %bitcast.7), calls=%async_computation | async-start | bytes 8388608
  58.3 58.6 %slice-start.1 = ((s8[6291456]{0:T(1024)(128)(4,1)}), s8[2097152]{0:T(1024)(128)(4,1)S(1)}, s32[]{:S(2)}) async-start(s8[6291456]{0:T(1024)(128)(4,1)} %bitcast.7), calls=%async_computation.1 | async-start | bytes 4194304
  59.8 77.5 %collective-permute-start.9 = (bf16[11,256,256]{2,1,0:T(8,128)(2,1)S(1)}, bf16[11,256,256]{2,1,0:T(8,128)(2,1)S(1)}, u32[]{:S(2)}, u32[]{:S(2)}) collective-permute-start(bf16[11,256,256]{2,1,0:T(8,128)(2,1)S(1)} %shard_map.40.after), channel_id=1, source_target_pairs={{0,3},{3,0},{4,7},{7,4},{8,11},{11,8},{12,15},{15,12},{16,19},{19,... | collective-permute-start | bytes 4325384 | tf_op jit(solution)/shard_map/ppermute | solution.py:322
  66.0 77.4 %collective-permute-start.11 = (bf16[11,256,256]{2,1,0:T(8,128)(2,1)S(1)}, bf16[11,256,256]{2,1,0:T(8,128)(2,1)S(1)}, u32[]{:S(2)}, u32[]{:S(2)}) collective-permute-start(bf16[11,256,256]{2,1,0:T(8,128)(2,1)S(1)} %shard_map.41.after), channel_id=1, source_target_pairs={{0,2},{3,1},{4,6},{7,5},{8,10},{11,9},{12,14},{15,13},{16,18},{19,... | collective-permute-start | bytes 4325384 | tf_op jit(solution)/shard_map/ppermute | solution.py:322
  127.2 16.2 %collective-permute-start.10 = (bf16[6,256,256]{2,1,0:T(8,128)(2,1)S(1)}, bf16[6,256,256]{2,1,0:T(8,128)(2,1)S(1)}, u32[]{:S(2)}, u32[]{:S(2)}) collective-permute-start(bf16[6,256,256]{2,1,0:T(8,128)(2,1)S(1)} %get-tuple-element.29), channel_id=1, source_target_pairs={{2,3},{1,0},{6,7},{5,4},{10,11},{9,8},{14,15},{13,12},{18,19},{17,... | collective-permute-start | bytes 2359304 | tf_op jit(solution)/shard_map/ppermute | solution.py:333
  132.3 17.2 %collective-permute-start.12 = (bf16[6,256,256]{2,1,0:T(8,128)(2,1)S(1)}, bf16[6,256,256]{2,1,0:T(8,128)(2,1)S(1)}, u32[]{:S(2)}, u32[]{:S(2)}) collective-permute-start(bf16[6,256,256]{2,1,0:T(8,128)(2,1)S(1)} %get-tuple-element.30), channel_id=1, source_target_pairs={{2,3},{1,0},{6,7},{5,4},{10,11},{9,8},{14,15},{13,12},{18,19},{17,... | collective-permute-start | bytes 2359304 | tf_op jit(solution)/shard_map/ppermute | solution.py:333
  133.6 1.9 %copy-start.2 = (bf16[1,256,512]{2,1,0:T(8,128)(2,1)S(1)}, bf16[1,256,512]{2,1,0:T(8,128)(2,1)}, u32[]{:S(2)}) copy-start(bf16[1,256,512]{2,1,0:T(8,128)(2,1)} %get-tuple-element.31.raw) | copy-start | bytes 786436

commit v7 on v6

--- a/solution.py
+++ b/solution.py
@@ -8,11 +8,11 @@
 from jax.sharding import PartitionSpec as P
 
 BF16 = jnp.bfloat16
-SMALL_FLOPS, OWN_FLOPS = 1024, 5 * 10**9
+COST = {"own": 2, "keys": 2, "products": 0, "tail": 1, "raw": 5, "crossed": 1, "update": 1, "gate": 0}
 ANYWHERE = pl.BlockSpec(memory_space=pl.ANY)
 
 
-def call(body, grid, in_specs, out_specs, out_shape, held=False, flops=SMALL_FLOPS):
+def call(kind, body, grid, in_specs, out_specs, out_shape, held=False):
     return pl.pallas_call(
         body,
         grid_spec=pltpu.PrefetchScalarGridSpec(
@@ -23,7 +23,9 @@
         compiler_params=pltpu.CompilerParams(
             vmem_limit_bytes=(8 + 3 * lax.axis_size("col")) * 1024 * 1024
         ),
-        cost_estimate=pl.CostEstimate(flops=flops, bytes_accessed=1024, transcendentals=0),
+        cost_estimate=pl.CostEstimate(
+            flops=1024 + int(COST[kind] * 1e9), bytes_accessed=1024, transcendentals=0
+        ),
     )
 
 
@@ -96,6 +98,7 @@
     couple_t = jax.ShapeDtypeStruct((size, size), BF16)
     keys_t = jax.ShapeDtypeStruct((cols, width, size), BF16)
     return call(
+        "keys",
         functools.partial(keys_body, rows),
         (1,),
         [whole(same), whole(other), whole(inverses_t)],
@@ -118,6 +121,7 @@
     rows = tiles_at(panel, step, lambda t, col: at(t))
     mine = tiles_at(trailing, step, lambda t, col: col * tiles + at(t))
     return call(
+        "own",
         own_body,
         (steps,),
         [rows, *map(whole, small), mine],
@@ -126,11 +130,10 @@
             jax.ShapeDtypeStruct(trailing.shape, BF16),
             jax.ShapeDtypeStruct(panel.shape, BF16),
         ],
-        flops=OWN_FLOPS,
     )(info, panel, *small, trailing)
 
 
-def products_body(offset, first, info, after, factored, keys_t, piece):
+def products_body(offset, first, info, after, factored, keys_t, piece, *last):
     del after
     tiles, size, width = factored.shape
     key_t = keys_t[info[1] ^ offset]
@@ -139,18 +142,40 @@
         rows = factored[start:stop].reshape((stop - start) * size, width)
         total = dot(rows, key_t).reshape(stop - start, size, size)
         piece[start - first:stop - first] = total.astype(BF16)
-
-
-def products(info, after, factored, keys_t, offset, first):
+    for array in last:
+        array[...] = piece[tiles - first - array.shape[0]:]
+
+
+def products(info, after, factored, keys_t, offset, first, last=0):
     tiles, size, _ = factored.shape
-    piece = shape_of(tiles - first, size)
-    return call(
+    shapes = [shape_of(count, size) for count in (tiles - first, last) if count]
+    return call(
+        "products",
         functools.partial(products_body, offset, first),
         (1,),
         [ANYWHERE, whole(factored), whole(keys_t)],
+        [whole(shape) for shape in shapes],
+        shapes,
+    )(info, after, factored, keys_t)
+
+
+def tail_body(offset, info, factored, keys_t, piece):
+    count, size, width = factored.shape
+    total = dot(factored[...].reshape(count * size, width), keys_t[info[1] ^ offset(info[1])])
+    piece[...] = total.reshape(count, size, size).astype(BF16)
+
+
+def tail_products(info, factored, keys_t, count, offset):
+    tiles, size, _ = factored.shape
+    piece = shape_of(count, size)
+    return call(
+        "tail",
+        functools.partial(tail_body, offset),
+        (1,),
+        [tiles_at(factored, count, lambda t, col: tiles - count), whole(keys_t)],
         whole(piece),
         piece,
-    )(info, after, factored, keys_t)
+    )(info, factored, keys_t)
 
 
 def raw_body(info, held, after, raw, inverses_t, couple_t, keys_t, trailing, out, done):
@@ -166,6 +191,7 @@
     spot = tiles_at(trailing, step, lambda t, col: place(col) + at(t))
     done = jax.ShapeDtypeStruct((8, 128), jnp.float32)
     return call(
+        "raw",
         raw_body,
         (steps,),
         [
@@ -181,25 +207,35 @@
     )(info, held, after, raw, *small, trailing)
 
 
-def crossed_body(cols, info, after, raw, inverses_t, couple_t, keys_t, *pieces):
+def crossed_body(cols, at, own, info, after, raw, factored, inverses_t, couple_t, keys_t, *pieces):
     del after
+    count, size, width = raw.shape
     left, right = factor_tiles(raw, inverses_t, couple_t)
+    place = pl.ds(at(pl.program_id(0)), count)
     col = info[1]
-    for k in range(cols // 2):
+    for k, piece in enumerate(pieces):
         target = jnp.clip(jnp.where(col < cols // 2, col - k, col + k), 0, cols - 1)
-        pieces[k][...] = times_key(left, right, keys_t[target]).astype(BF16)
-
-
-def crossed_tiles(info, after, raw, first, count, small, cols):
+        piece[place] = times_key(left, right, keys_t[target]).astype(BF16)
+    if own:
+        @pl.when(pl.program_id(0) == 0)
+        def _():
+            total = dot(factored[...].reshape(own * size, width), keys_t[col ^ 1])
+            pieces[1][pieces[1].shape[0] - own:] = total.reshape(own, size, size).astype(BF16)
+
+
+def crossed_tiles(info, after, raw, factored, own, small, cols):
+    count, size, _ = raw.shape
     step, steps, at = steps_of(count)
-    piece = shape_of(count, raw.shape[1])
-    return call(
-        functools.partial(crossed_body, cols),
+    tail = tiles_at(factored, max(own, 1), lambda t, col: factored.shape[0] - max(own, 1))
+    pieces = [shape_of(count + own * (k == 1), size) for k in range(cols // 2)]
+    return call(
+        "crossed",
+        functools.partial(crossed_body, cols, at, own),
         (steps,),
-        [ANYWHERE, tiles_at(raw, step, lambda t, col: first + at(t)), *map(whole, small)],
-        [tiles_at(piece, step, lambda t, col: at(t))] * (cols // 2),
-        [piece] * (cols // 2),
-    )(info, after, raw, *small)
+        [ANYWHERE, tiles_at(raw, step, lambda t, col: at(t)), tail, *map(whole, small)],
+        [whole(piece) for piece in pieces],
+        pieces,
+    )(info, after, raw, factored, *small)
 
 
 def update_body(which, info, held, trailing, *refs):
@@ -211,13 +247,16 @@
             out[...] = subtract(trailing, piece[...].astype(jnp.float32))
 
 
-def update(info, held, trailing, count, pieces, which):
-    step, steps, at = steps_of(count)
-
-    def place(col):
-        spot = pieces[0][2](col)
+def update(info, held, trailing, count, pieces, which, step=None):
+    if step is None:
+        step, steps, at = steps_of(count)
+    else:
+        steps, at = count // step, lambda t: t * step
+
+    def place(t, col):
+        spot = pieces[0][2](col, at(t))
         for i, (_, _, start) in enumerate(pieces[1:], 1):
-            spot = jnp.where(which(col) == i, start(col), spot)
+            spot = jnp.where(which(col) == i, start(col, at(t)), spot)
         return spot
 
     def chosen(i, array, first):
@@ -225,8 +264,9 @@
             array, step, lambda t, col: first + jnp.where(which(col) == i, at(t), 0)
         )
 
-    spot = tiles_at(trailing, step, lambda t, col: place(col) + at(t))
-    return call(
+    spot = tiles_at(trailing, step, place)
+    return call(
+        "update",
         functools.partial(update_body, which),
         (steps,),
         [ANYWHERE, spot] + [chosen(i, array, first) for i, (array, first, _) in enumerate(pieces)],
@@ -238,6 +278,7 @@
 
 def gate(array, waited):
     return call(
+        "gate",
         lambda *refs: None,
         (1,),
         [ANYWHERE] * (1 + len(waited)),
@@ -282,28 +323,9 @@
     low, high = cols // 2 - 1, cols // 2
     info = jnp.stack([lax.axis_index("row"), col_index]).astype(jnp.int32)
     inverses_t = jnp.swapaxes(inverses, 1, 2)
-
-    head_tiles = (cols + 1) // rows + 1
+    swap = [(low, high), (high, low)]
     beside = [(c, c ^ 1) for c in range(cols)]
-    inside = [(c, c ^ 1) for c in range(1, cols - 1)]
-
-    crossed = lax.ppermute(panel_cols, "col", [(low, high), (high, low)])
-    kept = spread_ends(panel_cols[:head_tiles], cols)
-    near_first = lax.ppermute(panel_cols[:head_tiles], "col", beside)
-    rest = panel_cols[head_tiles:]
-    kept = gate(kept, [rest])
-    passed = lax.ppermute(kept, "col", inside)
-    near_last = lax.ppermute(gate(rest, [kept, near_first]), "col", beside)
-    from_end = (col_index == 1) | (col_index == cols - 2)
-    passed = jnp.where(from_end, near_first, passed)
-    even = col_index % 2 == 0
-    head = jnp.where(even, kept, passed)
-
-    wanted = sorted({tile % rows for tile in range(1, cols + 2)})
-    same, other = spread_across(head, wanted, rows)
-    couple_t, keys_t = make_keys(info, same, other, inverses_t, rows, cols)
-    small = (inverses_t, couple_t, keys_t)
-    out, factored = own_tiles(info, panel_cols, small, trailing)
+    inside = beside[1:-1]
 
     sends = {
         offset: [
@@ -314,30 +336,60 @@
         for offset in range(cols - 1, 1, -1)
     }
     ends_only = all(c in (0, cols - 1) for pairs in sends.values() for c, _ in pairs)
+    head_tiles = (cols + 1) // rows + 1
     skipped = head_tiles if ends_only else 0
+    half = tiles // 2 if tiles % 2 == 0 else tiles
+    direct = 2 if ends_only and half > 3 else 0
+    last = tiles - direct
+
+    crossed = lax.ppermute(panel_cols[:last], "col", swap)
+    kept = spread_ends(panel_cols[:head_tiles], cols)
+    near_first = lax.ppermute(panel_cols[:head_tiles], "col", beside)
+    rest = panel_cols[head_tiles:last]
+    kept = gate(kept, [rest])
+    passed = lax.ppermute(kept, "col", inside)
+    near_rest = lax.ppermute(gate(rest, [kept, near_first]), "col", beside)
+    from_end = (col_index == 1) | (col_index == cols - 2)
+    passed = jnp.where(from_end, near_first, passed)
+    even = col_index % 2 == 0
+    head = jnp.where(even, kept, passed)
+
+    wanted = sorted({tile % rows for tile in range(1, cols + 2)})
+    same, other = spread_across(head, wanted, rows)
+    couple_t, keys_t = make_keys(info, same, other, inverses_t, rows, cols)
+    small = (inverses_t, couple_t, keys_t)
+    out, factored = own_tiles(info, panel_cols, small, trailing)
+
+    def inner(col):
+        return (col == low) | (col == high)
+
+    after = factored
+    if direct:
+        after = tail_products(
+            info, factored, keys_t, direct, lambda col: jnp.where(inner(col), 2, 1)
+        )
+        last_round = lax.ppermute(after, "col", [(0, 1), (1, 3), (3, 2), (2, 0)])
     arrived = {}
-    after = factored
     for offset, pairs in sends.items():
-        after = products(info, after, factored, keys_t, offset, skipped)
+        straight = direct if offset == high ^ low else 0
+        after, *last_swap = products(info, after, factored, keys_t, offset, skipped, straight)
         arrived[offset] = lax.ppermute(after, "col", pairs)
+        if straight:
+            last_crossed = lax.ppermute(last_swap[0], "col", swap)
+
+    after, *handed = crossed_tiles(info, after, crossed, factored, direct, small, cols)
+    mine = after
+    handed = [
+        lax.ppermute(piece, "col", [(high, high + k), (low, low - k)])
+        for k, piece in enumerate(handed, 1)
+    ]
+    got = handed[0]
+    for k, piece in enumerate(handed[1:], 2):
+        got = jnp.where((col_index == high + k) | (col_index == low - k), piece, got)
 
     out, after = raw_tiles(
-        info, out, after, near_last, small, trailing, lambda col: (col ^ 1) * tiles + head_tiles
+        info, out, after, near_rest, small, trailing, lambda col: (col ^ 1) * tiles + head_tiles
     )
-    half = tiles // 2 if tiles % 2 == 0 else tiles
-    mine, got = [], []
-    for first in range(0, tiles, half):
-        after, *handed = crossed_tiles(info, after, crossed, first, half, small, cols)
-        mine.append(after)
-        handed = [
-            lax.ppermute(piece, "col", [(high, high + k), (low, low - k)])
-            for k, piece in enumerate(handed, 1)
-        ]
-        got.append(handed[0])
-        for k, piece in enumerate(handed[1:], 2):
-            here = (col_index == high + k) | (col_index == low - k)
-            got[-1] = jnp.where(here, piece, got[-1])
-
     out, after = raw_tiles(
         info, out, after, near_first, small, trailing, lambda col: (col ^ 1) * tiles
     )
@@ -351,15 +403,17 @@
     def far_offset(col, slot=2):
         return slot + ((col ^ special_source(col, cols)) <= slot)
 
-    def inner(col):
-        return (col == low) | (col == high)
-
     def special(array, i):
-        return array, 0, lambda col: special_source(col, cols) * tiles + i * half
+        start = min(i * half, array.shape[0] - half)
+        return array, start, lambda col, tile: (
+            special_source(col, cols) * tiles + start + tile
+        )
 
     def far(offset, i):
-        first = min(i * half, tiles - skipped - half)
-        return arrived[offset], first, lambda col: (col ^ offset) * tiles + skipped + first
+        start = min(i * half, tiles - skipped - half)
+        return arrived[offset], start, lambda col, tile: (
+            (col ^ offset) * tiles + skipped + start + tile
+        )
 
     for slot in range(3, cols - 1):
         for i in range(tiles // half):
@@ -371,13 +425,29 @@
     for i in range(tiles // half):
         out = update(
             info, out, trailing, half,
-            [special(mine[i], i)] + [far(offset, i) for offset in outer_far],
+            [special(mine, i)] + [far(offset, i) for offset in outer_far],
             lambda col: jnp.where(inner(col), 0, far_offset(col) - outer_far[0] + 1),
         )
+    if direct:
+        def round_place(col, tile):
+            return jnp.where(inner(col), col ^ 1, special_source(col, cols)) * tiles + last + tile
+
+        out = update(info, out, trailing, direct, [(last_round, 0, round_place)], lambda col: 0)
+        crossed_place = lambda col, tile: special_source(col, cols) * tiles + last + tile
+        out = update(
+            info, out, trailing, direct,
+            [(last_crossed, 0, crossed_place), (last_round, 0, round_place)],
+            lambda col: jnp.where(inner(col), 0, 1),
+        )
     for i in range(tiles // half):
+        array, start, usual = special(got, i)
+
+        def place(col, tile, start=start, usual=usual):
+            return jnp.where(start + tile < last, usual(col, tile), (col ^ 1) * tiles + start + tile)
+
         out = update(
-            info, out, trailing, half, [special(got[i], i), far(2, i)],
-            lambda col: jnp.where(inner(col), 1, 0),
+            info, out, trailing, half, [(array, start, place), far(2, i)],
+            lambda col: jnp.where(inner(col), 1, 0), direct if i else None,
         )
     return out
 

time: 153 us -> 151 us (0.987)
  waiting for transfers between devices: 73.2 us -> 61.9 us
  starting transfers between devices: 27.9 us -> 34.6 us
  Pallas kernels: 36.3 us -> 38.9 us
    ppermute x2, starting transfers between devices: 6.06 us -> 15.2 us  [shards(): arrived[offset] = lax.ppermute(after, 'col', pairs)]
    ppermute x2 -> x4, waiting for transfers between devices: 49.6 us -> 44.2 us  [the longest x1 31.1 us: shards(): near_rest = lax.ppermute(gate(rest, [kept, near_first]), 'col', beside)]
    ppermute x2, waiting for transfers between devices: 2.94 us -> 0.01 us  [shards(): arrived[offset] = lax.ppermute(after, 'col', pairs)]
    ppermute x2 -> x1, waiting for transfers between devices: 4.56 us -> 1.64 us  [shards(): lax.ppermute(piece, 'col', [(high, high + k), (low, low - k)])]
    slice x1 -> x2, local copies, waits for them, and re-layouts: 2.14 us -> 5.05 us  [the longest x1 3.41 us: shards(): crossed = lax.ppermute(panel_cols[:last], 'col', swap)]
    pallas_call x15 -> x17, Pallas kernels: 36.3 us -> 38.9 us  [the longest x3 10.4 us: raw_tiles(): call('raw', raw_body, (steps,), [ANYWHERE, ANYWHERE, tiles_at(raw, step,...]
    ppermute x3, starting transfers between devices: 8.06 us -> 5.94 us  [spread_across(): same.append(lax.ppermute(head, 'row', [(r, r ^ offset) for r in wanted]))]
    unnamed x11, local copies, waits for them, and re-layouts: 5.76 us -> 3.88 us
  transfers between devices with their start and end apart: 13 -> 14, of which waited for: 9 -> 8; matrix products, arithmetic and copies ran while one was open for 5% -> 6% of each run, Pallas kernels for 23% -> 24%
where the time goes in v7:
time: 151 us; the launch traced here: 149 us
  waiting for transfers between devices  61.9 us (41%)
  Pallas kernels  38.9 us (26%)
  starting transfers between devices  34.6 us (23%)
  local copies, waits for them, and re-layouts  10.8 us (7%)
  other arithmetic  2.91 us (2%)
    ppermute x1, waiting for transfers between devices, shards(): near_rest = lax.ppermute(gate(rest, [kept, near_first]), 'col', beside)  31.1 us
    ppermute x2, starting transfers between devices, shards(): arrived[offset] = lax.ppermute(after, 'col', pairs)  15.2 us
    ppermute x1, waiting for transfers between devices, shards(): last_round = lax.ppermute(after, 'col', [(0, 1), (1, 3), (3, 2), (2, 0)])  13.1 us
    pallas_call x3, Pallas kernels, raw_tiles(): call('raw', raw_body, (steps,), [ANYWHERE, ANYWHERE, tiles_at(raw, step,...  10.4 us
    pallas_call x6, Pallas kernels, update(): call('update', functools.partial(update_body, which), (steps,), [ANYWHERE...  9.57 us
    ppermute x3, waiting for transfers between devices, spread_across(): same.append(lax.ppermute(head, 'row', [(r, r ^ offset) for r in wanted]))  6.86 us
    ppermute x3, starting transfers between devices, spread_across(): same.append(lax.ppermute(head, 'row', [(r, r ^ offset) for r in wanted]))  5.94 us
    pallas_call x1, Pallas kernels, crossed_tiles(): call('crossed', functools.partial(crossed_body, cols, at, own), (steps,),...  5.81 us
  transfers between devices with their start and end apart: 14, of which 8 were waited for; matrix products, arithmetic and copies ran while one was open for 6% of the time, Pallas kernels for 24%

profile of v7, /device:TPU:4, one launch (start us, length us, event | category | flops | bytes accessed | tf_op | source)
XLA Modules:
  0.0 149.3 jit_solution(13560021304082347797)
XLA Ops:
  0.0 0.0 copy-start.1
  0.0 1.8 %slice.10 = bf16[1,256,512]{2,1,0:T(8,128)(2,1)} slice(bf16[12,256,512]{2,1,0:T(8,128)(2,1)} %panel.1), slice={[0:1], [0:256], [0:512]} | slice | bytes 524288 | tf_op jit(solution)/shard_map/slice | solution.py:346
  1.8 5.2 %collective-permute-start = (bf16[1,256,512]{2,1,0:T(8,128)(2,1)}, bf16[1,256,512]{2,1,0:T(8,128)(2,1)}, u32[]{:S(2)}, u32[]{:S(2)}) collective-permute-start(bf16[1,256,512]{2,1,0:T(8,128)(2,1)} %slice.10), channel_id=1, source_target_pairs={{0,2},{3,1},{4,6},{7,5},{8,10},{11,9},{12,14},{15,13},{16,18},{19,... | collective-permute-start | bytes 786440 | tf_op jit(solution)/shard_map/ppermute | solution.py:299
  7.0 0.0 collective-permute-start.1
  7.0 3.4 %slice.12 = bf16[10,256,512]{2,1,0:T(8,128)(2,1)} slice(bf16[12,256,512]{2,1,0:T(8,128)(2,1)} %panel.1), slice={[0:10], [0:256], [0:512]} | slice | bytes 5242880 | tf_op jit(solution)/shard_map/slice | solution.py:345
  10.5 2.2 %collective-permute-start.7 = (bf16[10,256,512]{2,1,0:T(8,128)(2,1)}, bf16[10,256,512]{2,1,0:T(8,128)(2,1)}, u32[]{:S(2)}, u32[]{:S(2)}) collective-permute-start(bf16[10,256,512]{2,1,0:T(8,128)(2,1)} %slice.12), channel_id=1, source_target_pairs={{1,2},{2,1},{5,6},{6,5},{9,10},{10,9},{13,14},{14,13},{17,18},{18,... | collective-permute-start | bytes 7864328 | tf_op jit(solution)/shard_map/ppermute | solution.py:345
  12.7 0.0 copy-done.1
  12.7 1.6 %slice.11.refs_2_.refs_1_ = bf16[9,256,512]{2,1,0:T(8,128)(2,1)} slice(bf16[12,256,512]{2,1,0:T(8,128)(2,1)S(1)} %copy-done.1), slice={[1:10], [0:256], [0:512]} | slice | bytes 4718592 | tf_op jit(solution)/shard_map/slice | solution.py:348
  14.3 0.0 collective-permute-done
  14.4 0.5 shard_map.37.refs_2_
  14.9 1.3 collective-permute-start.2
  16.2 1.6 %collective-permute-done.1.refs_3_.raw = bf16[1,256,512]{2,1,0:T(8,128)(2,1)} collective-permute-done((bf16[1,256,512]{2,1,0:T(8,128)(2,1)}, bf16[1,256,512]{2,1,0:T(8,128)(2,1)}, u32[]{:S(2)}, u32[]{:S(2)}) %collective-permute-start.1) | collective-permute-done | bytes 262176 | tf_op jit(solution)/shard_map/ppermute | solution.py:347
  17.8 0.5 shard_map.44
  18.3 2.5 %collective-permute-start.8 = (bf16[9,256,512]{2,1,0:T(8,128)(2,1)}, bf16[9,256,512]{2,1,0:T(8,128)(2,1)}, u32[]{:S(2)}, u32[]{:S(2)}) collective-permute-start(bf16[9,256,512]{2,1,0:T(8,128)(2,1)} %shard_map.44), channel_id=1, source_target_pairs={{0,1},{1,0},{2,3},{3,2},{4,5},{5,4},{6,7},{7,6},{8,9},{9,8},{10,11... | collective-permute-start | bytes 7077896 | tf_op jit(solution)/shard_map/ppermute | solution.py:351
  20.9 5.8 %collective-permute-done.2 = bf16[1,256,512]{2,1,0:T(8,128)(2,1)} collective-permute-done((bf16[1,256,512]{2,1,0:T(8,128)(2,1)S(1)}, bf16[1,256,512]{2,1,0:T(8,128)(2,1)}, u32[]{:S(2)}, u32[]{:S(2)}) %collective-permute-start.2) | collective-permute-done | bytes 262176 | tf_op jit(solution)/shard_map/ppermute | solution.py:350
  26.6 1.7 %broadcast_select_fusion = (bf16[1,256,512]{2,1,0:T(8,128)(2,1)}, bf16[1,256,512]{2,1,0:T(8,128)(2,1)S(1)}) fusion(bf16[1,256,512]{2,1,0:T(8,128)(2,1)S(1)} %shard_map.37.refs_2_, pred[]{:T(512)S(6)} %eq.27, bf16[1,256,512]{2,1,0:T(8,128)(2,1)} %collective-permute-done.1.refs_3_.raw, bf16[1,256,512]{2,1,0:T(8,128)(2,1)} %collective-permute-done.2, ...), kind=kLoop, calls=%fused_computation.1 | loop fusion | flops 393216 | bytes 1310723 | tf_op jit(solution)/shard_map/jit(_where)/select_n | solution.py:397
  28.3 3.3 %collective-permute-start.5 = (bf16[1,256,512]{2,1,0:T(8,128)(2,1)S(1)}, bf16[1,256,512]{2,1,0:T(8,128)(2,1)S(1)}, u32[]{:S(2)}, u32[]{:S(2)}) collective-permute-start(bf16[1,256,512]{2,1,0:T(8,128)(2,1)S(1)} %get-tuple-element.32), channel_id=1, source_target_pairs={{4,28},{8,16},{12,20},{16,8},{20,12},{5,29},{9,17},{13,21},{17,9},... | collective-permute-start | bytes 786440 | tf_op jit(solution)/shard_map/ppermute | solution.py:309
  31.7 1.3 collective-permute-start.4
  33.0 1.3 collective-permute-start.3
  34.3 5.1 %collective-permute-done.5 = bf16[1,256,512]{2,1,0:T(8,128)(2,1)S(1)} collective-permute-done((bf16[1,256,512]{2,1,0:T(8,128)(2,1)S(1)}, bf16[1,256,512]{2,1,0:T(8,128)(2,1)S(1)}, u32[]{:S(2)}, u32[]{:S(2)}) %collective-permute-start.5) | collective-permute-done | bytes 262176 | tf_op jit(solution)/shard_map/ppermute | solution.py:309
  39.4 0.0 collective-permute-done.4
  39.4 1.7 %collective-permute-done.3 = bf16[1,256,512]{2,1,0:T(8,128)(2,1)S(1)} collective-permute-done((bf16[1,256,512]{2,1,0:T(8,128)(2,1)S(1)}, bf16[1,256,512]{2,1,0:T(8,128)(2,1)S(1)}, u32[]{:S(2)}, u32[]{:S(2)}) %collective-permute-start.3) | collective-permute-done | bytes 262176 | tf_op jit(solution)/shard_map/ppermute | solution.py:309
  41.2 1.1 pad_maximum_fusion.same
  42.3 0.0 collective-permute-start.6
  42.3 1.1 copy.15
  43.4 0.1 pad_add_fusion.info
  43.4 1.8 %collective-permute-done.6.other = bf16[4,1,256,512]{3,2,1,0:T(8,128)(2,1)} collective-permute-done((bf16[4,1,256,512]{3,2,1,0:T(8,128)(2,1)}, bf16[4,1,256,512]{3,2,1,0:T(8,128)(2,1)}, u32[]{:S(2)}, u32[]{:S(2)}) %collective-permute-start.6) | collective-permute-done | bytes 1048608 | tf_op jit(solution)/shard_map/ppermute | solution.py:311
  45.3 3.3 %shard_map.38 = (bf16[256,256]{1,0:T(8,128)(2,1)S(1)}, bf16[4,512,256]{2,1,0:T(8,128)(2,1)S(1)}) custom-call(s32[2]{0:T(128)S(1)} %pad_add_fusion.info, bf16[4,1,256,512]{3,2,1,0:T(8,128)(2,1)} %pad_maximum_fusion.same, bf16[4,1,256,512]{3,2,1,0:T(8,128)(2,1)} %collective-permute-done.6.other, bf16[2,256,256]{2,1,0:T(8,128)(2,1)S(1)} %bitcast.9), custom_call_target="tpu_custom_call" | custom-call | flops 2000001024 | bytes 1024 | tf_op jit(solution)/shard_map/pallas_call | solution.py:100
  48.6 0.0 copy-start
  48.6 2.8 %copy-done = bf16[48,256,256]{2,1,0:T(8,128)(2,1)S(1)} copy-done((bf16[48,256,256]{2,1,0:T(8,128)(2,1)S(1)}, bf16[48,256,256]{2,1,0:T(8,128)(2,1)}, u32[]{:S(2)}) %copy-start) | copy-done | bytes 6291480
  51.4 5.1 %shard_map.39 = (bf16[48,256,256]{2,1,0:T(8,128)(2,1)}, bf16[12,256,512]{2,1,0:T(8,128)(2,1)S(1)}) custom-call(s32[2]{0:T(128)S(1)} %pad_add_fusion.info, bf16[12,256,512]{2,1,0:T(8,128)(2,1)S(1)} %copy-done.1, bf16[2,256,256]{2,1,0:T(8,128)(2,1)S(1)} %bitcast.10, bf16[256,256]{1,0:T(8,128)(2,1)S(1)} %get-tuple-element.18.couple_t, ...), custom_call_target="tpu_custom_call" | custom-call | flops 2000001024 | bytes 1024 | tf_op jit(solution)/shard_map/pallas_call | solution.py:123
  56.4 0.8 shard_map.40.after
  57.3 0.1 collective-permute-start.10
  57.4 1.5 shard_map.41
  58.8 0.0 slice-start
  58.8 1.5 shard_map.42.after
  60.3 4.4 %collective-permute-start.9 = (bf16[11,256,256]{2,1,0:T(8,128)(2,1)S(1)}, bf16[11,256,256]{2,1,0:T(8,128)(2,1)S(1)}, u32[]{:S(2)}, u32[]{:S(2)}) collective-permute-start(bf16[11,256,256]{2,1,0:T(8,128)(2,1)S(1)} %get-tuple-element.22.after), channel_id=1, source_target_pairs={{0,3},{3,0},{4,7},{7,4},{8,11},{11,8},{12,15},{15,12},{16,19},{19,... | collective-permute-start | bytes 4325384 | tf_op jit(solution)/shard_map/ppermute | solution.py:376
  64.7 0.0 slice-start.1
  64.7 0.8 collective-permute-start.11
  65.5 0.0 collective-permute-done.7.raw
  65.5 10.8 %collective-permute-start.13 = (bf16[11,256,256]{2,1,0:T(8,128)(2,1)S(1)}, bf16[11,256,256]{2,1,0:T(8,128)(2,1)S(1)}, u32[]{:S(2)}, u32[]{:S(2)}) collective-permute-start(bf16[11,256,256]{2,1,0:T(8,128)(2,1)S(1)} %shard_map.42.after), channel_id=1, source_target_pairs={{0,2},{3,1},{4,6},{7,5},{8,10},{11,9},{12,14},{15,13},{16,18},{19,... | collective-permute-start | bytes 4325384 | tf_op jit(solution)/shard_map/ppermute | solution.py:376
  76.4 5.8 %shard_map.43 = (bf16[10,256,256]{2,1,0:T(8,128)(2,1)S(1)}, bf16[12,256,256]{2,1,0:T(8,128)(2,1)S(1)}) custom-call(s32[2]{0:T(128)S(1)} %pad_add_fusion.info, bf16[11,256,256]{2,1,0:T(8,128)(2,1)S(1)} %shard_map.42.after, bf16[10,256,512]{2,1,0:T(8,128)(2,1)} %collective-permute-done.7.raw, bf16[12,256,512]{2,1,0:T(8,128)(2,1)S(1)} %get-tuple-element.21.factored, ...), custom_call_target="tpu_custom_call" | custom-call | flops 1000001024 | bytes 1024 | tf_op jit(solution)/shard_map/pallas_call | solution.py:231
  82.2 31.1 %collective-permute-done.8.raw = bf16[9,256,512]{2,1,0:T(8,128)(2,1)} collective-permute-done((bf16[9,256,512]{2,1,0:T(8,128)(2,1)}, bf16[9,256,512]{2,1,0:T(8,128)(2,1)}, u32[]{:S(2)}, u32[]{:S(2)}) %collective-permute-start.8) | collective-permute-done | bytes 2359328 | tf_op jit(solution)/shard_map/ppermute | solution.py:351
  113.3 1.3 collective-permute-start.12
  114.6 0.0 slice-done
  114.6 0.0 slice-done.1
  114.6 5.7 %shard_map.45 = (bf16[48,256,256]{2,1,0:T(8,128)(2,1)}, f32[8,128]{1,0:T(8,128)S(1)}) custom-call(s32[2]{0:T(128)S(1)} %pad_add_fusion.info, bf16[48,256,256]{2,1,0:T(8,128)(2,1)} %get-tuple-element.20.held, bf16[10,256,256]{2,1,0:T(8,128)(2,1)S(1)} %get-tuple-element.23.after.refs_0_, ...), custom_call_target="tpu_custom_call", output_to_operand_aliasing={{0}: (1, {})} | custom-call | flops 5000001024 | bytes 1024 | tf_op jit(solution)/shard_map/pallas_call | solution.py:193
  120.4 0.0 copy-start.2
  120.4 2.8 %shard_map.46 = (bf16[48,256,256]{2,1,0:T(8,128)(2,1)}, f32[8,128]{1,0:T(8,128)S(1)}) custom-call(s32[2]{0:T(128)S(1)} %pad_add_fusion.info, bf16[48,256,256]{2,1,0:T(8,128)(2,1)} %get-tuple-element.24.held, f32[8,128]{1,0:T(8,128)S(1)} %get-tuple-element.25.after, ...), custom_call_target="tpu_custom_call", output_to_operand_aliasing={{0}: (1, {})} | custom-call | flops 5000001024 | bytes 1024 | tf_op jit(solution)/shard_map/pallas_call | solution.py:193
  123.2 0.0 copy-done.2
  123.2 1.8 %shard_map.47 = (bf16[48,256,256]{2,1,0:T(8,128)(2,1)}, f32[8,128]{1,0:T(8,128)}) custom-call(s32[2]{0:T(128)S(1)} %pad_add_fusion.info, bf16[48,256,256]{2,1,0:T(8,128)(2,1)} %get-tuple-element.26.held, f32[8,128]{1,0:T(8,128)S(1)} %get-tuple-element.27.after, bf16[1,256,512]{2,1,0:T(8,128)(2,1)S(1)} %copy-done.2, ...), custom_call_target="tpu_custom_call", output_to_operand_aliasing={{0}: (1, {})} | custom-call | flops 5000001024 | bytes 1024 | tf_op jit(solution)/shard_map/pallas_call | solution.py:193
  125.0 0.0 collective-permute-done.9.refs_1_
  125.0 1.6 %shard_map.48.held = bf16[48,256,256]{2,1,0:T(8,128)(2,1)} custom-call(s32[2]{0:T(128)S(1)} %pad_add_fusion.info, bf16[48,256,256]{2,1,0:T(8,128)(2,1)} %get-tuple-element.28.held, bf16[48,256,256]{2,1,0:T(8,128)(2,1)S(1)} %bitcast.8, bf16[10,256,256]{2,1,0:T(8,128)(2,1)S(1)} %get-tuple-element.23.after.refs_0_, ...), custom_call_target="tpu_custom_call", output_to_operand_aliasing={{}: (1, {})} | custom-call | flops 1000001024 | bytes 1024 | tf_op jit(solution)/shard_map/pallas_call | solution.py:268
  126.6 1.6 %shard_map.49.held = bf16[48,256,256]{2,1,0:T(8,128)(2,1)} custom-call(s32[2]{0:T(128)S(1)} %pad_add_fusion.info, bf16[48,256,256]{2,1,0:T(8,128)(2,1)} %shard_map.48.held, bf16[48,256,256]{2,1,0:T(8,128)(2,1)S(1)} %bitcast.8, bf16[10,256,256]{2,1,0:T(8,128)(2,1)S(1)} %get-tuple-element.23.after.refs_0_, ...), custom_call_target="tpu_custom_call", output_to_operand_aliasing={{}: (1, {})} | custom-call | flops 1000001024 | bytes 1024 | tf_op jit(solution)/shard_map/pallas_call | solution.py:268
  128.2 13.1 %collective-permute-done.10.refs_0_.refs_1_ = bf16[2,256,256]{2,1,0:T(8,128)(2,1)S(1)} collective-permute-done((bf16[2,256,256]{2,1,0:T(8,128)(2,1)S(1)}, bf16[2,256,256]{2,1,0:T(8,128)(2,1)S(1)}, u32[]{:S(2)}, u32[]{:S(2)}) %collective-permute-start.10) | collective-permute-done | bytes 262176 | tf_op jit(solution)/shard_map/ppermute | solution.py:371
  141.3 1.3 shard_map.50.held
  142.6 0.0 collective-permute-done.11.refs_0_
  142.6 1.3 shard_map.51.held
  143.9 0.0 collective-permute-done.13.refs_1_
  143.9 1.6 %collective-permute-done.12.refs_0_ = bf16[12,256,256]{2,1,0:T(8,128)(2,1)S(1)} collective-permute-done((bf16[12,256,256]{2,1,0:T(8,128)(2,1)S(1)}, bf16[12,256,256]{2,1,0:T(8,128)(2,1)S(1)}, u32[]{:S(2)}, u32[]{:S(2)}) %collective-permute-start.12) | collective-permute-done | bytes 1572896 | tf_op jit(solution)/shard_map/ppermute | solution.py:383
  145.6 1.6 %shard_map.52.held = bf16[48,256,256]{2,1,0:T(8,128)(2,1)} custom-call(s32[2]{0:T(128)S(1)} %pad_add_fusion.info, bf16[48,256,256]{2,1,0:T(8,128)(2,1)} %shard_map.51.held, bf16[48,256,256]{2,1,0:T(8,128)(2,1)S(1)} %bitcast.8, bf16[12,256,256]{2,1,0:T(8,128)(2,1)S(1)} %collective-permute-done.12.refs_0_, ...), custom_call_target="tpu_custom_call", output_to_operand_aliasing={{}: (1, {})} | custom-call | flops 1000001024 | bytes 1024 | tf_op jit(solution)/shard_map/pallas_call | solution.py:268
  147.1 2.1 %shard_map.53 = bf16[48,256,256]{2,1,0:T(8,128)(2,1)} custom-call(s32[2]{0:T(128)S(1)} %pad_add_fusion.info, bf16[48,256,256]{2,1,0:T(8,128)(2,1)} %shard_map.52.held, bf16[48,256,256]{2,1,0:T(8,128)(2,1)S(1)} %bitcast.8, bf16[12,256,256]{2,1,0:T(8,128)(2,1)S(1)} %collective-permute-done.12.refs_0_, ...), custom_call_target="tpu_custom_call", output_to_operand_aliasing={{}: (1, {})} | custom-call | flops 1000001024 | bytes 1024 | tf_op jit(solution)/shard_map/pallas_call | solution.py:268
  (3 shorter events, 0.0 us)
Async XLA Ops:
  0.0 12.7 %copy-start.1 = (bf16[12,256,512]{2,1,0:T(8,128)(2,1)S(1)}, bf16[12,256,512]{2,1,0:T(8,128)(2,1)}, u32[]{:S(2)}) copy-start(bf16[12,256,512]{2,1,0:T(8,128)(2,1)} %panel.1) | copy-start | bytes 9437188
  1.8 12.5 %collective-permute-start = (bf16[1,256,512]{2,1,0:T(8,128)(2,1)}, bf16[1,256,512]{2,1,0:T(8,128)(2,1)}, u32[]{:S(2)}, u32[]{:S(2)}) collective-permute-start(bf16[1,256,512]{2,1,0:T(8,128)(2,1)} %slice.10), channel_id=1, source_target_pairs={{0,2},{3,1},{4,6},{7,5},{8,10},{11,9},{12,14},{15,13},{16,18},{19,... | collective-permute-start | bytes 786440 | tf_op jit(solution)/shard_map/ppermute | solution.py:299
  7.0 10.8 %collective-permute-start.1 = (bf16[1,256,512]{2,1,0:T(8,128)(2,1)}, bf16[1,256,512]{2,1,0:T(8,128)(2,1)}, u32[]{:S(2)}, u32[]{:S(2)}) collective-permute-start(bf16[1,256,512]{2,1,0:T(8,128)(2,1)} %slice.10), channel_id=1, source_target_pairs={{0,1},{1,0},{2,3},{3,2},{4,5},{5,4},{6,7},{7,6},{8,9},{9,8},{10,11... | collective-permute-start | bytes 786440 | tf_op jit(solution)/shard_map/ppermute | solution.py:347
  10.5 55.1 %collective-permute-start.7 = (bf16[10,256,512]{2,1,0:T(8,128)(2,1)}, bf16[10,256,512]{2,1,0:T(8,128)(2,1)}, u32[]{:S(2)}, u32[]{:S(2)}) collective-permute-start(bf16[10,256,512]{2,1,0:T(8,128)(2,1)} %slice.12), channel_id=1, source_target_pairs={{1,2},{2,1},{5,6},{6,5},{9,10},{10,9},{13,14},{14,13},{17,18},{18,... | collective-permute-start | bytes 7864328 | tf_op jit(solution)/shard_map/ppermute | solution.py:345
  14.9 11.8 %collective-permute-start.2 = (bf16[1,256,512]{2,1,0:T(8,128)(2,1)S(1)}, bf16[1,256,512]{2,1,0:T(8,128)(2,1)}, u32[]{:S(2)}, u32[]{:S(2)}) collective-permute-start(bf16[1,256,512]{2,1,0:T(8,128)(2,1)S(1)} %shard_map.37.refs_2_), channel_id=1, source_target_pairs={{1,0},{2,3},{5,4},{6,7},{9,8},{10,11},{13,12},{14,15},{17,16},{18,... | collective-permute-start | bytes 786440 | tf_op jit(solution)/shard_map/ppermute | solution.py:350
  18.3 95.0 %collective-permute-start.8 = (bf16[9,256,512]{2,1,0:T(8,128)(2,1)}, bf16[9,256,512]{2,1,0:T(8,128)(2,1)}, u32[]{:S(2)}, u32[]{:S(2)}) collective-permute-start(bf16[9,256,512]{2,1,0:T(8,128)(2,1)} %shard_map.44), channel_id=1, source_target_pairs={{0,1},{1,0},{2,3},{3,2},{4,5},{5,4},{6,7},{7,6},{8,9},{9,8},{10,11... | collective-permute-start | bytes 7077896 | tf_op jit(solution)/shard_map/ppermute | solution.py:351
  28.3 11.1 %collective-permute-start.5 = (bf16[1,256,512]{2,1,0:T(8,128)(2,1)S(1)}, bf16[1,256,512]{2,1,0:T(8,128)(2,1)S(1)}, u32[]{:S(2)}, u32[]{:S(2)}) collective-permute-start(bf16[1,256,512]{2,1,0:T(8,128)(2,1)S(1)} %get-tuple-element.32), channel_id=1, source_target_pairs={{4,28},{8,16},{12,20},{16,8},{20,12},{5,29},{9,17},{13,21},{17,9},... | collective-permute-start | bytes 786440 | tf_op jit(solution)/shard_map/ppermute | solution.py:309
  31.7 7.8 %collective-permute-start.4 = (bf16[1,256,512]{2,1,0:T(8,128)(2,1)S(1)}, bf16[1,256,512]{2,1,0:T(8,128)(2,1)S(1)}, u32[]{:S(2)}, u32[]{:S(2)}) collective-permute-start(bf16[1,256,512]{2,1,0:T(8,128)(2,1)S(1)} %get-tuple-element.32), channel_id=1, source_target_pairs={{4,20},{8,24},{12,28},{16,0},{20,4},{5,21},{9,25},{13,29},{17,1},{... | collective-permute-start | bytes 786440 | tf_op jit(solution)/shard_map/ppermute | solution.py:309
  33.0 8.2 %collective-permute-start.3 = (bf16[1,256,512]{2,1,0:T(8,128)(2,1)S(1)}, bf16[1,256,512]{2,1,0:T(8,128)(2,1)S(1)}, u32[]{:S(2)}, u32[]{:S(2)}) collective-permute-start(bf16[1,256,512]{2,1,0:T(8,128)(2,1)S(1)} %get-tuple-element.32), channel_id=1, source_target_pairs={{4,12},{8,0},{12,4},{16,24},{20,28},{5,13},{9,1},{13,5},{17,25},{2... | collective-permute-start | bytes 786440 | tf_op jit(solution)/shard_map/ppermute | solution.py:309
  42.3 3.0 %collective-permute-start.6 = (bf16[4,1,256,512]{3,2,1,0:T(8,128)(2,1)}, bf16[4,1,256,512]{3,2,1,0:T(8,128)(2,1)}, u32[]{:S(2)}, u32[]{:S(2)}) collective-permute-start(bf16[4,1,256,512]{3,2,1,0:T(8,128)(2,1)} %pad_maximum_fusion.same), channel_id=1, source_target_pairs={{0,4},{4,0},{8,12},{12,8},{16,20},{20,16},{24,28},{28,24},{1,5},{5... | collective-permute-start | bytes 3145736 | tf_op jit(solution)/shard_map/ppermute | solution.py:311
  48.6 2.8 %copy-start = (bf16[48,256,256]{2,1,0:T(8,128)(2,1)S(1)}, bf16[48,256,256]{2,1,0:T(8,128)(2,1)}, u32[]{:S(2)}) copy-start(bf16[48,256,256]{2,1,0:T(8,128)(2,1)} %trailing.19) | copy-start | bytes 18874372
  57.3 84.0 %collective-permute-start.10 = (bf16[2,256,256]{2,1,0:T(8,128)(2,1)S(1)}, bf16[2,256,256]{2,1,0:T(8,128)(2,1)S(1)}, u32[]{:S(2)}, u32[]{:S(2)}) collective-permute-start(bf16[2,256,256]{2,1,0:T(8,128)(2,1)S(1)} %shard_map.40.after), channel_id=1, source_target_pairs={{0,1},{1,3},{3,2},{2,0},{4,5},{5,7},{7,6},{6,4},{8,9},{9,11},{11,1... | collective-permute-start | bytes 786440 | tf_op jit(solution)/shard_map/ppermute | solution.py:371
  58.8 55.8 %slice-start = ((s8[6291456]{0:T(1024)(128)(4,1)}), s8[4194304]{0:T(1024)(128)(4,1)S(1)}, s32[]{:S(2)}) async-start(s8[6291456]{0:T(1024)(128)(4,1)} %bitcast.7), calls=%async_computation | async-start | bytes 8388608
  60.3 64.7 %collective-permute-start.9 = (bf16[11,256,256]{2,1,0:T(8,128)(2,1)S(1)}, bf16[11,256,256]{2,1,0:T(8,128)(2,1)S(1)}, u32[]{:S(2)}, u32[]{:S(2)}) collective-permute-start(bf16[11,256,256]{2,1,0:T(8,128)(2,1)S(1)} %get-tuple-element.22.after), channel_id=1, source_target_pairs={{0,3},{3,0},{4,7},{7,4},{8,11},{11,8},{12,15},{15,12},{16,19},{19,... | collective-permute-start | bytes 4325384 | tf_op jit(solution)/shard_map/ppermute | solution.py:376
  64.7 49.9 %slice-start.1 = ((s8[6291456]{0:T(1024)(128)(4,1)}), s8[2097152]{0:T(1024)(128)(4,1)S(1)}, s32[]{:S(2)}) async-start(s8[6291456]{0:T(1024)(128)(4,1)} %bitcast.7), calls=%async_computation.1 | async-start | bytes 4194304
  64.7 77.9 %collective-permute-start.11 = (bf16[2,256,256]{2,1,0:T(8,128)(2,1)S(1)}, bf16[2,256,256]{2,1,0:T(8,128)(2,1)S(1)}, u32[]{:S(2)}, u32[]{:S(2)}) collective-permute-start(bf16[2,256,256]{2,1,0:T(8,128)(2,1)S(1)} %get-tuple-element.29), channel_id=1, source_target_pairs={{1,2},{2,1},{5,6},{6,5},{9,10},{10,9},{13,14},{14,13},{17,18},{18,... | collective-permute-start | bytes 786440 | tf_op jit(solution)/shard_map/ppermute | solution.py:378
  65.5 78.4 %collective-permute-start.13 = (bf16[11,256,256]{2,1,0:T(8,128)(2,1)S(1)}, bf16[11,256,256]{2,1,0:T(8,128)(2,1)S(1)}, u32[]{:S(2)}, u32[]{:S(2)}) collective-permute-start(bf16[11,256,256]{2,1,0:T(8,128)(2,1)S(1)} %shard_map.42.after), channel_id=1, source_target_pairs={{0,2},{3,1},{4,6},{7,5},{8,10},{11,9},{12,14},{15,13},{16,18},{19,... | collective-permute-start | bytes 4325384 | tf_op jit(solution)/shard_map/ppermute | solution.py:376
  113.3 32.2 %collective-permute-start.12 = (bf16[12,256,256]{2,1,0:T(8,128)(2,1)S(1)}, bf16[12,256,256]{2,1,0:T(8,128)(2,1)S(1)}, u32[]{:S(2)}, u32[]{:S(2)}) collective-permute-start(bf16[12,256,256]{2,1,0:T(8,128)(2,1)S(1)} %get-tuple-element.30), channel_id=1, source_target_pairs={{2,3},{1,0},{6,7},{5,4},{10,11},{9,8},{14,15},{13,12},{18,19},{17,... | collective-permute-start | bytes 4718600 | tf_op jit(solution)/shard_map/ppermute | solution.py:383
  120.4 2.8 %copy-start.2 = (bf16[1,256,512]{2,1,0:T(8,128)(2,1)S(1)}, bf16[1,256,512]{2,1,0:T(8,128)(2,1)}, u32[]{:S(2)}) copy-start(bf16[1,256,512]{2,1,0:T(8,128)(2,1)} %get-tuple-element.31.raw) | copy-start | bytes 786436
